TPU v7x, 512 devices: a whole 4x8x8 slice. The times are simulated.
512 devices in a mesh: row: 16 (over y, core), col: 32 (over z, x).
Axes of the slice: x: 4, y: 8, z: 8, core: 2. Of those that a mesh axis runs over, the one named last changes fastest.
Arguments:
- matrix: float32 [8192, 8192], P('row', 'col'), as said below
Outputs:
- panels: float32 [8192, 512], P(('row', 'col'))
- trailing_part: float32 [8192, 8192], P('row', 'col')
Inputs may be any that keep to these rules, and one draw needn't show every extreme that they name: matrix is symmetric and positive definite.
All inputs are finite; a program needn't handle non-finite values.
Results may differ from a plain program's by a relative error of at most 0.00007.
Values sent between devices are 32-bit elements; how exact they have to be, the bound alone decides.
No kernel may reach another device: no remote copies, remote signals or barrier semaphores. Data moves between devices by JAX's collectives and lax.ppermute only.
A program may use at most 64 MiB of HBM per device.

v0:
```python
import jax
import jax.numpy as jnp
from jax import lax
from jax.sharding import PartitionSpec as P


def from_root(block, axis, holder):
    block = jnp.where(lax.axis_index(axis) == holder, block, jnp.zeros_like(block))
    return lax.psum(block, axis)


def product_t(left, right):
    return jnp.dot(
        left, right.T, precision=lax.Precision.HIGHEST, preferred_element_type=jnp.float32
    )


def factor_panel(panel, which, row_index, global_rows):
    rows_dev, width = panel.shape
    offset = which * width - row_index * rows_dev
    holds = jnp.logical_and(offset >= 0, offset < rows_dev)
    local_off = jnp.clip(offset, 0, rows_dev - width)
    piece = lax.dynamic_slice_in_dim(panel, local_off, width, 0)
    diag = from_root(piece, "row", which * width // rows_dev)
    lower = jnp.linalg.cholesky(diag)
    solved = lax.linalg.triangular_solve(
        lower, panel, left_side=False, lower=True, transpose_a=True
    )
    cleared = jnp.where(global_rows[:, None] < which * width, 0.0, solved)
    placed = lax.dynamic_update_slice(cleared, lower, (local_off, jnp.int32(0)))
    return jnp.where(holds, placed, cleared)


def update_block(block, factor_rows, which, col_index):
    rows_dev, width = block.shape
    start = col_index * width
    piece = lax.dynamic_slice_in_dim(factor_rows, start % rows_dev, width, 0)
    matching = from_root(piece, "row", start // rows_dev)
    updated = block - product_t(factor_rows, matching)
    return jnp.where(col_index == which, factor_rows, updated)


def on_device(matrix):
    rows_dev, width = matrix.shape
    row_index = lax.axis_index("row")
    col_index = lax.axis_index("col")
    global_rows = row_index * rows_dev + jnp.arange(rows_dev, dtype=jnp.int32)
    global_cols = col_index * width + jnp.arange(width, dtype=jnp.int32)
    first_panel = from_root(matrix, "col", 0)
    first_rows = factor_panel(first_panel, 0, row_index, global_rows)
    after_first = update_block(matrix, first_rows, 0, col_index)
    second_panel = from_root(after_first, "col", 1)
    second_rows_fac = factor_panel(second_panel, 1, row_index, global_rows)
    after_second = update_block(after_first, second_rows_fac, 1, col_index)
    outside = jnp.logical_or(global_rows[:, None] < 2 * width, global_cols[None, :] < 2 * width)
    trailing_part = jnp.where(outside, 0.0, after_second)
    sub_rows = rows_dev // lax.axis_size("col")
    both_panels = jnp.concatenate([first_rows, second_rows_fac], axis=1)
    panels = lax.dynamic_slice_in_dim(both_panels, col_index * sub_rows, sub_rows, 0)
    return (panels, trailing_part)


def solution(mesh):
    placed = (P("row", "col"),)
    return jax.shard_map(
        on_device,
        mesh=mesh,
        in_specs=placed,
        out_specs=(P(("row", "col"), None), P("row", "col")),
        check_vma=False,
    )
```

profile of v0, /device:TPU:1, one launch (start us, length us, event | category | flops | bytes accessed | tf_op | source)
XLA Modules:
  0.0 938.9 jit_solution(12588465488957224640)
XLA Ops:
  7.2 1.2 copy.3
  8.5 0.8 broadcast_select_fusion.1
  9.4 162.7 %all-reduce.8.cloned.1.call-done = f32[512,256]{0,1:T(8,128)} async-done(((f32[512,256]{0,1:T(8,128)}), f32[512,256]{0,1:T(8,128)}) %all-reduce.8.cloned.1.call-update) | async-done | bytes 524304 | tf_op jit(solution)/shard_map/psum | solution.py:9
  172.1 1.8 dynamic-slice_select_fusion.5
  174.0 115.9 %all-reduce.10.cloned.1.call-done = f32[256,256]{0,1:T(8,128)} async-done(((f32[256,256]{0,1:T(8,128)}), f32[256,256]{0,1:T(8,128)}) %all-reduce.10.cloned.1.call-update) | async-done | bytes 262160 | tf_op jit(solution)/shard_map/psum | solution.py:9
  290.0 1.1 copy.4
  291.2 11.7 %cholesky.130 = f32[128,128]{1,0:T(8,128)S(1)} custom-call(f32[128,128]{1,0:T(8,128)S(1)} %cholesky.194), custom_call_target="Cholesky" | custom-call | tf_op jit(solution)/shard_map/jit(cholesky)/cholesky | solution.py:25
  303.0 9.8 %custom-call.13 = f32[1,128,128]{1,2,0:T(8,128)S(1)} custom-call(f32[1,128,128]{2,1,0:T(8,128)S(1)} %get-tuple-element.53), custom_call_target="InvertDiagBlocksLowerTriangular" | custom-call | tf_op jit(solution)/shard_map/jit(cholesky)/cholesky | solution.py:25
  313.5 11.7 %cholesky.147 = f32[128,128]{1,0:T(8,128)S(1)} custom-call(f32[128,128]{1,0:T(8,128)S(1)} %convolution_subtract_fusion.5), custom_call_target="Cholesky" | custom-call | tf_op jit(solution)/shard_map/jit(cholesky)/cholesky | solution.py:25
  327.5 4.5 while.4
  328.3 1.4 dynamic-slice.16
  330.5 1.4 dynamic-slice.16
  332.1 19.7 %custom-call.14 = f32[2,128,128]{1,2,0:T(8,128)S(1)} custom-call(f32[2,128,128]{2,1,0:T(8,128)S(1)} %get-tuple-element.18), custom_call_target="InvertDiagBlocksLowerTriangular" | custom-call | tf_op jit(solution)/shard_map/triangular_solve/custom-call.0 | solution.py:26
  353.2 1.9 select_n.111
  355.2 0.7 dynamic-slice_select_fusion.3
  356.0 114.7 %all-reduce.12.cloned.1.call-done = f32[256,256]{0,1:T(8,128)} async-done(((f32[256,256]{0,1:T(8,128)}), f32[256,256]{0,1:T(8,128)}) %all-reduce.12.cloned.1.call-update) | async-done | bytes 262160 | tf_op jit(solution)/shard_map/psum | solution.py:9
  470.7 2.4 broadcast_select_fusion
  473.2 157.2 %all-reduce.14.cloned.1.call-done = f32[512,256]{0,1:T(8,128)} async-done(((f32[512,256]{0,1:T(8,128)}), f32[512,256]{0,1:T(8,128)}) %all-reduce.14.cloned.1.call-update) | async-done | bytes 524304 | tf_op jit(solution)/shard_map/psum | solution.py:9
  630.4 1.8 dynamic-slice_select_fusion.2
  632.4 115.7 %all-reduce.16.cloned.1.call-done = f32[256,256]{0,1:T(8,128)} async-done(((f32[256,256]{0,1:T(8,128)}), f32[256,256]{0,1:T(8,128)}) %all-reduce.16.cloned.1.call-update) | async-done | bytes 262160 | tf_op jit(solution)/shard_map/psum | solution.py:9
  748.0 1.1 copy.10
  749.3 11.7 %cholesky.164 = f32[128,128]{1,0:T(8,128)S(1)} custom-call(f32[128,128]{1,0:T(8,128)S(1)} %cholesky.197), custom_call_target="Cholesky" | custom-call | tf_op jit(solution)/shard_map/jit(cholesky)/cholesky | solution.py:25
  761.1 9.8 %custom-call.15 = f32[1,128,128]{1,2,0:T(8,128)S(1)} custom-call(f32[1,128,128]{2,1,0:T(8,128)S(1)} %get-tuple-element.51), custom_call_target="InvertDiagBlocksLowerTriangular" | custom-call | tf_op jit(solution)/shard_map/jit(cholesky)/cholesky | solution.py:25
  771.5 11.7 %cholesky.181 = f32[128,128]{1,0:T(8,128)S(1)} custom-call(f32[128,128]{1,0:T(8,128)S(1)} %convolution_subtract_fusion.4), custom_call_target="Cholesky" | custom-call | tf_op jit(solution)/shard_map/jit(cholesky)/cholesky | solution.py:25
  786.2 4.6 while.5
  787.0 1.4 dynamic-slice.18
  789.2 1.4 dynamic-slice.18
  790.7 19.7 %custom-call.16 = f32[2,128,128]{1,2,0:T(8,128)S(1)} custom-call(f32[2,128,128]{2,1,0:T(8,128)S(1)} %get-tuple-element.19), custom_call_target="InvertDiagBlocksLowerTriangular" | custom-call | tf_op jit(solution)/shard_map/triangular_solve/custom-call.0 | solution.py:26
  811.9 1.9 select_n.125
  815.5 113.9 %all-reduce.18.cloned.1.call-done = f32[256,256]{0,1:T(8,128)} async-done(((f32[256,256]{0,1:T(8,128)}), f32[256,256]{0,1:T(8,128)}) %all-reduce.18.cloned.1.call-update) | async-done | bytes 262160 | tf_op jit(solution)/shard_map/psum | solution.py:9
  929.4 1.7 fusion.1
  931.1 1.0 copy.16
  (82 shorter events, 11.7 us)
Async XLA Ops:
  7.2 164.9 %all-reduce.8.cloned.1.call-start = ((), (), s32[]{:S(2)}) async-start(), calls=%async_computation | async-start | bytes 1048576 | tf_op jit(solution)/shard_map/psum | solution.py:9
  9.3 280.6 %all-reduce.10.cloned.1.call-start = ((), (), s32[]{:S(2)}) async-start(), calls=%async_computation.1 | async-start | bytes 524288 | tf_op jit(solution)/shard_map/psum | solution.py:9
  173.9 296.8 %all-reduce.12.cloned.1.call-start = ((), (), s32[]{:S(2)}) async-start(), calls=%async_computation.2 | async-start | bytes 524288 | tf_op jit(solution)/shard_map/psum | solution.py:9
  290.0 1.2 copy-start.2
  327.5 24.2 %copy-start = (f32[512,256]{0,1:T(8,128)S(1)}, f32[512,256]{0,1:T(8,128)}, u32[]{:S(2)}) copy-start(f32[512,256]{0,1:T(8,128)} %all-reduce.8.cloned.1.call-done) | copy-start | bytes 1572868
  355.9 274.5 %all-reduce.14.cloned.1.call-start = ((), (), s32[]{:S(2)}) async-start(), calls=%async_computation.3 | async-start | bytes 1048576 | tf_op jit(solution)/shard_map/psum | solution.py:9
  473.2 274.9 %all-reduce.16.cloned.1.call-start = ((), (), s32[]{:S(2)}) async-start(), calls=%async_computation.4 | async-start | bytes 524288 | tf_op jit(solution)/shard_map/psum | solution.py:9
  632.3 297.1 %all-reduce.18.cloned.1.call-start = ((), (), s32[]{:S(2)}) async-start(), calls=%async_computation.5 | async-start | bytes 524288 | tf_op jit(solution)/shard_map/psum | solution.py:9
  748.0 1.2 copy-start.3
  786.1 24.3 %copy-start.1 = (f32[512,256]{0,1:T(8,128)S(1)}, f32[512,256]{0,1:T(8,128)}, u32[]{:S(2)}) copy-start(f32[512,256]{0,1:T(8,128)} %all-reduce.14.cloned.1.call-done) | copy-start | bytes 1572868
Sparse Core Ops, SparseCore 0:
  12.0 160.0 all-reduce.7
  175.1 114.8 all-reduce.9
  356.0 114.6 all-reduce.11
  474.9 155.4 all-reduce.13
  633.1 114.8 all-reduce.15
  814.7 114.6 all-reduce.17
where the time goes:
time: 939 us
  waiting for transfers between devices  780 us (83%)
  other arithmetic  115 us (12%)
  local copies, waits for them, and re-layouts  18.2 us (2%)
  between operations  17.3 us (2%)
    psum x6, waiting for transfers between devices, from_root(): return lax.psum(block, axis)  780 us
    another operation x13, other arithmetic, factor_panel(): lower = jnp.linalg.cholesky(diag)  68.7 us
    another operation x5, other arithmetic, factor_panel(): lax.linalg.triangular_solve(lower, panel, left_side=False, lower=True, tr...  39.4 us
  transfers between devices with their start and end apart: 6, of which 6 were waited for; matrix products, arithmetic and copies ran while one was open for 0% of the time, Pallas kernels for 0%

commit v1 on v0

v1 whole, which is shorter than its diff:
```python
import jax, jax.numpy as jnp
from jax import lax
from jax.experimental import pallas as pl
from jax.experimental.pallas import tpu as pltpu
from jax.sharding import PartitionSpec as P

HI = lax.Precision.HIGHEST
B = 128
S8 = 8

def rep(x):
    return jnp.broadcast_to(x, (S8, B))

def factor_tile(d_ref, m_ref, lt_ref):
    tiles = B // S8
    for b in range(tiles):
        rows = pl.ds(b * S8, S8)
        d = d_ref[rows, :]
        m = m_ref[rows, :]
        cols = [rep(d[:, b * S8 + k : b * S8 + k + 1]) for k in range(S8)]
        s = {}
        for i in range(S8):
            for k in range(i, S8):
                s[i, k] = rep(cols[k][i : i + 1, :])
        rd = [rep(d[j : j + 1, :]) for j in range(S8)]
        rm = [rep(m[j : j + 1, :]) for j in range(S8)]
        u, qd, qm, scale = {}, [], [], []
        for j in range(S8):
            inv = 1.0 / s[j, j]
            scale.append(lax.rsqrt(s[j, j]))
            for k in range(j + 1, S8):
                u[j, k] = s[j, k] * inv
            for i in range(j + 1, S8):
                for k in range(i, S8):
                    s[i, k] = s[i, k] - s[j, i] * u[j, k]
            qd.append(rd[j] * inv)
            qm.append(rm[j] * inv)
            for k in range(j + 1, S8):
                rd[k] = rd[k] - s[j, k] * qd[j]
                rm[k] = rm[k] - s[j, k] * qm[j]
        for t in range(b + 1, tiles):
            at = pl.ds(t * S8, S8)
            dt = d_ref[at, :]
            mt = m_ref[at, :]
            c = [rep(dt[:, b * S8 + k : b * S8 + k + 1]) for k in range(S8)]
            for j in range(S8):
                for k in range(j + 1, S8):
                    c[k] = c[k] - c[j] * u[j, k]
            for j in range(S8):
                dt = dt - c[j] * qd[j]
                mt = mt - c[j] * qm[j]
            d_ref[at, :] = dt
            m_ref[at, :] = mt
        sub = lax.broadcasted_iota(jnp.int32, (S8, B), 0)
        od, om = rd[0] * scale[0], rm[0] * scale[0]
        for j in range(1, S8):
            od = jnp.where(sub == j, rd[j] * scale[j], od)
            om = jnp.where(sub == j, rm[j] * scale[j], om)
        lt_ref[rows, :] = od
        m_ref[rows, :] = om

def dot(a, b, dims=((1,), (0,))):
    return lax.dot_general(a, b, (dims, ((), ())), precision=HI, preferred_element_type=jnp.float32)

BLOCKS = tuple((i, j) for i in range(4) for j in range(i + 1))


def chol_kernel(g_ref, l_ref, inv_ref, s_ref, d_ref, m_ref, lt_ref):
    n = l_ref.shape[0]
    s_ref[...] = jnp.zeros((n, n), jnp.float32)
    for at, (i, j) in enumerate(BLOCKS):
        s_ref[i * B : (i + 1) * B, j * B : (j + 1) * B] = g_ref[:, at].reshape(B, B)
    ri = lax.broadcasted_iota(jnp.int32, (n, n), 0)
    ci = lax.broadcasted_iota(jnp.int32, (n, n), 1)
    inv_ref[...] = jnp.where(ri == ci, 1.0, 0.0).astype(jnp.float32)
    l_ref[...] = jnp.zeros((n, n), jnp.float32)
    r128 = lax.broadcasted_iota(jnp.int32, (B, B), 0)
    c128 = lax.broadcasted_iota(jnp.int32, (B, B), 1)
    eye = jnp.where(r128 == c128, 1.0, 0.0).astype(jnp.float32)
    rn = lax.broadcasted_iota(jnp.int32, (n, B), 0)

    def step(k, carry):
        off = pl.multiple_of(k * B, B)
        d_ref[...] = s_ref[pl.ds(off, B), pl.ds(off, B)]
        m_ref[...] = eye
        factor_tile(d_ref, m_ref, lt_ref)
        inv = m_ref[...]
        lower = jnp.where(r128 >= c128, lt_ref[...].T, 0.0)
        below = dot(s_ref[:, pl.ds(off, B)], inv, ((1,), (1,)))
        below = jnp.where(rn >= off + B, below, 0.0)
        l_ref[:, pl.ds(off, B)] = below
        l_ref[pl.ds(off, B), pl.ds(off, B)] = lower
        mine = dot(inv, inv_ref[pl.ds(off, B), :])
        s_ref[...] -= dot(below, below, ((1,), (1,)))
        inv_ref[...] -= dot(below, mine)
        inv_ref[pl.ds(off, B), :] = mine
        return carry

    lax.fori_loop(0, n // B, step, 0)


def whole():
    return pl.BlockSpec(memory_space=pltpu.VMEM)


def chol(gathered):
    n = 4 * B
    out = jax.ShapeDtypeStruct((n, n), jnp.float32)
    return pl.pallas_call(
        chol_kernel,
        out_shape=(out, out),
        in_specs=[whole()],
        out_specs=(whole(), whole()),
        scratch_shapes=[pltpu.VMEM((n, n), jnp.float32)] + [pltpu.VMEM((B, B), jnp.float32)] * 3,
        compiler_params=pltpu.CompilerParams(vmem_limit_bytes=40 * 2**20),
    )(gathered)


def final_kernel(x_ref, mine_ref, far_ref, top_ref, l_ref, inv_ref, panel_ref, out_ref, u_ref, f_ref):
    row, col = lax.axis_index("row"), lax.axis_index("col")
    z = col // 8
    inv = inv_ref[...]
    top = jnp.concatenate([top_ref[:, i].reshape(B, -1) for i in range(4)], axis=0)
    u_ref[...] = dot(inv, top)
    for s in range(4):
        piece = mine_ref[...] if s == 0 else far_ref[s - 1]
        at = pl.multiple_of(lax.rem(z + 4 - s, 4) * B, B)
        f_ref[pl.ds(at, B), :] = dot(piece, inv, ((1,), (1,)))

    @pl.when(row == 0)
    def _():
        f_ref[...] = l_ref[...]

    panel_ref[...] = f_ref[pl.ds(pl.multiple_of(col * 16, 16), 16), :]
    live = jnp.logical_and(row > 0, col > 1)

    @pl.when(live)
    def _():
        out_ref[...] = x_ref[...] - dot(f_ref[...], u_ref[...])

    @pl.when(jnp.logical_not(live))
    def _():
        out_ref[...] = jnp.zeros_like(out_ref)


def final(x, mine, far, top, lower, inv):
    return pl.pallas_call(
        final_kernel,
        out_shape=(
            jax.ShapeDtypeStruct((16, 512), jnp.float32),
            jax.ShapeDtypeStruct((512, 256), jnp.float32),
        ),
        in_specs=[whole()] * 6,
        out_specs=(whole(), whole()),
        scratch_shapes=[pltpu.VMEM((512, 256), jnp.float32), pltpu.VMEM((512, 512), jnp.float32)],
        compiler_params=pltpu.CompilerParams(vmem_limit_bytes=40 * 2**20),
    )(x, mine, far, top, lower, inv)


def on_device(x):
    col = lax.axis_index("col")
    first = col == 0
    z = col // 8

    def send(v, pairs):
        return lax.ppermute(v, "col", pairs)

    part = [x[q * B : (q + 1) * B] for q in range(4)]
    moved = [send(part[q], [(0, 8 * q), (1, 8 * q + 1)]) for q in range(1, 4)]
    quarter = jnp.where(z == 0, part[0], moved[0] + moved[1] + moved[2])
    quarter = jnp.where(col % 8 < 2, quarter, 0.0)
    planes = range(0, 32, 8)
    quarter += send(quarter, [(p + i, p + i + 4) for p in planes for i in (0, 1)])
    quarter += send(quarter, [(p + i, p + i + 2) for p in planes for i in (0, 1, 4, 5)])
    other = send(quarter, [(i, i ^ 1) for i in range(32)])
    even = col % 2 == 0
    mine = jnp.concatenate(
        [jnp.where(even, quarter, other), jnp.where(even, other, quarter)], axis=1
    )
    far = jnp.stack([send(mine, [(i, (i + 8 * s) % 32) for i in range(32)]) for s in (1, 2, 3)])

    split = x.reshape(4, 16, 8, 256).transpose(1, 0, 2, 3)
    piece = lax.all_to_all(split, "row", 0, 0)[0]
    swapped = send(piece, [(0, 1), (1, 0)])
    left = jnp.where(first, piece, swapped)
    right = jnp.where(first, swapped, piece)
    groups = []
    for i, j in BLOCKS:
        side = left if j < 2 else right
        groups.append(side[i, :, (j % 2) * B : (j % 2 + 1) * B])
    packed = jnp.where(col < 2, jnp.stack(groups), 0.0)
    packed += sum(send(packed, [(0, 8 * q), (1, 8 * q + 1)]) for q in range(1, 4))
    packed += sum(send(packed, [(p + i, p + i + s) for p in planes for i in (0, 1)]) for s in (2, 4, 6))
    gathered = lax.all_gather(packed, "row")
    lower, inv = chol(gathered)
    top = lax.all_gather(piece, "row")
    return final(x, mine, far, top, lower, inv)


def solution(mesh):
    return jax.shard_map(
        on_device,
        mesh=mesh,
        in_specs=(P("row", "col"),),
        out_specs=(P(("row", "col"), None), P("row", "col")),
        check_vma=False,
    )
```

time: 939 us -> 153 us (0.16)
  waiting for transfers between devices: 780 us -> 21.8 us
  other arithmetic: 115 us -> 0.21 us
  starting transfers between devices: 0.25 us -> 57.4 us
  blocking collectives: 0 us -> 35.7 us
  Pallas kernels: 0 us -> 34.3 us
  between operations: 17.3 us -> 0.99 us
  local copies, waits for them, and re-layouts: 18.2 us -> 2 us
    psum x6 -> x0, waiting for transfers between devices: 780 us -> none  [from_root(): return lax.psum(block, axis)]
    another operation x18 -> x1, other arithmetic: 108 us -> 0.05 us  [on_device(): jnp.stack([send(mine, [(i, (i + 8 * s) % 32) for i in range(32)]) for s i...]
    ppermute x0 -> x16, starting transfers between devices: none -> 49.4 us  [send(): return lax.ppermute(v, 'col', pairs)]
    all_gather x0 -> x2, blocking collectives: none -> 35.7 us  [the longest x1 18.6 us: on_device(): top = lax.all_gather(piece, 'row')]
    pallas_call x0 -> x2, Pallas kernels: none -> 34.3 us  [the longest x1 29.1 us: chol(): pl.pallas_call(chol_kernel, out_shape=(out, out), in_specs=[whole()], out...]
    ppermute x0 -> x16, waiting for transfers between devices: none -> 18.6 us  [send(): return lax.ppermute(v, 'col', pairs)]
  transfers between devices with their start and end apart: 6 -> 17, of which waited for: 6 -> 6; matrix products, arithmetic and copies ran while one was open for 0% -> 1% of each run, Pallas kernels for 0% -> 0%
where the time goes in v1:
time: 153 us; the launch traced here: 152 us
  starting transfers between devices  57.4 us (38%)
  blocking collectives  35.7 us (23%)
  Pallas kernels  34.3 us (22%)
  waiting for transfers between devices  21.8 us (14%)
  local copies, waits for them, and re-layouts  2 us (1%)
    ppermute x16, starting transfers between devices, send(): return lax.ppermute(v, 'col', pairs)  49.4 us
    pallas_call x1, Pallas kernels, chol(): pl.pallas_call(chol_kernel, out_shape=(out, out), in_specs=[whole()], out...  29.1 us
    all_gather x1, blocking collectives, on_device(): top = lax.all_gather(piece, 'row')  18.6 us
    ppermute x16, waiting for transfers between devices, send(): return lax.ppermute(v, 'col', pairs)  18.6 us
    all_gather x1, blocking collectives, on_device(): gathered = lax.all_gather(packed, 'row')  17.1 us
    all_to_all x1, starting transfers between devices, on_device(): piece = lax.all_to_all(split, 'row', 0, 0)[0]  8.07 us
    pallas_call x1, Pallas kernels, final(): pl.pallas_call(final_kernel, out_shape=(jax.ShapeDtypeStruct((16, 512), j...  5.15 us
    all_to_all x1, waiting for transfers between devices, on_device(): piece = lax.all_to_all(split, 'row', 0, 0)[0]  3.17 us
  transfers between devices with their start and end apart: 17, of which 6 were waited for; matrix products, arithmetic and copies ran while one was open for 1% of the time, Pallas kernels for 0%

profile of v1, /device:TPU:1, one launch (start us, length us, event | category | flops | bytes accessed | tf_op | source)
XLA Modules:
  0.0 152.4 jit_solution(1616245222656849410)
XLA Ops:
  0.6 1.1 fusion
  1.8 6.6 %collective-permute-start = (f32[128,256]{1,0:T(8,128)S(1)}, f32[128,256]{1,0:T(8,128)S(1)}, u32[]{:S(2)}, u32[]{:S(2)}) collective-permute-start(f32[128,256]{1,0:T(8,128)S(1)} %get-tuple-element.12), channel_id=1, source_target_pairs={{0,8},{1,9},{32,40},{33,41},{64,72},{65,73},{96,104},{97,105},{128... | collective-permute-start | bytes 393224 | tf_op jit(solution)/shard_map/ppermute | solution.py:166
  8.4 5.5 %collective-permute-start.1 = (f32[128,256]{1,0:T(8,128)S(1)}, f32[128,256]{1,0:T(8,128)S(1)}, u32[]{:S(2)}, u32[]{:S(2)}) collective-permute-start(f32[128,256]{1,0:T(8,128)S(1)} %get-tuple-element.10), channel_id=1, source_target_pairs={{0,16},{1,17},{32,48},{33,49},{64,80},{65,81},{96,112},{97,113},{1... | collective-permute-start | bytes 393224 | tf_op jit(solution)/shard_map/ppermute | solution.py:166
  13.9 1.3 collective-permute-start.2
  15.2 0.9 copy.5
  16.1 8.1 %all-to-all-start = ((f32[16,4,8,256]{3,2,1,0:T(8,128)}), f32[16,4,8,256]{3,2,1,0:T(8,128)S(1)}, u32[]{:S(2)}, u32[]{:S(2)}) async-start(f32[16,4,8,256]{3,2,1,0:T(8,128)} %copy.5), calls=%async_computation | async-start | bytes 1048576 | tf_op jit(solution)/shard_map/all_to_all | solution.py:183
  24.2 0.0 collective-permute-done.1
  24.2 0.0 collective-permute-done.2
  24.2 1.3 collective-permute-start.3
  25.5 3.0 %collective-permute-done.3 = f32[128,256]{1,0:T(8,128)S(1)} collective-permute-done((f32[128,256]{1,0:T(8,128)S(1)}, f32[128,256]{1,0:T(8,128)S(1)}, u32[]{:S(2)}, u32[]{:S(2)}) %collective-permute-start.3) | collective-permute-done | bytes 131104 | tf_op jit(solution)/shard_map/ppermute | solution.py:166
  28.5 1.3 collective-permute-start.4
  29.8 2.4 %collective-permute-done.4 = f32[128,256]{1,0:T(8,128)S(1)} collective-permute-done((f32[128,256]{1,0:T(8,128)S(1)}, f32[128,256]{1,0:T(8,128)S(1)}, u32[]{:S(2)}, u32[]{:S(2)}) %collective-permute-start.4) | collective-permute-done | bytes 131104 | tf_op jit(solution)/shard_map/ppermute | solution.py:166
  32.3 3.1 %collective-permute-start.5 = (f32[128,256]{1,0:T(8,128)S(1)}, f32[128,256]{1,0:T(8,128)S(1)}, u32[]{:S(2)}, u32[]{:S(2)}) collective-permute-start(f32[128,256]{1,0:T(8,128)S(1)} %add.43), channel_id=1, source_target_pairs={{0,1},{1,0},{2,3},{3,2},{4,5},{5,4},{6,7},{7,6},{8,9},{9,8},{10,11... | collective-permute-start | bytes 393224 | tf_op jit(solution)/shard_map/ppermute | solution.py:166
  35.4 2.9 %collective-permute-done.5 = f32[128,256]{1,0:T(8,128)S(1)} collective-permute-done((f32[128,256]{1,0:T(8,128)S(1)}, f32[128,256]{1,0:T(8,128)S(1)}, u32[]{:S(2)}, u32[]{:S(2)}) %collective-permute-start.5) | collective-permute-done | bytes 131104 | tf_op jit(solution)/shard_map/ppermute | solution.py:166
  38.3 3.2 %all-to-all-done = f32[16,4,8,256]{3,2,1,0:T(8,128)S(1)} async-done(((f32[16,4,8,256]{3,2,1,0:T(8,128)}), f32[16,4,8,256]{3,2,1,0:T(8,128)S(1)}, u32[]{:S(2)}, u32[]{:S(2)}) %all-to-all-start) | async-done | bytes 524320 | tf_op jit(solution)/shard_map/all_to_all | solution.py:183
  41.5 3.1 %collective-permute-start.9 = (f32[4,8,256]{2,1,0:T(8,128)S(1)}, f32[4,8,256]{2,1,0:T(8,128)S(1)}, u32[]{:S(2)}, u32[]{:S(2)}) collective-permute-start(f32[4,8,256]{2,1,0:T(8,128)S(1)} %get-tuple-element.8), channel_id=1, source_target_pairs={{0,1},{1,0},{32,33},{33,32},{64,65},{65,64},{96,97},{97,96},{128,1... | collective-permute-start | bytes 98312 | tf_op jit(solution)/shard_map/ppermute | solution.py:166
  44.6 1.9 %collective-permute-start.6 = (f32[128,512]{1,0:T(8,128)S(1)}, f32[128,512]{1,0:T(8,128)S(1)}, u32[]{:S(2)}, u32[]{:S(2)}) collective-permute-start(f32[128,512]{1,0:T(8,128)S(1)} %pad_maximum_fusion.1.mine_ref), channel_id=1, source_target_pairs={{0,8},{1,9},{2,10},{3,11},{4,12},{5,13},{6,14},{7,15},{8,16},{9,17... | collective-permute-start | bytes 786440 | tf_op jit(solution)/shard_map/ppermute | solution.py:166
  46.5 1.9 %collective-permute-start.7 = (f32[128,512]{1,0:T(8,128)S(1)}, f32[128,512]{1,0:T(8,128)S(1)}, u32[]{:S(2)}, u32[]{:S(2)}) collective-permute-start(f32[128,512]{1,0:T(8,128)S(1)} %pad_maximum_fusion.1.mine_ref), channel_id=1, source_target_pairs={{0,16},{1,17},{2,18},{3,19},{4,20},{5,21},{6,22},{7,23},{8,24},{9,... | collective-permute-start | bytes 786440 | tf_op jit(solution)/shard_map/ppermute | solution.py:166
  48.5 5.5 %collective-permute-start.8 = (f32[128,512]{1,0:T(8,128)S(1)}, f32[128,512]{1,0:T(8,128)S(1)}, u32[]{:S(2)}, u32[]{:S(2)}) collective-permute-start(f32[128,512]{1,0:T(8,128)S(1)} %pad_maximum_fusion.1.mine_ref), channel_id=1, source_target_pairs={{0,24},{1,25},{2,26},{3,27},{4,28},{5,29},{6,30},{7,31},{8,0},{9,1... | collective-permute-start | bytes 786440 | tf_op jit(solution)/shard_map/ppermute | solution.py:166
  54.1 4.0 %collective-permute-start.10 = (f32[10,8,128]{2,1,0:T(8,128)S(1)}, f32[10,8,128]{2,1,0:T(8,128)S(1)}, u32[]{:S(2)}, u32[]{:S(2)}) collective-permute-start(f32[10,8,128]{2,1,0:T(8,128)S(1)} %broadcast_select_fusion.2), channel_id=1, source_target_pairs={{0,8},{1,9},{32,40},{33,41},{64,72},{65,73},{96,104},{97,105},{128... | collective-permute-start | bytes 122888 | tf_op jit(solution)/shard_map/ppermute | solution.py:166
  58.1 4.0 %collective-permute-start.11 = (f32[10,8,128]{2,1,0:T(8,128)S(1)}, f32[10,8,128]{2,1,0:T(8,128)S(1)}, u32[]{:S(2)}, u32[]{:S(2)}) collective-permute-start(f32[10,8,128]{2,1,0:T(8,128)S(1)} %broadcast_select_fusion.2), channel_id=1, source_target_pairs={{0,16},{1,17},{32,48},{33,49},{64,80},{65,81},{96,112},{97,113},{1... | collective-permute-start | bytes 122888 | tf_op jit(solution)/shard_map/ppermute | solution.py:166
  62.1 1.3 collective-permute-start.12
  63.4 4.7 %collective-permute-done.7 = f32[128,512]{1,0:T(8,128)S(1)} collective-permute-done((f32[128,512]{1,0:T(8,128)S(1)}, f32[128,512]{1,0:T(8,128)S(1)}, u32[]{:S(2)}, u32[]{:S(2)}) %collective-permute-start.7) | collective-permute-done | bytes 262176 | tf_op jit(solution)/shard_map/ppermute | solution.py:166
  68.1 5.6 %collective-permute-done.8 = f32[128,512]{1,0:T(8,128)S(1)} collective-permute-done((f32[128,512]{1,0:T(8,128)S(1)}, f32[128,512]{1,0:T(8,128)S(1)}, u32[]{:S(2)}, u32[]{:S(2)}) %collective-permute-start.8) | collective-permute-done | bytes 262176 | tf_op jit(solution)/shard_map/ppermute | solution.py:166
  73.7 0.1 pad_maximum_fusion.far_ref
  73.8 6.0 %collective-permute-start.13 = (f32[10,8,128]{2,1,0:T(8,128)S(1)}, f32[10,8,128]{2,1,0:T(8,128)S(1)}, u32[]{:S(2)}, u32[]{:S(2)}) collective-permute-start(f32[10,8,128]{2,1,0:T(8,128)S(1)} %add_add_fusion.1), channel_id=1, source_target_pairs={{0,2},{1,3},{8,10},{9,11},{16,18},{17,19},{24,26},{25,27},{32,34},... | collective-permute-start | bytes 122888 | tf_op jit(solution)/shard_map/ppermute | solution.py:166
  79.7 1.3 collective-permute-start.14
  81.0 1.3 collective-permute-start.15
  82.3 18.6 %all_gather.9.top_ref = f32[16,4,8,256]{3,2,1,0:T(8,128)S(1)} all-gather(f32[1,4,8,256]{3,2,1,0:T(8,128)S(1)} %get-tuple-element.9), channel_id=1, replica_groups=mesh['row'=16,'col'=32] {'row'}, dimensions={0}, use_global_device_ids=true | all-gather | bytes 557056 | tf_op jit(solution)/shard_map/all_gather | solution.py:196
  101.0 17.1 %all-gather = f32[160,8,128]{2,1,0:T(8,128)S(1)} all-gather(f32[10,8,128]{2,1,0:T(8,128)S(1)} %add_add_fusion), channel_id=2, replica_groups=mesh['row'=16,'col'=32] {'row'}, dimensions={0}, use_global_device_ids=true | all-gather | bytes 696320 | tf_op jit(solution)/shard_map/all_gather | solution.py:194
  118.1 29.1 %shard_map.30 = (f32[512,512]{1,0:T(8,128)S(1)}, f32[512,512]{1,0:T(8,128)S(1)}) custom-call(f32[16,10,8,128]{3,2,1,0:T(8,128)S(1)} %bitcast.12), custom_call_target="tpu_custom_call" | custom-call | tf_op jit(solution)/shard_map/pallas_call | solution.py:109
  147.3 5.1 %shard_map.31 = (f32[16,512]{1,0:T(8,128)}, f32[512,256]{1,0:T(8,128)}) custom-call(f32[512,256]{1,0:T(8,128)S(1)} %copy-done, f32[128,512]{1,0:T(8,128)S(1)} %pad_maximum_fusion.1.mine_ref, f32[3,128,512]{2,1,0:T(8,128)S(1)} %pad_maximum_fusion.far_ref, f32[16,4,8,256]{3,2,1,0:T(8,128)S(1)} %all_gather.9.top_ref, f32[512,512]{1,0:T(8,128)S(1)} %get-tuple-element.4.l_ref, ...), custom_call_target="tpu_custom_call" | custom-call | tf_op jit(solution)/shard_map/pallas_call | solution.py:147
  (30 shorter events, 0.2 us)
Async XLA Ops:
  0.6 14.6 %copy-start = (f32[512,256]{1,0:T(8,128)S(1)}, f32[512,256]{1,0:T(8,128)}, u32[]{:S(2)}) copy-start(f32[512,256]{1,0:T(8,128)} %x_ref.1) | copy-start | bytes 1572868
  1.8 22.4 %collective-permute-start = (f32[128,256]{1,0:T(8,128)S(1)}, f32[128,256]{1,0:T(8,128)S(1)}, u32[]{:S(2)}, u32[]{:S(2)}) collective-permute-start(f32[128,256]{1,0:T(8,128)S(1)} %get-tuple-element.12), channel_id=1, source_target_pairs={{0,8},{1,9},{32,40},{33,41},{64,72},{65,73},{96,104},{97,105},{128... | collective-permute-start | bytes 393224 | tf_op jit(solution)/shard_map/ppermute | solution.py:166
  8.4 15.7 %collective-permute-start.1 = (f32[128,256]{1,0:T(8,128)S(1)}, f32[128,256]{1,0:T(8,128)S(1)}, u32[]{:S(2)}, u32[]{:S(2)}) collective-permute-start(f32[128,256]{1,0:T(8,128)S(1)} %get-tuple-element.10), channel_id=1, source_target_pairs={{0,16},{1,17},{32,48},{33,49},{64,80},{65,81},{96,112},{97,113},{1... | collective-permute-start | bytes 393224 | tf_op jit(solution)/shard_map/ppermute | solution.py:166
  13.9 10.3 %collective-permute-start.2 = (f32[128,256]{1,0:T(8,128)S(1)}, f32[128,256]{1,0:T(8,128)S(1)}, u32[]{:S(2)}, u32[]{:S(2)}) collective-permute-start(f32[128,256]{1,0:T(8,128)S(1)} %get-tuple-element.11), channel_id=1, source_target_pairs={{0,24},{1,25},{32,56},{33,57},{64,88},{65,89},{96,120},{97,121},{1... | collective-permute-start | bytes 393224 | tf_op jit(solution)/shard_map/ppermute | solution.py:166
  16.1 25.4 %all-to-all-start = ((f32[16,4,8,256]{3,2,1,0:T(8,128)}), f32[16,4,8,256]{3,2,1,0:T(8,128)S(1)}, u32[]{:S(2)}, u32[]{:S(2)}) async-start(f32[16,4,8,256]{3,2,1,0:T(8,128)} %copy.5), calls=%async_computation | async-start | bytes 1048576 | tf_op jit(solution)/shard_map/all_to_all | solution.py:183
  24.2 4.3 %collective-permute-start.3 = (f32[128,256]{1,0:T(8,128)S(1)}, f32[128,256]{1,0:T(8,128)S(1)}, u32[]{:S(2)}, u32[]{:S(2)}) collective-permute-start(f32[128,256]{1,0:T(8,128)S(1)} %select_select_fusion), channel_id=1, source_target_pairs={{0,4},{1,5},{8,12},{9,13},{16,20},{17,21},{24,28},{25,29},{32,36},... | collective-permute-start | bytes 393224 | tf_op jit(solution)/shard_map/ppermute | solution.py:166
  28.5 3.7 %collective-permute-start.4 = (f32[128,256]{1,0:T(8,128)S(1)}, f32[128,256]{1,0:T(8,128)S(1)}, u32[]{:S(2)}, u32[]{:S(2)}) collective-permute-start(f32[128,256]{1,0:T(8,128)S(1)} %add.42), channel_id=1, source_target_pairs={{0,2},{1,3},{4,6},{5,7},{8,10},{9,11},{12,14},{13,15},{16,18},{17,... | collective-permute-start | bytes 393224 | tf_op jit(solution)/shard_map/ppermute | solution.py:166
  32.3 6.0 %collective-permute-start.5 = (f32[128,256]{1,0:T(8,128)S(1)}, f32[128,256]{1,0:T(8,128)S(1)}, u32[]{:S(2)}, u32[]{:S(2)}) collective-permute-start(f32[128,256]{1,0:T(8,128)S(1)} %add.43), channel_id=1, source_target_pairs={{0,1},{1,0},{2,3},{3,2},{4,5},{5,4},{6,7},{7,6},{8,9},{9,8},{10,11... | collective-permute-start | bytes 393224 | tf_op jit(solution)/shard_map/ppermute | solution.py:166
  41.5 12.5 %collective-permute-start.9 = (f32[4,8,256]{2,1,0:T(8,128)S(1)}, f32[4,8,256]{2,1,0:T(8,128)S(1)}, u32[]{:S(2)}, u32[]{:S(2)}) collective-permute-start(f32[4,8,256]{2,1,0:T(8,128)S(1)} %get-tuple-element.8), channel_id=1, source_target_pairs={{0,1},{1,0},{32,33},{33,32},{64,65},{65,64},{96,97},{97,96},{128,1... | collective-permute-start | bytes 98312 | tf_op jit(solution)/shard_map/ppermute | solution.py:166
  44.6 17.4 %collective-permute-start.6 = (f32[128,512]{1,0:T(8,128)S(1)}, f32[128,512]{1,0:T(8,128)S(1)}, u32[]{:S(2)}, u32[]{:S(2)}) collective-permute-start(f32[128,512]{1,0:T(8,128)S(1)} %pad_maximum_fusion.1.mine_ref), channel_id=1, source_target_pairs={{0,8},{1,9},{2,10},{3,11},{4,12},{5,13},{6,14},{7,15},{8,16},{9,17... | collective-permute-start | bytes 786440 | tf_op jit(solution)/shard_map/ppermute | solution.py:166
  46.5 21.6 %collective-permute-start.7 = (f32[128,512]{1,0:T(8,128)S(1)}, f32[128,512]{1,0:T(8,128)S(1)}, u32[]{:S(2)}, u32[]{:S(2)}) collective-permute-start(f32[128,512]{1,0:T(8,128)S(1)} %pad_maximum_fusion.1.mine_ref), channel_id=1, source_target_pairs={{0,16},{1,17},{2,18},{3,19},{4,20},{5,21},{6,22},{7,23},{8,24},{9,... | collective-permute-start | bytes 786440 | tf_op jit(solution)/shard_map/ppermute | solution.py:166
  48.5 25.2 %collective-permute-start.8 = (f32[128,512]{1,0:T(8,128)S(1)}, f32[128,512]{1,0:T(8,128)S(1)}, u32[]{:S(2)}, u32[]{:S(2)}) collective-permute-start(f32[128,512]{1,0:T(8,128)S(1)} %pad_maximum_fusion.1.mine_ref), channel_id=1, source_target_pairs={{0,24},{1,25},{2,26},{3,27},{4,28},{5,29},{6,30},{7,31},{8,0},{9,1... | collective-permute-start | bytes 786440 | tf_op jit(solution)/shard_map/ppermute | solution.py:166
  54.1 19.6 %collective-permute-start.10 = (f32[10,8,128]{2,1,0:T(8,128)S(1)}, f32[10,8,128]{2,1,0:T(8,128)S(1)}, u32[]{:S(2)}, u32[]{:S(2)}) collective-permute-start(f32[10,8,128]{2,1,0:T(8,128)S(1)} %broadcast_select_fusion.2), channel_id=1, source_target_pairs={{0,8},{1,9},{32,40},{33,41},{64,72},{65,73},{96,104},{97,105},{128... | collective-permute-start | bytes 122888 | tf_op jit(solution)/shard_map/ppermute | solution.py:166
  58.1 15.6 %collective-permute-start.11 = (f32[10,8,128]{2,1,0:T(8,128)S(1)}, f32[10,8,128]{2,1,0:T(8,128)S(1)}, u32[]{:S(2)}, u32[]{:S(2)}) collective-permute-start(f32[10,8,128]{2,1,0:T(8,128)S(1)} %broadcast_select_fusion.2), channel_id=1, source_target_pairs={{0,16},{1,17},{32,48},{33,49},{64,80},{65,81},{96,112},{97,113},{1... | collective-permute-start | bytes 122888 | tf_op jit(solution)/shard_map/ppermute | solution.py:166
  62.1 11.7 %collective-permute-start.12 = (f32[10,8,128]{2,1,0:T(8,128)S(1)}, f32[10,8,128]{2,1,0:T(8,128)S(1)}, u32[]{:S(2)}, u32[]{:S(2)}) collective-permute-start(f32[10,8,128]{2,1,0:T(8,128)S(1)} %broadcast_select_fusion.2), channel_id=1, source_target_pairs={{0,24},{1,25},{32,56},{33,57},{64,88},{65,89},{96,120},{97,121},{1... | collective-permute-start | bytes 122888 | tf_op jit(solution)/shard_map/ppermute | solution.py:166
  73.8 27.2 %collective-permute-start.13 = (f32[10,8,128]{2,1,0:T(8,128)S(1)}, f32[10,8,128]{2,1,0:T(8,128)S(1)}, u32[]{:S(2)}, u32[]{:S(2)}) collective-permute-start(f32[10,8,128]{2,1,0:T(8,128)S(1)} %add_add_fusion.1), channel_id=1, source_target_pairs={{0,2},{1,3},{8,10},{9,11},{16,18},{17,19},{24,26},{25,27},{32,34},... | collective-permute-start | bytes 122888 | tf_op jit(solution)/shard_map/ppermute | solution.py:166
  79.7 21.3 %collective-permute-start.14 = (f32[10,8,128]{2,1,0:T(8,128)S(1)}, f32[10,8,128]{2,1,0:T(8,128)S(1)}, u32[]{:S(2)}, u32[]{:S(2)}) collective-permute-start(f32[10,8,128]{2,1,0:T(8,128)S(1)} %add_add_fusion.1), channel_id=1, source_target_pairs={{0,4},{1,5},{8,12},{9,13},{16,20},{17,21},{24,28},{25,29},{32,36},... | collective-permute-start | bytes 122888 | tf_op jit(solution)/shard_map/ppermute | solution.py:166
  81.0 20.0 %collective-permute-start.15 = (f32[10,8,128]{2,1,0:T(8,128)S(1)}, f32[10,8,128]{2,1,0:T(8,128)S(1)}, u32[]{:S(2)}, u32[]{:S(2)}) collective-permute-start(f32[10,8,128]{2,1,0:T(8,128)S(1)} %add_add_fusion.1), channel_id=1, source_target_pairs={{0,6},{1,7},{8,14},{9,15},{16,22},{17,23},{24,30},{25,31},{32,38},... | collective-permute-start | bytes 122888 | tf_op jit(solution)/shard_map/ppermute | solution.py:166

commit v2 on v1

v2 whole, which is shorter than its diff:
```python
import functools

import jax, jax.numpy as jnp
from jax import lax
from jax.experimental import pallas as pl
from jax.experimental.pallas import tpu as pltpu
from jax.sharding import PartitionSpec as P

HI = lax.Precision.HIGHEST
B = 128
S8 = 8

def rep(x):
    return jnp.broadcast_to(x, (S8, B))

def factor_tile(d_ref, m_ref, lt_ref):
    tiles = B // S8
    for b in range(tiles):
        rows = pl.ds(b * S8, S8)
        d = d_ref[rows, :]
        m = m_ref[rows, :]
        cols = [rep(d[:, b * S8 + k : b * S8 + k + 1]) for k in range(S8)]
        s = {}
        for i in range(S8):
            for k in range(i, S8):
                s[i, k] = rep(cols[k][i : i + 1, :])
        rd = [rep(d[j : j + 1, :]) for j in range(S8)]
        rm = [rep(m[j : j + 1, :]) for j in range(S8)]
        u, qd, qm, scale = {}, [], [], []
        for j in range(S8):
            inv = 1.0 / s[j, j]
            scale.append(lax.rsqrt(s[j, j]))
            for k in range(j + 1, S8):
                u[j, k] = s[j, k] * inv
            for i in range(j + 1, S8):
                for k in range(i, S8):
                    s[i, k] = s[i, k] - s[j, i] * u[j, k]
            qd.append(rd[j] * inv)
            qm.append(rm[j] * inv)
            for k in range(j + 1, S8):
                rd[k] = rd[k] - s[j, k] * qd[j]
                rm[k] = rm[k] - s[j, k] * qm[j]
        for t in range(b + 1, tiles):
            at = pl.ds(t * S8, S8)
            dt = d_ref[at, :]
            mt = m_ref[at, :]
            c = [rep(dt[:, b * S8 + k : b * S8 + k + 1]) for k in range(S8)]
            for j in range(S8):
                for k in range(j + 1, S8):
                    c[k] = c[k] - c[j] * u[j, k]
            for j in range(S8):
                dt = dt - c[j] * qd[j]
                mt = mt - c[j] * qm[j]
            d_ref[at, :] = dt
            m_ref[at, :] = mt
        sub = lax.broadcasted_iota(jnp.int32, (S8, B), 0)
        od, om = rd[0] * scale[0], rm[0] * scale[0]
        for j in range(1, S8):
            od = jnp.where(sub == j, rd[j] * scale[j], od)
            om = jnp.where(sub == j, rm[j] * scale[j], om)
        lt_ref[rows, :] = od
        m_ref[rows, :] = om

def dot(a, b, dims=((1,), (0,))):
    return lax.dot_general(a, b, (dims, ((), ())), precision=HI, preferred_element_type=jnp.float32)

BLOCKS = tuple((i, j) for i in range(4) for j in range(i + 1))
N = 4 * B


def eliminate(first, last, l_ref, inv_ref, s_ref, d_ref, m_ref, lt_ref):
    r128 = lax.broadcasted_iota(jnp.int32, (B, B), 0)
    c128 = lax.broadcasted_iota(jnp.int32, (B, B), 1)
    eye = jnp.where(r128 == c128, 1.0, 0.0).astype(jnp.float32)
    for k in range(first, last):
        lo, hi = k * B, (k + 1) * B
        d_ref[...] = s_ref[lo:hi, lo:hi]
        m_ref[...] = eye
        factor_tile(d_ref, m_ref, lt_ref)
        inv = m_ref[...]
        l_ref[lo:hi, lo:hi] = jnp.where(r128 >= c128, lt_ref[...].T, 0.0)
        inv_ref[lo:hi, lo:hi] = inv
        if k:
            inv_ref[lo:hi, :lo] = dot(inv, inv_ref[lo:hi, :lo])
        if hi < N:
            below = dot(s_ref[hi:, lo:hi], inv, ((1,), (1,)))
            l_ref[hi:, lo:hi] = below
            for i in range(k + 1, N // B):
                a, z = i * B, (i + 1) * B
                mine = below[a - hi : z - hi]
                s_ref[a:z, hi:z] -= dot(mine, below[: z - hi], ((1,), (1,)))
                inv_ref[a:z, :hi] -= dot(mine, inv_ref[lo:hi, :hi])


def first_kernel(g_ref, after_ref, s_ref, l_ref, inv_ref, d_ref, m_ref, lt_ref):
    del after_ref
    s_ref[...] = jnp.zeros((N, N), jnp.float32)
    for at, (i, j) in enumerate(BLOCKS):
        s_ref[i * B : (i + 1) * B, j * B : (j + 1) * B] = g_ref[:, at].reshape(B, B)
    inv_ref[...] = jnp.zeros((N, N), jnp.float32)
    l_ref[...] = jnp.zeros((N, N), jnp.float32)
    eliminate(0, 2, l_ref, inv_ref, s_ref, d_ref, m_ref, lt_ref)


def second_kernel(s_in, l_in, inv_in, after_ref, s_ref, l_ref, inv_ref, d_ref, m_ref, lt_ref):
    del s_in, l_in, inv_in, after_ref
    eliminate(2, 4, l_ref, inv_ref, s_ref, d_ref, m_ref, lt_ref)


def whole():
    return pl.BlockSpec(memory_space=pltpu.VMEM)


def anywhere():
    return pl.BlockSpec(memory_space=pl.ANY)


PARAMS = pltpu.CompilerParams(vmem_limit_bytes=40 * 2**20)
SQUARE = jax.ShapeDtypeStruct((N, N), jnp.float32)


def first_half(gathered, after):
    return pl.pallas_call(
        first_kernel,
        out_shape=(SQUARE,) * 3,
        in_specs=[whole(), anywhere()],
        out_specs=(whole(),) * 3,
        scratch_shapes=[pltpu.VMEM((B, B), jnp.float32)] * 3,
        compiler_params=PARAMS,
    )(gathered, after)


def second_half(s, lower, inv, after):
    return pl.pallas_call(
        second_kernel,
        out_shape=(SQUARE,) * 3,
        in_specs=[whole()] * 3 + [anywhere()],
        out_specs=(whole(),) * 3,
        input_output_aliases={0: 0, 1: 1, 2: 2},
        scratch_shapes=[pltpu.VMEM((B, B), jnp.float32)] * 3,
        compiler_params=PARAMS,
    )(s, lower, inv, after)


def final_kernel(x_ref, own_ref, other_ref, top_ref, l_ref, inv_ref, panel_ref, out_ref, u_ref, f_ref):
    row, col = lax.axis_index("row"), lax.axis_index("col")
    inv = inv_ref[...]
    top = jnp.concatenate([top_ref[:, 0, i].reshape(B, -1) for i in range(4)], axis=0)
    u_ref[...] = dot(inv, top)
    even = lax.rem(col, 2) == 0
    half = 2 * B

    def factor(left_ref, right_ref):
        f_ref[:, :half] = dot(left_ref[...], inv[:half, :half], ((1,), (1,)))
        f_ref[:, half:] = dot(left_ref[...], inv[half:, :half], ((1,), (1,))) + dot(
            right_ref[...], inv[half:, half:], ((1,), (1,))
        )

    @pl.when(jnp.logical_and(row > 0, even))
    def _():
        factor(own_ref, other_ref)

    @pl.when(jnp.logical_and(row > 0, jnp.logical_not(even)))
    def _():
        factor(other_ref, own_ref)

    @pl.when(row == 0)
    def _():
        f_ref[...] = l_ref[...]

    panel_ref[...] = f_ref[pl.ds(pl.multiple_of(col * 16, 16), 16), :]
    live = jnp.logical_and(row > 0, col > 1)

    @pl.when(live)
    def _():
        out_ref[...] = x_ref[...] - dot(f_ref[...], u_ref[...])

    @pl.when(jnp.logical_not(live))
    def _():
        out_ref[...] = jnp.zeros_like(out_ref)


def final(x, own, other, top, lower, inv):
    return pl.pallas_call(
        final_kernel,
        out_shape=(
            jax.ShapeDtypeStruct((16, 512), jnp.float32),
            jax.ShapeDtypeStruct((512, 256), jnp.float32),
        ),
        in_specs=[whole()] * 6,
        out_specs=(whole(), whole()),
        scratch_shapes=[pltpu.VMEM((512, 256), jnp.float32), pltpu.VMEM((512, 512), jnp.float32)],
        compiler_params=PARAMS,
    )(x, own, other, top, lower, inv)


def either(value, options):
    found = value == options[0]
    for option in options[1:]:
        found = jnp.logical_or(found, value == option)
    return found


def merge_kernel(takes, have_ref, got_ref, after_ref, out_ref):
    del after_ref
    col = lax.axis_index("col")
    take = takes(col // 8, lax.rem(col, 8))

    @pl.when(take)
    def _():
        out_ref[...] = got_ref[...]

    @pl.when(jnp.logical_not(take))
    def _():
        out_ref[...] = have_ref[...]


def merge(takes, have, got, after):
    return pl.pallas_call(
        functools.partial(merge_kernel, takes),
        out_shape=jax.ShapeDtypeStruct(have.shape, have.dtype),
        in_specs=[whole(), whole(), anywhere()],
        out_specs=whole(),
        compiler_params=PARAMS,
    )(have, got, after)


def pack_kernel(piece_ref, swapped_ref, out_ref):
    col = lax.axis_index("col")

    def put(left_ref, right_ref):
        for at, (i, j) in enumerate(BLOCKS):
            side_ref = left_ref if j < 2 else right_ref
            out_ref[at] = side_ref[i, :, (j % 2) * B : (j % 2 + 1) * B]

    @pl.when(col == 0)
    def _():
        put(piece_ref, swapped_ref)

    @pl.when(col == 1)
    def _():
        put(swapped_ref, piece_ref)

    @pl.when(col > 1)
    def _():
        out_ref[...] = jnp.zeros_like(out_ref)


def pack(piece, swapped):
    return pl.pallas_call(
        pack_kernel,
        out_shape=jax.ShapeDtypeStruct((len(BLOCKS), 8, B), jnp.float32),
        in_specs=[whole()] * 2,
        out_specs=whole(),
        compiler_params=PARAMS,
    )(piece, swapped)


def on_device(x):
    planes = range(0, 32, 8)

    def send(v, pairs):
        return lax.ppermute(v, "col", pairs)

    got = send(x, [(0, 16), (1, 17)])

    split = x.reshape(4, 16, 8, 256).transpose(1, 0, 2, 3)
    turned = lax.all_to_all(split, "row", 0, 0)
    piece = turned[0]
    top = lax.all_gather(turned[:2], "row")
    half = merge(lambda z, xi: z != 0, x, got, piece)
    got = send(half, [(0, 8), (1, 9), (16, 24), (17, 25)])

    packed = pack(piece, send(piece, [(0, 1), (1, 0)]))
    packed += sum(send(packed, [(0, 8 * q), (1, 8 * q + 1)]) for q in range(1, 4))
    half = merge(lambda z, xi: lax.rem(z, 2) == 1, half, got, packed)
    got = send(half, [(p + i, p + j) for p in planes for i, j in ((0, 6), (1, 3))])
    packed += sum(send(packed, [(p + i, p + i + s) for p in planes for i in (0, 1)]) for s in (2, 4, 6))
    gathered = lax.all_gather(packed, "row")

    half = merge(lambda z, xi: either(xi, (3, 6)), half, got, gathered)
    got = send(half, [(p + i, p + j) for p in planes for i, j in ((0, 2), (6, 4), (1, 7), (3, 5))])
    state = first_half(gathered, half)
    half = merge(lambda z, xi: either(xi, (2, 4, 5, 7)), half, got, state[0])
    other = send(half, [(i, i ^ 1) for i in range(32)])
    _, lower, inv = second_half(*state, half)
    return final(x, half, other, top, lower, inv)


def solution(mesh):
    return jax.shard_map(
        on_device,
        mesh=mesh,
        in_specs=(P("row", "col"),),
        out_specs=(P(("row", "col"), None), P("row", "col")),
        check_vma=False,
    )
```

time: 153 us -> 126 us (0.82)
  blocking collectives: 35.7 us -> 20.5 us
  between operations: 0.99 us -> 14.2 us
  starting transfers between devices: 57.4 us -> 44.8 us
  Pallas kernels: 34.3 us -> 25.9 us
  waiting for transfers between devices: 21.8 us -> 15.4 us
  local copies, waits for them, and re-layouts: 2 us -> 3.76 us
    all_gather x1 -> x0, blocking collectives: 18.6 us -> none  [on_device(): top = lax.all_gather(piece, 'row')]
    ppermute x16 -> x12, starting transfers between devices: 49.4 us -> 34.4 us  [send(): return lax.ppermute(v, 'col', pairs)]
    ppermute x16 -> x12, waiting for transfers between devices: 18.6 us -> 7.16 us  [send(): return lax.ppermute(v, 'col', pairs)]
    pallas_call x1 -> x7, Pallas kernels: 29.1 us -> 21.5 us  [the longest x1 11.3 us: first_half(): pl.pallas_call(first_kernel, out_shape=(SQUARE,) * 3, in_specs=[whole(),...]
    all_to_all x1, waiting for transfers between devices: 3.17 us -> 8.22 us  [on_device(): turned = lax.all_to_all(split, 'row', 0, 0)]
    all_gather x1, blocking collectives: 17.1 us -> 20.5 us  [on_device(): gathered = lax.all_gather(packed, 'row')]
    all_to_all x1, starting transfers between devices: 8.07 us -> 10.4 us  [on_device(): turned = lax.all_to_all(split, 'row', 0, 0)]
    reshape x0 -> x1, local copies, waits for them, and re-layouts: none -> 1.89 us  [on_device(): split = x.reshape(4, 16, 8, 256).transpose(1, 0, 2, 3)]
  transfers between devices with their start and end apart: 17 -> 14, of which waited for: 6 -> 6; matrix products, arithmetic and copies ran while one was open for 1% -> 1% of each run, Pallas kernels for 0% -> 17%
where the time goes in v2:
time: 126 us; the launch traced here: 125 us
  starting transfers between devices  44.8 us (36%)
  Pallas kernels  25.9 us (21%)
  blocking collectives  20.5 us (16%)
  waiting for transfers between devices  15.4 us (12%)
  between operations  14.2 us (11%)
  local copies, waits for them, and re-layouts  3.76 us (3%)
    ppermute x12, starting transfers between devices, send(): return lax.ppermute(v, 'col', pairs)  34.4 us
    all_gather x1, blocking collectives, on_device(): gathered = lax.all_gather(packed, 'row')  20.5 us
    pallas_call x1, Pallas kernels, first_half(): pl.pallas_call(first_kernel, out_shape=(SQUARE,) * 3, in_specs=[whole(),...  11.3 us
    all_to_all x1, starting transfers between devices, on_device(): turned = lax.all_to_all(split, 'row', 0, 0)  10.4 us
    pallas_call x1, Pallas kernels, second_half(): pl.pallas_call(second_kernel, out_shape=(SQUARE,) * 3, in_specs=[whole()]...  9.94 us
    all_to_all x1, waiting for transfers between devices, on_device(): turned = lax.all_to_all(split, 'row', 0, 0)  8.22 us
    ppermute x12, waiting for transfers between devices, send(): return lax.ppermute(v, 'col', pairs)  7.16 us
    pallas_call x1, Pallas kernels, final(): pl.pallas_call(final_kernel, out_shape=(jax.ShapeDtypeStruct((16, 512), j...  4.43 us
  transfers between devices with their start and end apart: 14, of which 6 were waited for; matrix products, arithmetic and copies ran while one was open for 1% of the time, Pallas kernels for 17%

profile of v2, /device:TPU:1, one launch (start us, length us, event | category | flops | bytes accessed | tf_op | source)
XLA Modules:
  0.0 124.7 jit_solution(11481902027429176222)
XLA Ops:
  7.2 1.9 %copy.9 = f32[4,16,8,256]{3,2,0,1:T(8,128)} copy(f32[4,16,8,256]{3,2,1,0:T(8,128)} %bitcast.10) | data formatting | bytes 1048576 | tf_op jit(solution)/shard_map/reshape | solution.py:267
  9.1 10.4 %all-to-all-start = ((f32[16,4,8,256]{3,2,1,0:T(8,128)}), f32[16,4,8,256]{3,2,1,0:T(8,128)S(1)}, u32[]{:S(2)}, u32[]{:S(2)}) async-start(f32[16,4,8,256]{3,2,1,0:T(8,128)} %bitcast.7), calls=%async_computation | async-start | bytes 1048576 | tf_op jit(solution)/shard_map/all_to_all | solution.py:268
  19.4 0.0 all-gather.4.cloned.1.call-start
  19.5 9.1 %collective-permute-start = (f32[512,256]{1,0:T(8,128)S(1)}, f32[512,256]{1,0:T(8,128)S(1)}, u32[]{:S(2)}, u32[]{:S(2)}) collective-permute-start(f32[512,256]{1,0:T(8,128)S(1)} %copy-done), channel_id=1, source_target_pairs={{0,16},{1,17},{32,48},{33,49},{64,80},{65,81},{96,112},{97,113},{1... | collective-permute-start | bytes 1572872 | tf_op jit(solution)/shard_map/ppermute | solution.py:263
  28.6 8.2 %all-to-all-done = f32[16,4,8,256]{3,2,1,0:T(8,128)S(1)} async-done(((f32[16,4,8,256]{3,2,1,0:T(8,128)}), f32[16,4,8,256]{3,2,1,0:T(8,128)S(1)}, u32[]{:S(2)}, u32[]{:S(2)}) %all-to-all-start) | async-done | bytes 524320 | tf_op jit(solution)/shard_map/all_to_all | solution.py:268
  36.8 3.0 %collective-permute-done.got_ref = f32[512,256]{1,0:T(8,128)S(1)} collective-permute-done((f32[512,256]{1,0:T(8,128)S(1)}, f32[512,256]{1,0:T(8,128)S(1)}, u32[]{:S(2)}, u32[]{:S(2)}) %collective-permute-start) | collective-permute-done | bytes 524320 | tf_op jit(solution)/shard_map/ppermute | solution.py:263
  39.8 1.3 %collective-permute-start.1 = (f32[512,256]{1,0:T(8,128)S(1)}, f32[512,256]{1,0:T(8,128)S(1)}, u32[]{:S(2)}, u32[]{:S(2)}) collective-permute-start(f32[512,256]{1,0:T(8,128)S(1)} %shard_map.30.have_ref), channel_id=1, source_target_pairs={{0,8},{1,9},{16,24},{17,25},{32,40},{33,41},{48,56},{49,57},{64,72... | collective-permute-start | bytes 1572872 | tf_op jit(solution)/shard_map/ppermute | solution.py:263
  41.1 0.6 slice.9
  41.8 0.0 all-gather.4.cloned.1.call-update
  41.8 3.1 %collective-permute-start.2 = (f32[4,8,256]{2,1,0:T(8,128)S(1)}, f32[4,8,256]{2,1,0:T(8,128)S(1)}, u32[]{:S(2)}, u32[]{:S(2)}) collective-permute-start(f32[4,8,256]{2,1,0:T(8,128)S(1)} %slice_bitcast_fusion.after_ref.piece_ref), channel_id=1, source_target_pairs={{0,1},{1,0},{32,33},{33,32},{64,65},{65,64},{96,97},{97,96},{128,1... | collective-permute-start | bytes 98312 | tf_op jit(solution)/shard_map/ppermute | solution.py:263
  44.9 1.5 %collective-permute-done.2.swapped_ref = f32[4,8,256]{2,1,0:T(8,128)S(1)} collective-permute-done((f32[4,8,256]{2,1,0:T(8,128)S(1)}, f32[4,8,256]{2,1,0:T(8,128)S(1)}, u32[]{:S(2)}, u32[]{:S(2)}) %collective-permute-start.2) | collective-permute-done | bytes 32800 | tf_op jit(solution)/shard_map/ppermute | solution.py:263
  46.5 1.3 %collective-permute-start.3 = (f32[10,8,128]{2,1,0:T(8,128)S(1)}, f32[10,8,128]{2,1,0:T(8,128)S(1)}, u32[]{:S(2)}, u32[]{:S(2)}) collective-permute-start(f32[10,8,128]{2,1,0:T(8,128)S(1)} %shard_map.31), channel_id=1, source_target_pairs={{0,8},{1,9},{32,40},{33,41},{64,72},{65,73},{96,104},{97,105},{128... | collective-permute-start | bytes 122888 | tf_op jit(solution)/shard_map/ppermute | solution.py:263
  47.8 4.2 %collective-permute-start.4 = (f32[10,8,128]{2,1,0:T(8,128)S(1)}, f32[10,8,128]{2,1,0:T(8,128)S(1)}, u32[]{:S(2)}, u32[]{:S(2)}) collective-permute-start(f32[10,8,128]{2,1,0:T(8,128)S(1)} %shard_map.31), channel_id=1, source_target_pairs={{0,16},{1,17},{32,48},{33,49},{64,80},{65,81},{96,112},{97,113},{1... | collective-permute-start | bytes 122888 | tf_op jit(solution)/shard_map/ppermute | solution.py:263
  51.9 1.3 %collective-permute-start.5 = (f32[10,8,128]{2,1,0:T(8,128)S(1)}, f32[10,8,128]{2,1,0:T(8,128)S(1)}, u32[]{:S(2)}, u32[]{:S(2)}) collective-permute-start(f32[10,8,128]{2,1,0:T(8,128)S(1)} %shard_map.31), channel_id=1, source_target_pairs={{0,24},{1,25},{32,56},{33,57},{64,88},{65,89},{96,120},{97,121},{1... | collective-permute-start | bytes 122888 | tf_op jit(solution)/shard_map/ppermute | solution.py:263
  53.2 0.0 collective-permute-done.3
  53.2 0.3 collective-permute-done.4
  53.5 0.8 collective-permute-done.5
  54.3 1.3 %collective-permute-start.7 = (f32[10,8,128]{2,1,0:T(8,128)S(1)}, f32[10,8,128]{2,1,0:T(8,128)S(1)}, u32[]{:S(2)}, u32[]{:S(2)}) collective-permute-start(f32[10,8,128]{2,1,0:T(8,128)S(1)} %add_add_fusion.1.after_ref), channel_id=1, source_target_pairs={{0,2},{1,3},{8,10},{9,11},{16,18},{17,19},{24,26},{25,27},{32,34},... | collective-permute-start | bytes 122888 | tf_op jit(solution)/shard_map/ppermute | solution.py:263
  55.6 1.3 %collective-permute-start.8 = (f32[10,8,128]{2,1,0:T(8,128)S(1)}, f32[10,8,128]{2,1,0:T(8,128)S(1)}, u32[]{:S(2)}, u32[]{:S(2)}) collective-permute-start(f32[10,8,128]{2,1,0:T(8,128)S(1)} %add_add_fusion.1.after_ref), channel_id=1, source_target_pairs={{0,4},{1,5},{8,12},{9,13},{16,20},{17,21},{24,28},{25,29},{32,36},... | collective-permute-start | bytes 122888 | tf_op jit(solution)/shard_map/ppermute | solution.py:263
  56.9 1.3 %collective-permute-start.9 = (f32[10,8,128]{2,1,0:T(8,128)S(1)}, f32[10,8,128]{2,1,0:T(8,128)S(1)}, u32[]{:S(2)}, u32[]{:S(2)}) collective-permute-start(f32[10,8,128]{2,1,0:T(8,128)S(1)} %add_add_fusion.1.after_ref), channel_id=1, source_target_pairs={{0,6},{1,7},{8,14},{9,15},{16,22},{17,23},{24,30},{25,31},{32,38},... | collective-permute-start | bytes 122888 | tf_op jit(solution)/shard_map/ppermute | solution.py:263
  58.2 0.1 shard_map.32.have_ref
  58.3 1.3 %collective-permute-start.6 = (f32[512,256]{1,0:T(8,128)S(1)}, f32[512,256]{1,0:T(8,128)S(1)}, u32[]{:S(2)}, u32[]{:S(2)}) collective-permute-start(f32[512,256]{1,0:T(8,128)S(1)} %shard_map.32.have_ref), channel_id=1, source_target_pairs={{0,6},{1,3},{8,14},{9,11},{16,22},{17,19},{24,30},{25,27},{32,38},... | collective-permute-start | bytes 1572872 | tf_op jit(solution)/shard_map/ppermute | solution.py:263
  59.7 20.5 %all-gather = f32[160,8,128]{2,1,0:T(8,128)S(1)} all-gather(f32[10,8,128]{2,1,0:T(8,128)S(1)} %add_add_fusion), channel_id=2, replica_groups=mesh['row'=16,'col'=32] {'row'}, dimensions={0}, use_global_device_ids=true | all-gather | bytes 696320 | tf_op jit(solution)/shard_map/all_gather | solution.py:279
  80.2 2.5 %collective-permute-start.10 = (f32[512,256]{1,0:T(8,128)S(1)}, f32[512,256]{1,0:T(8,128)S(1)}, u32[]{:S(2)}, u32[]{:S(2)}) collective-permute-start(f32[512,256]{1,0:T(8,128)S(1)} %shard_map.33.after_ref.have_ref), channel_id=1, source_target_pairs={{0,2},{6,4},{1,7},{3,5},{8,10},{14,12},{9,15},{11,13},{16,18},{22,... | collective-permute-start | bytes 1572872 | tf_op jit(solution)/shard_map/ppermute | solution.py:263
  82.7 11.3 %shard_map.34 = (f32[512,512]{1,0:T(8,128)S(1)}, f32[512,512]{1,0:T(8,128)S(1)}, f32[512,512]{1,0:T(8,128)S(1)}) custom-call(f32[16,10,8,128]{3,2,1,0:T(8,128)S(1)} %bitcast.9, f32[512,256]{1,0:T(8,128)S(1)} %shard_map.33.after_ref.have_ref), custom_call_target="tpu_custom_call" | custom-call | tf_op jit(solution)/shard_map/pallas_call | solution.py:123
  94.1 0.1 shard_map.35.after_ref.own_ref
  94.2 6.5 %collective-permute-start.11 = (f32[512,256]{1,0:T(8,128)S(1)}, f32[512,256]{1,0:T(8,128)}, u32[]{:S(2)}, u32[]{:S(2)}) collective-permute-start(f32[512,256]{1,0:T(8,128)S(1)} %shard_map.35.after_ref.own_ref), channel_id=1, source_target_pairs={{0,1},{1,0},{2,3},{3,2},{4,5},{5,4},{6,7},{7,6},{8,9},{9,8},{10,11... | collective-permute-start | bytes 1572872 | tf_op jit(solution)/shard_map/ppermute | solution.py:263
  100.7 9.9 %shard_map.36 = (f32[512,512]{1,0:T(8,128)S(1)}, f32[512,512]{1,0:T(8,128)S(1)}, f32[512,512]{1,0:T(8,128)S(1)}) custom-call(f32[512,512]{1,0:T(8,128)S(1)} %get-tuple-element.7.after_ref.s_in, f32[512,512]{1,0:T(8,128)S(1)} %get-tuple-element.8.l_in, ...), custom_call_target="tpu_custom_call", output_to_operand_aliasing={{0}: (0, {}), {1}: (1, {}), {2}: (2, {})} | custom-call | tf_op jit(solution)/shard_map/pallas_call | solution.py:134
  110.6 0.0 all-gather.4.cloned.1.call-done
  110.7 1.5 %collective-permute-done.11.other_ref = f32[512,256]{1,0:T(8,128)} collective-permute-done((f32[512,256]{1,0:T(8,128)S(1)}, f32[512,256]{1,0:T(8,128)}, u32[]{:S(2)}, u32[]{:S(2)}) %collective-permute-start.11) | collective-permute-done | bytes 524320 | tf_op jit(solution)/shard_map/ppermute | solution.py:263
  112.2 1.2 copy-done.1
  113.4 4.4 %shard_map.37 = (f32[16,512]{1,0:T(8,128)}, f32[512,256]{1,0:T(8,128)}) custom-call(f32[512,256]{1,0:T(8,128)S(1)} %copy-done, f32[512,256]{1,0:T(8,128)S(1)} %shard_map.35.after_ref.own_ref, f32[512,256]{1,0:T(8,128)} %collective-permute-done.11.other_ref, f32[16,2,4,8,256]{4,3,2,1,0:T(8,128)S(1)} %bitcast.11, f32[512,512]{1,0:T(8,128)S(1)} %get-tuple-element.10.l_ref, ...), custom_call_target="tpu_custom_call" | custom-call | tf_op jit(solution)/shard_map/pallas_call | solution.py:184
  (15 shorter events, 0.1 us)
Async XLA Ops:
  9.1 10.4 %copy-start = (f32[512,256]{1,0:T(8,128)S(1)}, f32[512,256]{1,0:T(8,128)}, u32[]{:S(2)}) copy-start(f32[512,256]{1,0:T(8,128)} %x_ref.1) | copy-start | bytes 1572868
  9.1 27.7 %all-to-all-start = ((f32[16,4,8,256]{3,2,1,0:T(8,128)}), f32[16,4,8,256]{3,2,1,0:T(8,128)S(1)}, u32[]{:S(2)}, u32[]{:S(2)}) async-start(f32[16,4,8,256]{3,2,1,0:T(8,128)} %bitcast.7), calls=%async_computation | async-start | bytes 1048576 | tf_op jit(solution)/shard_map/all_to_all | solution.py:268
  19.4 91.2 %all-gather.4.cloned.1.call-start = ((), (), s32[]{:S(2)}) async-start(), calls=%async_computation.1 | async-start | bytes 1114112 | tf_op jit(solution)/shard_map/all_gather | solution.py:270
  19.5 20.3 %collective-permute-start = (f32[512,256]{1,0:T(8,128)S(1)}, f32[512,256]{1,0:T(8,128)S(1)}, u32[]{:S(2)}, u32[]{:S(2)}) collective-permute-start(f32[512,256]{1,0:T(8,128)S(1)} %copy-done), channel_id=1, source_target_pairs={{0,16},{1,17},{32,48},{33,49},{64,80},{65,81},{96,112},{97,113},{1... | collective-permute-start | bytes 1572872 | tf_op jit(solution)/shard_map/ppermute | solution.py:263
  39.8 18.4 %collective-permute-start.1 = (f32[512,256]{1,0:T(8,128)S(1)}, f32[512,256]{1,0:T(8,128)S(1)}, u32[]{:S(2)}, u32[]{:S(2)}) collective-permute-start(f32[512,256]{1,0:T(8,128)S(1)} %shard_map.30.have_ref), channel_id=1, source_target_pairs={{0,8},{1,9},{16,24},{17,25},{32,40},{33,41},{48,56},{49,57},{64,72... | collective-permute-start | bytes 1572872 | tf_op jit(solution)/shard_map/ppermute | solution.py:263
  41.8 4.7 %collective-permute-start.2 = (f32[4,8,256]{2,1,0:T(8,128)S(1)}, f32[4,8,256]{2,1,0:T(8,128)S(1)}, u32[]{:S(2)}, u32[]{:S(2)}) collective-permute-start(f32[4,8,256]{2,1,0:T(8,128)S(1)} %slice_bitcast_fusion.after_ref.piece_ref), channel_id=1, source_target_pairs={{0,1},{1,0},{32,33},{33,32},{64,65},{65,64},{96,97},{97,96},{128,1... | collective-permute-start | bytes 98312 | tf_op jit(solution)/shard_map/ppermute | solution.py:263
  46.5 6.7 %collective-permute-start.3 = (f32[10,8,128]{2,1,0:T(8,128)S(1)}, f32[10,8,128]{2,1,0:T(8,128)S(1)}, u32[]{:S(2)}, u32[]{:S(2)}) collective-permute-start(f32[10,8,128]{2,1,0:T(8,128)S(1)} %shard_map.31), channel_id=1, source_target_pairs={{0,8},{1,9},{32,40},{33,41},{64,72},{65,73},{96,104},{97,105},{128... | collective-permute-start | bytes 122888 | tf_op jit(solution)/shard_map/ppermute | solution.py:263
  47.8 5.8 %collective-permute-start.4 = (f32[10,8,128]{2,1,0:T(8,128)S(1)}, f32[10,8,128]{2,1,0:T(8,128)S(1)}, u32[]{:S(2)}, u32[]{:S(2)}) collective-permute-start(f32[10,8,128]{2,1,0:T(8,128)S(1)} %shard_map.31), channel_id=1, source_target_pairs={{0,16},{1,17},{32,48},{33,49},{64,80},{65,81},{96,112},{97,113},{1... | collective-permute-start | bytes 122888 | tf_op jit(solution)/shard_map/ppermute | solution.py:263
  51.9 2.4 %collective-permute-start.5 = (f32[10,8,128]{2,1,0:T(8,128)S(1)}, f32[10,8,128]{2,1,0:T(8,128)S(1)}, u32[]{:S(2)}, u32[]{:S(2)}) collective-permute-start(f32[10,8,128]{2,1,0:T(8,128)S(1)} %shard_map.31), channel_id=1, source_target_pairs={{0,24},{1,25},{32,56},{33,57},{64,88},{65,89},{96,120},{97,121},{1... | collective-permute-start | bytes 122888 | tf_op jit(solution)/shard_map/ppermute | solution.py:263
  54.3 5.3 %collective-permute-start.7 = (f32[10,8,128]{2,1,0:T(8,128)S(1)}, f32[10,8,128]{2,1,0:T(8,128)S(1)}, u32[]{:S(2)}, u32[]{:S(2)}) collective-permute-start(f32[10,8,128]{2,1,0:T(8,128)S(1)} %add_add_fusion.1.after_ref), channel_id=1, source_target_pairs={{0,2},{1,3},{8,10},{9,11},{16,18},{17,19},{24,26},{25,27},{32,34},... | collective-permute-start | bytes 122888 | tf_op jit(solution)/shard_map/ppermute | solution.py:263
  55.6 4.0 %collective-permute-start.8 = (f32[10,8,128]{2,1,0:T(8,128)S(1)}, f32[10,8,128]{2,1,0:T(8,128)S(1)}, u32[]{:S(2)}, u32[]{:S(2)}) collective-permute-start(f32[10,8,128]{2,1,0:T(8,128)S(1)} %add_add_fusion.1.after_ref), channel_id=1, source_target_pairs={{0,4},{1,5},{8,12},{9,13},{16,20},{17,21},{24,28},{25,29},{32,36},... | collective-permute-start | bytes 122888 | tf_op jit(solution)/shard_map/ppermute | solution.py:263
  56.9 2.7 %collective-permute-start.9 = (f32[10,8,128]{2,1,0:T(8,128)S(1)}, f32[10,8,128]{2,1,0:T(8,128)S(1)}, u32[]{:S(2)}, u32[]{:S(2)}) collective-permute-start(f32[10,8,128]{2,1,0:T(8,128)S(1)} %add_add_fusion.1.after_ref), channel_id=1, source_target_pairs={{0,6},{1,7},{8,14},{9,15},{16,22},{17,23},{24,30},{25,31},{32,38},... | collective-permute-start | bytes 122888 | tf_op jit(solution)/shard_map/ppermute | solution.py:263
  58.3 21.9 %collective-permute-start.6 = (f32[512,256]{1,0:T(8,128)S(1)}, f32[512,256]{1,0:T(8,128)S(1)}, u32[]{:S(2)}, u32[]{:S(2)}) collective-permute-start(f32[512,256]{1,0:T(8,128)S(1)} %shard_map.32.have_ref), channel_id=1, source_target_pairs={{0,6},{1,3},{8,14},{9,11},{16,22},{17,19},{24,30},{25,27},{32,38},... | collective-permute-start | bytes 1572872 | tf_op jit(solution)/shard_map/ppermute | solution.py:263
  80.2 13.9 %collective-permute-start.10 = (f32[512,256]{1,0:T(8,128)S(1)}, f32[512,256]{1,0:T(8,128)S(1)}, u32[]{:S(2)}, u32[]{:S(2)}) collective-permute-start(f32[512,256]{1,0:T(8,128)S(1)} %shard_map.33.after_ref.have_ref), channel_id=1, source_target_pairs={{0,2},{6,4},{1,7},{3,5},{8,10},{14,12},{9,15},{11,13},{16,18},{22,... | collective-permute-start | bytes 1572872 | tf_op jit(solution)/shard_map/ppermute | solution.py:263
  94.2 18.0 %collective-permute-start.11 = (f32[512,256]{1,0:T(8,128)S(1)}, f32[512,256]{1,0:T(8,128)}, u32[]{:S(2)}, u32[]{:S(2)}) collective-permute-start(f32[512,256]{1,0:T(8,128)S(1)} %shard_map.35.after_ref.own_ref), channel_id=1, source_target_pairs={{0,1},{1,0},{2,3},{3,2},{4,5},{5,4},{6,7},{7,6},{8,9},{9,8},{10,11... | collective-permute-start | bytes 1572872 | tf_op jit(solution)/shard_map/ppermute | solution.py:263
  112.2 1.2 copy-start.1
Sparse Core Ops, SparseCore 0:
  41.9 41.8 all-gather.3

commit v3 on v2

--- a/solution.py
+++ b/solution.py
@@ -64,8 +64,9 @@
 def dot(a, b, dims=((1,), (0,))):
     return lax.dot_general(a, b, (dims, ((), ())), precision=HI, preferred_element_type=jnp.float32)
 
-BLOCKS = tuple((i, j) for i in range(4) for j in range(i + 1))
 N = 4 * B
+LEFT = ((0, 0), (1, 0), (1, 1), (2, 0), (3, 0))
+RIGHT = ((2, 2), (3, 2), (3, 3), (1, 2), (1, 3))
 
 
 def eliminate(first, last, l_ref, inv_ref, s_ref, d_ref, m_ref, lt_ref):
@@ -95,16 +96,20 @@
 def first_kernel(g_ref, after_ref, s_ref, l_ref, inv_ref, d_ref, m_ref, lt_ref):
     del after_ref
     s_ref[...] = jnp.zeros((N, N), jnp.float32)
-    for at, (i, j) in enumerate(BLOCKS):
-        s_ref[i * B : (i + 1) * B, j * B : (j + 1) * B] = g_ref[:, at].reshape(B, B)
+    for at, (i, j) in enumerate(LEFT + RIGHT):
+        for r in range(16):
+            p = (r % 2) * 8 + r // 2
+            s_ref[i * B + p * 8 : i * B + p * 8 + 8, j * B : (j + 1) * B] = g_ref[r, at]
+    for i, j in RIGHT[3:]:
+        s_ref[j * B : (j + 1) * B, i * B : (i + 1) * B] = s_ref[i * B : (i + 1) * B, j * B : (j + 1) * B].T
     inv_ref[...] = jnp.zeros((N, N), jnp.float32)
     l_ref[...] = jnp.zeros((N, N), jnp.float32)
-    eliminate(0, 2, l_ref, inv_ref, s_ref, d_ref, m_ref, lt_ref)
+    eliminate(0, 3, l_ref, inv_ref, s_ref, d_ref, m_ref, lt_ref)
 
 
 def second_kernel(s_in, l_in, inv_in, after_ref, s_ref, l_ref, inv_ref, d_ref, m_ref, lt_ref):
     del s_in, l_in, inv_in, after_ref
-    eliminate(2, 4, l_ref, inv_ref, s_ref, d_ref, m_ref, lt_ref)
+    eliminate(3, 4, l_ref, inv_ref, s_ref, d_ref, m_ref, lt_ref)
 
 
 def whole():
@@ -142,31 +147,27 @@
     )(s, lower, inv, after)
 
 
-def final_kernel(x_ref, own_ref, other_ref, top_ref, l_ref, inv_ref, panel_ref, out_ref, u_ref, f_ref):
+def final_kernel(x_ref, mine_ref, f1_ref, f2_ref, f3_ref, top_ref, far_ref, l_ref, inv_ref, panel_ref, out_ref, u_ref, f_ref):
     row, col = lax.axis_index("row"), lax.axis_index("col")
     inv = inv_ref[...]
-    top = jnp.concatenate([top_ref[:, 0, i].reshape(B, -1) for i in range(4)], axis=0)
-    u_ref[...] = dot(inv, top)
-    even = lax.rem(col, 2) == 0
-    half = 2 * B
-
-    def factor(left_ref, right_ref):
-        f_ref[:, :half] = dot(left_ref[...], inv[:half, :half], ((1,), (1,)))
-        f_ref[:, half:] = dot(left_ref[...], inv[half:, :half], ((1,), (1,))) + dot(
-            right_ref[...], inv[half:, half:], ((1,), (1,))
-        )
-
-    @pl.when(jnp.logical_and(row > 0, even))
-    def _():
-        factor(own_ref, other_ref)
-
-    @pl.when(jnp.logical_and(row > 0, jnp.logical_not(even)))
-    def _():
-        factor(other_ref, own_ref)
+
+    @pl.when(lax.rem(row, 2) == 0)
+    def _():
+        u_ref[...] = dot(inv, top_ref[...])
+
+    @pl.when(lax.rem(row, 2) == 1)
+    def _():
+        u_ref[...] = dot(inv, far_ref[...])
 
     @pl.when(row == 0)
     def _():
         f_ref[...] = l_ref[...]
+
+    @pl.when(row > 0)
+    def _():
+        for s, ref in enumerate((mine_ref, f1_ref, f2_ref, f3_ref)):
+            at = pl.multiple_of(lax.rem(col // 8 + 4 - s, 4) * B, B)
+            f_ref[pl.ds(at, B), :] = dot(ref[...], inv, ((1,), (1,)))
 
     panel_ref[...] = f_ref[pl.ds(pl.multiple_of(col * 16, 16), 16), :]
     live = jnp.logical_and(row > 0, col > 1)
@@ -180,18 +181,23 @@
         out_ref[...] = jnp.zeros_like(out_ref)
 
 
-def final(x, own, other, top, lower, inv):
+def final(x, mine, far, top, down, lower, inv):
     return pl.pallas_call(
         final_kernel,
         out_shape=(
             jax.ShapeDtypeStruct((16, 512), jnp.float32),
             jax.ShapeDtypeStruct((512, 256), jnp.float32),
         ),
-        in_specs=[whole()] * 6,
+        in_specs=[whole()] * 9,
         out_specs=(whole(), whole()),
         scratch_shapes=[pltpu.VMEM((512, 256), jnp.float32), pltpu.VMEM((512, 512), jnp.float32)],
         compiler_params=PARAMS,
-    )(x, own, other, top, lower, inv)
+    )(x, mine, *far, top, down, lower, inv)
+
+
+def place():
+    row, col = lax.axis_index("row"), lax.axis_index("col")
+    return row // 2, lax.rem(row, 2), col // 8, lax.rem(col, 8)
 
 
 def either(value, options):
@@ -201,90 +207,169 @@
     return found
 
 
-def merge_kernel(takes, have_ref, got_ref, after_ref, out_ref):
-    del after_ref
-    col = lax.axis_index("col")
-    take = takes(col // 8, lax.rem(col, 8))
-
+def choose(out_ref, take, yes_ref, no_ref):
     @pl.when(take)
     def _():
-        out_ref[...] = got_ref[...]
+        out_ref[...] = yes_ref[...]
 
     @pl.when(jnp.logical_not(take))
     def _():
-        out_ref[...] = have_ref[...]
-
-
-def merge(takes, have, got, after):
-    return pl.pallas_call(
-        functools.partial(merge_kernel, takes),
-        out_shape=jax.ShapeDtypeStruct(have.shape, have.dtype),
-        in_specs=[whole(), whole(), anywhere()],
+        out_ref[...] = no_ref[...]
+
+
+def like(*values):
+    return tuple(jax.ShapeDtypeStruct(v.shape, v.dtype) for v in values)
+
+
+def local(kernel, values, outs, aliases={}):
+    return pl.pallas_call(
+        kernel,
+        out_shape=outs,
+        in_specs=[whole()] * len(values),
+        out_specs=(whole(),) * len(outs),
+        input_output_aliases=aliases,
+        compiler_params=PARAMS,
+    )(*values)
+
+
+def spread_kernel(x_ref, f1_ref, f2_ref, f3_ref, cur_ref, half_ref, piece_ref):
+    y, core, z, xi = place()
+    for q, ref in enumerate((None, f1_ref, f2_ref, f3_ref)):
+
+        @pl.when(z == q)
+        def _(q=q, ref=ref):
+            half_ref[...] = x_ref[:B] if q == 0 else ref[...]
+
+    holds = jnp.logical_and(z == 0, xi < 2)
+
+    @pl.when(holds)
+    def _():
+        piece_ref[...] = cur_ref[0]
+
+    @pl.when(jnp.logical_not(holds))
+    def _():
+        piece_ref[...] = jnp.zeros_like(piece_ref)
+
+
+def pair_kernel(own_ref, other_ref, half_ref, far_ref, x_ref, down_ref, both_ref, half_out, top_ref):
+    y, core, z, xi = place()
+    even = lax.rem(xi, 2) == 0
+
+    @pl.when(z > 0)
+    def _():
+        both_ref[...] = jnp.zeros_like(both_ref)
+
+    @pl.when(jnp.logical_and(z == 0, even))
+    def _():
+        both_ref[:5] = own_ref[...]
+        both_ref[5:] = other_ref[...]
+
+    @pl.when(jnp.logical_and(z == 0, jnp.logical_not(even)))
+    def _():
+        both_ref[:5] = other_ref[...]
+        both_ref[5:] = own_ref[...]
+
+    choose(half_out, xi >= 4, far_ref, half_ref)
+    choose(top_ref, y >= 4, down_ref, x_ref)
+
+
+def sum_kernel(b0_ref, b1_ref, b2_ref, b3_ref, half_ref, far_ref, both_ref, half_out):
+    y, core, z, xi = place()
+    both_ref[...] = (b0_ref[...] + b1_ref[...]) + (b2_ref[...] + b3_ref[...])
+    choose(half_out, either(lax.rem(xi, 4), (2, 3)), far_ref, half_ref)
+
+
+def join_kernel(g_in, half_ref, far_ref, top_ref, down_ref, g_ref, mine_ref, top_out):
+    del g_in, g_ref
+    y, core, z, xi = place()
+    even = lax.rem(xi, 2) == 0
+    left, right = mine_ref.at[:, : 2 * B], mine_ref.at[:, 2 * B :]
+    choose(left, even, half_ref, far_ref)
+    choose(right, even, far_ref, half_ref)
+    choose(top_out, lax.rem(y // 2, 2) == 1, down_ref, top_ref)
+
+
+def last_kernel(s_in, top_ref, down_ref, f1_ref, f2_ref, f3_ref, s_ref, top_out):
+    del s_in, s_ref, f1_ref, f2_ref, f3_ref
+    y, core, z, xi = place()
+    choose(top_out, lax.rem(y, 2) == 1, down_ref, top_ref)
+
+
+def pack_kernel(x_ref, out_ref):
+    def put(blocks):
+        for at, (i, j) in enumerate(blocks):
+            j = j % 2
+            for p in range(16):
+                out_ref[p, at] = x_ref[i * B + p * 8 : i * B + p * 8 + 8, j * B : (j + 1) * B]
+
+    @pl.when(lax.axis_index("col") == 0)
+    def _():
+        put(LEFT)
+
+    @pl.when(lax.axis_index("col") > 0)
+    def _():
+        put(RIGHT)
+
+
+def pack(x):
+    return pl.pallas_call(
+        pack_kernel,
+        out_shape=jax.ShapeDtypeStruct((16, 5, 8, B), jnp.float32),
+        in_specs=[whole()],
         out_specs=whole(),
         compiler_params=PARAMS,
-    )(have, got, after)
-
-
-def pack_kernel(piece_ref, swapped_ref, out_ref):
-    col = lax.axis_index("col")
-
-    def put(left_ref, right_ref):
-        for at, (i, j) in enumerate(BLOCKS):
-            side_ref = left_ref if j < 2 else right_ref
-            out_ref[at] = side_ref[i, :, (j % 2) * B : (j % 2 + 1) * B]
-
-    @pl.when(col == 0)
-    def _():
-        put(piece_ref, swapped_ref)
-
-    @pl.when(col == 1)
-    def _():
-        put(swapped_ref, piece_ref)
-
-    @pl.when(col > 1)
-    def _():
-        out_ref[...] = jnp.zeros_like(out_ref)
-
-
-def pack(piece, swapped):
-    return pl.pallas_call(
-        pack_kernel,
-        out_shape=jax.ShapeDtypeStruct((len(BLOCKS), 8, B), jnp.float32),
-        in_specs=[whole()] * 2,
-        out_specs=whole(),
-        compiler_params=PARAMS,
-    )(piece, swapped)
+    )(x)
 
 
 def on_device(x):
+    row = lax.axis_index("row")
     planes = range(0, 32, 8)
 
-    def send(v, pairs):
+    def along(v, pairs):
         return lax.ppermute(v, "col", pairs)
 
-    got = send(x, [(0, 16), (1, 17)])
-
-    split = x.reshape(4, 16, 8, 256).transpose(1, 0, 2, 3)
-    turned = lax.all_to_all(split, "row", 0, 0)
-    piece = turned[0]
-    top = lax.all_gather(turned[:2], "row")
-    half = merge(lambda z, xi: z != 0, x, got, piece)
-    got = send(half, [(0, 8), (1, 9), (16, 24), (17, 25)])
-
-    packed = pack(piece, send(piece, [(0, 1), (1, 0)]))
-    packed += sum(send(packed, [(0, 8 * q), (1, 8 * q + 1)]) for q in range(1, 4))
-    half = merge(lambda z, xi: lax.rem(z, 2) == 1, half, got, packed)
-    got = send(half, [(p + i, p + j) for p in planes for i, j in ((0, 6), (1, 3))])
-    packed += sum(send(packed, [(p + i, p + i + s) for p in planes for i in (0, 1)]) for s in (2, 4, 6))
-    gathered = lax.all_gather(packed, "row")
-
-    half = merge(lambda z, xi: either(xi, (3, 6)), half, got, gathered)
-    got = send(half, [(p + i, p + j) for p in planes for i, j in ((0, 2), (6, 4), (1, 7), (3, 5))])
-    state = first_half(gathered, half)
-    half = merge(lambda z, xi: either(xi, (2, 4, 5, 7)), half, got, state[0])
-    other = send(half, [(i, i ^ 1) for i in range(32)])
-    _, lower, inv = second_half(*state, half)
-    return final(x, half, other, top, lower, inv)
+    def across(v, pairs):
+        return lax.ppermute(v, "row", pairs)
+
+    far = [along(x[q * B : (q + 1) * B], [(0, 8 * q), (1, 8 * q + 1)]) for q in (1, 2, 3)]
+    down = across(x, [(0, 8)])
+
+    cur = pack(x)
+    got = across(cur[8:], [(0, 1)])
+    cur = jnp.where(row % 2 == 1, got, cur[:8])
+    for step in (4, 2, 1):
+        pairs = [(2 * y + k, 2 * (y + step) + k) for y in range(0, 8, 2 * step) for k in (0, 1)]
+        got = across(cur[step:], pairs)
+        cur = jnp.where((row // 2) // step % 2 == 1, got, cur[:step])
+
+    quarter = jax.ShapeDtypeStruct((B, 2 * B), jnp.float32)
+    some = jax.ShapeDtypeStruct((5, 8, B), jnp.float32)
+    full = jax.ShapeDtypeStruct((10, 8, B), jnp.float32)
+    half, piece = local(spread_kernel, (x, *far, cur), (quarter, some))
+    far = along(half, [(p + i, p + i + 4) for p in planes for i in (0, 1)])
+    piece += sum(along(piece, [(0, s), (1, 1 + s)]) for s in (2, 4, 6))
+    swapped = along(piece, [(i, i ^ 1) for i in range(8)])
+    both, half, top = local(
+        pair_kernel, (piece, swapped, half, far, x, down), (full, quarter) + like(x)
+    )
+    far = along(half, [(p + i, p + i + 2) for p in planes for i in (0, 1, 4, 5)])
+    down = across(top, [(0, 4), (8, 12)])
+    parts = [along(both, [(i, 8 * q + i) for i in range(8)]) for q in (1, 2, 3)]
+    both, half = local(sum_kernel, (both, *parts, half, far), (full, quarter))
+    other = along(half, [(i, i ^ 1) for i in range(32)])
+    gathered = lax.all_gather(both, "row")
+
+    wide = jax.ShapeDtypeStruct((B, 4 * B), jnp.float32)
+    gathered, mine, top = local(
+        join_kernel, (gathered, half, other, top, down), like(gathered) + (wide,) + like(top), {0: 0}
+    )
+    far = [along(mine, [(i, (i + 8 * s) % 32) for i in range(32)]) for s in (1, 2, 3)]
+    down = across(top, [(4 * q, 4 * q + 2) for q in range(4)])
+    s, lower, inv = first_half(gathered, mine)
+    s, top = local(last_kernel, (s, top, down, *far), like(s, top), {0: 0})
+    down = across(top, [(2 * q, 2 * q + 1) for q in range(8)])
+    _, lower, inv = second_half(s, lower, inv, top)
+    return final(x, mine, far, top, down, lower, inv)
 
 
 def solution(mesh):

time: 126 us -> 132 us (1.048)
  the two profiles are of different devices: /device:TPU:1 before, /device:TPU:72 now
where the time goes in v3:
time: 132 us; the launch traced here: 131 us
  starting transfers between devices  40.7 us (31%)
  waiting for transfers between devices  37.4 us (28%)
  Pallas kernels  29.1 us (22%)
  blocking collectives  21.8 us (17%)
    ppermute x16, starting transfers between devices, along(): return lax.ppermute(v, 'col', pairs)  33.1 us
    all_gather x1, blocking collectives, on_device(): gathered = lax.all_gather(both, 'row')  21.8 us
    ppermute x8, waiting for transfers between devices, across(): return lax.ppermute(v, 'row', pairs)  21.5 us
    pallas_call x1, Pallas kernels, first_half(): pl.pallas_call(first_kernel, out_shape=(SQUARE,) * 3, in_specs=[whole(),...  16.9 us
    ppermute x16, waiting for transfers between devices, along(): return lax.ppermute(v, 'col', pairs)  15.9 us
    ppermute x8, starting transfers between devices, across(): return lax.ppermute(v, 'row', pairs)  7.58 us
    pallas_call x1, Pallas kernels, final(): pl.pallas_call(final_kernel, out_shape=(jax.ShapeDtypeStruct((16, 512), j...  7.26 us
    pallas_call x1, Pallas kernels, second_half(): pl.pallas_call(second_kernel, out_shape=(SQUARE,) * 3, in_specs=[whole()]...  4.63 us
  transfers between devices with their start and end apart: 24, of which 7 were waited for; matrix products, arithmetic and copies ran while one was open for 0% of the time, Pallas kernels for 16%

profile of v3, /device:TPU:72, one launch (start us, length us, event | category | flops | bytes accessed | tf_op | source)
XLA Modules:
  0.0 131.2 jit_solution(3478632105524175418)
XLA Ops:
  0.6 1.0 copy-done
  1.7 0.7 collective-permute-start.3
  2.5 0.8 collective-permute-start.4
  4.1 0.7 collective-permute-start.12
  4.8 1.3 collective-permute-start.6
  6.2 0.7 collective-permute-start.2
  6.9 0.7 collective-permute-start.1
  7.5 0.7 collective-permute-start
  8.2 21.5 %collective-permute-done.6 = f32[1,5,8,128]{3,2,1,0:T(8,128)S(1)} collective-permute-done((f32[1,5,8,128]{3,2,1,0:T(8,128)S(1)}, f32[1,5,8,128]{3,2,1,0:T(8,128)S(1)}, u32[]{:S(2)}, u32[]{:S(2)}) %collective-permute-start.6) | collective-permute-done | bytes 20512 | tf_op jit(solution)/shard_map/ppermute | solution.py:332
  30.5 1.3 collective-permute-start.8
  32.5 1.3 collective-permute-start.11
  33.8 5.5 %collective-permute-done.8 = f32[5,8,128]{2,1,0:T(8,128)S(1)} collective-permute-done((f32[5,8,128]{2,1,0:T(8,128)S(1)}, f32[5,8,128]{2,1,0:T(8,128)S(1)}, u32[]{:S(2)}, u32[]{:S(2)}) %collective-permute-start.8) | collective-permute-done | bytes 20512 | tf_op jit(solution)/shard_map/ppermute | solution.py:329
  39.3 2.5 %collective-permute-start.10 = (f32[5,8,128]{2,1,0:T(8,128)S(1)}, f32[5,8,128]{2,1,0:T(8,128)S(1)}, u32[]{:S(2)}, u32[]{:S(2)}) collective-permute-start(f32[5,8,128]{2,1,0:T(8,128)S(1)} %add_add_fusion.own_ref), channel_id=1, source_target_pairs={{0,1},{1,0},{2,3},{3,2},{4,5},{5,4},{6,7},{7,6},{32,33},{33,32},{3... | collective-permute-start | bytes 61448 | tf_op jit(solution)/shard_map/ppermute | solution.py:329
  41.8 3.3 %collective-permute-done.10.other_ref = f32[5,8,128]{2,1,0:T(8,128)S(1)} collective-permute-done((f32[5,8,128]{2,1,0:T(8,128)S(1)}, f32[5,8,128]{2,1,0:T(8,128)S(1)}, u32[]{:S(2)}, u32[]{:S(2)}) %collective-permute-start.10) | collective-permute-done | bytes 20512 | tf_op jit(solution)/shard_map/ppermute | solution.py:329
  45.2 0.7 collective-permute-start.18
  45.9 3.7 %collective-permute-start.16 = (f32[128,256]{1,0:T(8,128)S(1)}, f32[128,256]{1,0:T(8,128)S(1)}, u32[]{:S(2)}, u32[]{:S(2)}) collective-permute-start(f32[128,256]{1,0:T(8,128)S(1)} %get-tuple-element.22.half_ref), channel_id=1, source_target_pairs={{0,2},{1,3},{4,6},{5,7},{8,10},{9,11},{12,14},{13,15},{16,18},{17,... | collective-permute-start | bytes 393224 | tf_op jit(solution)/shard_map/ppermute | solution.py:329
  49.6 1.3 collective-permute-start.15
  50.9 1.3 collective-permute-start.14
  52.2 1.3 collective-permute-start.13
  53.9 1.3 collective-permute-done.13.b1_ref
  55.2 3.3 %collective-permute-start.17 = (f32[128,256]{1,0:T(8,128)S(1)}, f32[128,256]{1,0:T(8,128)S(1)}, u32[]{:S(2)}, u32[]{:S(2)}) collective-permute-start(f32[128,256]{1,0:T(8,128)S(1)} %get-tuple-element.24.half_ref), channel_id=1, source_target_pairs={{0,1},{1,0},{2,3},{3,2},{4,5},{5,4},{6,7},{7,6},{8,9},{9,8},{10,11... | collective-permute-start | bytes 393224 | tf_op jit(solution)/shard_map/ppermute | solution.py:329
  58.5 21.8 %all-gather = f32[160,8,128]{2,1,0:T(8,128)S(1)} all-gather(f32[10,8,128]{2,1,0:T(8,128)S(1)} %get-tuple-element.23), channel_id=2, replica_groups=mesh['row'=16,'col'=32] {'row'}, dimensions={0}, use_global_device_ids=true | all-gather | bytes 696320 | tf_op jit(solution)/shard_map/all_gather | solution.py:360
  80.4 1.3 collective-permute-start.22
  81.7 3.8 %collective-permute-start.21 = (f32[128,512]{1,0:T(8,128)S(1)}, f32[128,512]{1,0:T(8,128)S(1)}, u32[]{:S(2)}, u32[]{:S(2)}) collective-permute-start(f32[128,512]{1,0:T(8,128)S(1)} %get-tuple-element.26.after_ref.mine_ref), channel_id=1, source_target_pairs={{0,24},{1,25},{2,26},{3,27},{4,28},{5,29},{6,30},{7,31},{8,0},{9,1... | collective-permute-start | bytes 786440 | tf_op jit(solution)/shard_map/ppermute | solution.py:329
  85.4 6.9 %collective-permute-start.20 = (f32[128,512]{1,0:T(8,128)S(1)}, f32[128,512]{1,0:T(8,128)S(1)}, u32[]{:S(2)}, u32[]{:S(2)}) collective-permute-start(f32[128,512]{1,0:T(8,128)S(1)} %get-tuple-element.26.after_ref.mine_ref), channel_id=1, source_target_pairs={{0,16},{1,17},{2,18},{3,19},{4,20},{5,21},{6,22},{7,23},{8,24},{9,... | collective-permute-start | bytes 786440 | tf_op jit(solution)/shard_map/ppermute | solution.py:329
  92.3 3.2 %collective-permute-start.19 = (f32[128,512]{1,0:T(8,128)S(1)}, f32[128,512]{1,0:T(8,128)S(1)}, u32[]{:S(2)}, u32[]{:S(2)}) collective-permute-start(f32[128,512]{1,0:T(8,128)S(1)} %get-tuple-element.26.after_ref.mine_ref), channel_id=1, source_target_pairs={{0,8},{1,9},{2,10},{3,11},{4,12},{5,13},{6,14},{7,15},{8,16},{9,17... | collective-permute-start | bytes 786440 | tf_op jit(solution)/shard_map/ppermute | solution.py:329
  95.5 16.9 %shard_map.35 = (f32[512,512]{1,0:T(8,128)S(1)}, f32[512,512]{1,0:T(8,128)S(1)}, f32[512,512]{1,0:T(8,128)S(1)}) custom-call(f32[16,10,8,128]{3,2,1,0:T(8,128)S(1)} %get-tuple-element.27.g_ref, f32[128,512]{1,0:T(8,128)S(1)} %get-tuple-element.26.after_ref.mine_ref), custom_call_target="tpu_custom_call" | custom-call | tf_op jit(solution)/shard_map/pallas_call | solution.py:128
  112.4 0.7 collective-permute-done.20.f2_ref
  113.1 4.7 %collective-permute-done.19.f1_ref = f32[128,512]{1,0:T(8,128)S(1)} collective-permute-done((f32[128,512]{1,0:T(8,128)S(1)}, f32[128,512]{1,0:T(8,128)S(1)}, u32[]{:S(2)}, u32[]{:S(2)}) %collective-permute-start.19) | collective-permute-done | bytes 262176 | tf_op jit(solution)/shard_map/ppermute | solution.py:329
  117.9 1.5 %collective-permute-start.23 = (f32[512,256]{1,0:T(8,128)S(1)}, f32[512,256]{1,0:T(8,128)S(1)}, u32[]{:S(2)}, u32[]{:S(2)}) collective-permute-start(f32[512,256]{1,0:T(8,128)S(1)} %get-tuple-element.30.after_ref.top_ref), channel_id=1, source_target_pairs={{0,32},{64,96},{128,160},{192,224},{256,288},{320,352},{384,416},{... | collective-permute-start | bytes 1572872 | tf_op jit(solution)/shard_map/ppermute | solution.py:332
  119.3 4.6 %shard_map.37 = (f32[512,512]{1,0:T(8,128)S(1)}, f32[512,512]{1,0:T(8,128)S(1)}, f32[512,512]{1,0:T(8,128)S(1)}) custom-call(f32[512,512]{1,0:T(8,128)S(1)} %get-tuple-element.31.s_in, f32[512,512]{1,0:T(8,128)S(1)} %get-tuple-element.32.l_in, f32[512,512]{1,0:T(8,128)S(1)} %get-tuple-element.33.inv_in, ...), custom_call_target="tpu_custom_call", output_to_operand_aliasing={{0}: (0, {}), {1}: (1, {}), {2}: (2, {})} | custom-call | tf_op jit(solution)/shard_map/pallas_call | solution.py:139
  124.0 7.3 %shard_map.38 = (f32[16,512]{1,0:T(8,128)}, f32[512,256]{1,0:T(8,128)}) custom-call(f32[512,256]{1,0:T(8,128)S(1)} %copy-done.1, f32[128,512]{1,0:T(8,128)S(1)} %get-tuple-element.26.after_ref.mine_ref, f32[128,512]{1,0:T(8,128)S(1)} %collective-permute-done.19.f1_ref, f32[128,512]{1,0:T(8,128)S(1)} %collective-permute-done.20.f2_ref, ...), custom_call_target="tpu_custom_call" | custom-call | tf_op jit(solution)/shard_map/pallas_call | solution.py:185
  (40 shorter events, 2.8 us)
Async XLA Ops:
  0.6 1.0 copy-start
  1.7 0.7 collective-permute-start.3
  2.4 1.6 %copy-start.1 = (f32[512,256]{1,0:T(8,128)S(1)}, f32[512,256]{1,0:T(8,128)}, u32[]{:S(2)}) copy-start(f32[512,256]{1,0:T(8,128)} %x_ref.7) | copy-start | bytes 1572868
  2.5 0.9 collective-permute-start.4
  3.4 1.4 %collective-permute-start.5 = (f32[2,5,8,128]{3,2,1,0:T(8,128)S(1)}, f32[2,5,8,128]{3,2,1,0:T(8,128)S(1)}, u32[]{:S(2)}, u32[]{:S(2)}) collective-permute-start(f32[2,5,8,128]{3,2,1,0:T(8,128)S(1)} %slice.48), channel_id=1, source_target_pairs={{0,128},{32,160},{256,384},{288,416},{1,129},{33,161},{257,385},{2... | collective-permute-start | bytes 122888 | tf_op jit(solution)/shard_map/ppermute | solution.py:332
  4.1 41.0 %collective-permute-start.12 = (f32[512,256]{1,0:T(8,128)S(1)}, f32[512,256]{1,0:T(8,128)S(1)}, u32[]{:S(2)}, u32[]{:S(2)}) collective-permute-start(f32[512,256]{1,0:T(8,128)S(1)} %copy-done.1), channel_id=1, source_target_pairs={{0,256},{1,257},{2,258},{3,259},{4,260},{5,261},{6,262},{7,263},{8... | collective-permute-start | bytes 1572872 | tf_op jit(solution)/shard_map/ppermute | solution.py:332
  4.8 24.9 %collective-permute-start.6 = (f32[1,5,8,128]{3,2,1,0:T(8,128)S(1)}, f32[1,5,8,128]{3,2,1,0:T(8,128)S(1)}, u32[]{:S(2)}, u32[]{:S(2)}) collective-permute-start(f32[1,5,8,128]{3,2,1,0:T(8,128)S(1)} %slice.50), channel_id=1, source_target_pairs={{0,64},{32,96},{128,192},{160,224},{256,320},{288,352},{384,448},{... | collective-permute-start | bytes 61448 | tf_op jit(solution)/shard_map/ppermute | solution.py:332
  6.2 23.6 %collective-permute-start.2 = (f32[128,256]{1,0:T(8,128)S(1)}, f32[128,256]{1,0:T(8,128)S(1)}, u32[]{:S(2)}, u32[]{:S(2)}) collective-permute-start(f32[128,256]{1,0:T(8,128)S(1)} %get-tuple-element.36), channel_id=1, source_target_pairs={{0,24},{1,25},{32,56},{33,57},{64,88},{65,89},{96,120},{97,121},{1... | collective-permute-start | bytes 393224 | tf_op jit(solution)/shard_map/ppermute | solution.py:329
  6.9 22.9 %collective-permute-start.1 = (f32[128,256]{1,0:T(8,128)S(1)}, f32[128,256]{1,0:T(8,128)S(1)}, u32[]{:S(2)}, u32[]{:S(2)}) collective-permute-start(f32[128,256]{1,0:T(8,128)S(1)} %get-tuple-element.37), channel_id=1, source_target_pairs={{0,16},{1,17},{32,48},{33,49},{64,80},{65,81},{96,112},{97,113},{1... | collective-permute-start | bytes 393224 | tf_op jit(solution)/shard_map/ppermute | solution.py:329
  7.5 22.2 %collective-permute-start = (f32[128,256]{1,0:T(8,128)S(1)}, f32[128,256]{1,0:T(8,128)S(1)}, u32[]{:S(2)}, u32[]{:S(2)}) collective-permute-start(f32[128,256]{1,0:T(8,128)S(1)} %get-tuple-element.38), channel_id=1, source_target_pairs={{0,8},{1,9},{32,40},{33,41},{64,72},{65,73},{96,104},{97,105},{128... | collective-permute-start | bytes 393224 | tf_op jit(solution)/shard_map/ppermute | solution.py:329
  29.8 3.9 %collective-permute-start.9 = (f32[5,8,128]{2,1,0:T(8,128)S(1)}, f32[5,8,128]{2,1,0:T(8,128)S(1)}, u32[]{:S(2)}, u32[]{:S(2)}) collective-permute-start(f32[5,8,128]{2,1,0:T(8,128)S(1)} %get-tuple-element.19), channel_id=1, source_target_pairs={{0,6},{1,7},{32,38},{33,39},{64,70},{65,71},{96,102},{97,103},{128... | collective-permute-start | bytes 61448 | tf_op jit(solution)/shard_map/ppermute | solution.py:329
  30.5 8.8 %collective-permute-start.8 = (f32[5,8,128]{2,1,0:T(8,128)S(1)}, f32[5,8,128]{2,1,0:T(8,128)S(1)}, u32[]{:S(2)}, u32[]{:S(2)}) collective-permute-start(f32[5,8,128]{2,1,0:T(8,128)S(1)} %get-tuple-element.19), channel_id=1, source_target_pairs={{0,4},{1,5},{32,36},{33,37},{64,68},{65,69},{96,100},{97,101},{128... | collective-permute-start | bytes 61448 | tf_op jit(solution)/shard_map/ppermute | solution.py:329
  31.8 7.5 %collective-permute-start.7 = (f32[5,8,128]{2,1,0:T(8,128)S(1)}, f32[5,8,128]{2,1,0:T(8,128)S(1)}, u32[]{:S(2)}, u32[]{:S(2)}) collective-permute-start(f32[5,8,128]{2,1,0:T(8,128)S(1)} %get-tuple-element.19), channel_id=1, source_target_pairs={{0,2},{1,3},{32,34},{33,35},{64,66},{65,67},{96,98},{97,99},{128,1... | collective-permute-start | bytes 61448 | tf_op jit(solution)/shard_map/ppermute | solution.py:329
  32.5 12.6 %collective-permute-start.11 = (f32[128,256]{1,0:T(8,128)S(1)}, f32[128,256]{1,0:T(8,128)S(1)}, u32[]{:S(2)}, u32[]{:S(2)}) collective-permute-start(f32[128,256]{1,0:T(8,128)S(1)} %get-tuple-element.20.half_ref), channel_id=1, source_target_pairs={{0,4},{1,5},{8,12},{9,13},{16,20},{17,21},{24,28},{25,29},{32,36},... | collective-permute-start | bytes 393224 | tf_op jit(solution)/shard_map/ppermute | solution.py:329
  39.3 5.8 %collective-permute-start.10 = (f32[5,8,128]{2,1,0:T(8,128)S(1)}, f32[5,8,128]{2,1,0:T(8,128)S(1)}, u32[]{:S(2)}, u32[]{:S(2)}) collective-permute-start(f32[5,8,128]{2,1,0:T(8,128)S(1)} %add_add_fusion.own_ref), channel_id=1, source_target_pairs={{0,1},{1,0},{2,3},{3,2},{4,5},{5,4},{6,7},{7,6},{32,33},{33,32},{3... | collective-permute-start | bytes 61448 | tf_op jit(solution)/shard_map/ppermute | solution.py:329
  45.2 35.1 %collective-permute-start.18 = (f32[512,256]{1,0:T(8,128)S(1)}, f32[512,256]{1,0:T(8,128)S(1)}, u32[]{:S(2)}, u32[]{:S(2)}) collective-permute-start(f32[512,256]{1,0:T(8,128)S(1)} %get-tuple-element.25.top_ref), channel_id=1, source_target_pairs={{0,128},{256,384},{1,129},{257,385},{2,130},{258,386},{3,131},{259... | collective-permute-start | bytes 1572872 | tf_op jit(solution)/shard_map/ppermute | solution.py:332
  45.9 9.3 %collective-permute-start.16 = (f32[128,256]{1,0:T(8,128)S(1)}, f32[128,256]{1,0:T(8,128)S(1)}, u32[]{:S(2)}, u32[]{:S(2)}) collective-permute-start(f32[128,256]{1,0:T(8,128)S(1)} %get-tuple-element.22.half_ref), channel_id=1, source_target_pairs={{0,2},{1,3},{4,6},{5,7},{8,10},{9,11},{12,14},{13,15},{16,18},{17,... | collective-permute-start | bytes 393224 | tf_op jit(solution)/shard_map/ppermute | solution.py:329
  49.6 3.9 %collective-permute-start.15 = (f32[10,8,128]{2,1,0:T(8,128)S(1)}, f32[10,8,128]{2,1,0:T(8,128)S(1)}, u32[]{:S(2)}, u32[]{:S(2)}) collective-permute-start(f32[10,8,128]{2,1,0:T(8,128)S(1)} %get-tuple-element.21.b0_ref), channel_id=1, source_target_pairs={{0,24},{1,25},{2,26},{3,27},{4,28},{5,29},{6,30},{7,31},{32,56},{3... | collective-permute-start | bytes 122888 | tf_op jit(solution)/shard_map/ppermute | solution.py:329
  50.9 3.0 %collective-permute-start.14 = (f32[10,8,128]{2,1,0:T(8,128)S(1)}, f32[10,8,128]{2,1,0:T(8,128)S(1)}, u32[]{:S(2)}, u32[]{:S(2)}) collective-permute-start(f32[10,8,128]{2,1,0:T(8,128)S(1)} %get-tuple-element.21.b0_ref), channel_id=1, source_target_pairs={{0,16},{1,17},{2,18},{3,19},{4,20},{5,21},{6,22},{7,23},{32,48},{3... | collective-permute-start | bytes 122888 | tf_op jit(solution)/shard_map/ppermute | solution.py:329
  52.2 3.0 %collective-permute-start.13 = (f32[10,8,128]{2,1,0:T(8,128)S(1)}, f32[10,8,128]{2,1,0:T(8,128)S(1)}, u32[]{:S(2)}, u32[]{:S(2)}) collective-permute-start(f32[10,8,128]{2,1,0:T(8,128)S(1)} %get-tuple-element.21.b0_ref), channel_id=1, source_target_pairs={{0,8},{1,9},{2,10},{3,11},{4,12},{5,13},{6,14},{7,15},{32,40},{33,... | collective-permute-start | bytes 122888 | tf_op jit(solution)/shard_map/ppermute | solution.py:329
  55.2 25.1 %collective-permute-start.17 = (f32[128,256]{1,0:T(8,128)S(1)}, f32[128,256]{1,0:T(8,128)S(1)}, u32[]{:S(2)}, u32[]{:S(2)}) collective-permute-start(f32[128,256]{1,0:T(8,128)S(1)} %get-tuple-element.24.half_ref), channel_id=1, source_target_pairs={{0,1},{1,0},{2,3},{3,2},{4,5},{5,4},{6,7},{7,6},{8,9},{9,8},{10,11... | collective-permute-start | bytes 393224 | tf_op jit(solution)/shard_map/ppermute | solution.py:329
  80.4 37.4 %collective-permute-start.22 = (f32[512,256]{1,0:T(8,128)S(1)}, f32[512,256]{1,0:T(8,128)S(1)}, u32[]{:S(2)}, u32[]{:S(2)}) collective-permute-start(f32[512,256]{1,0:T(8,128)S(1)} %get-tuple-element.29.top_ref), channel_id=1, source_target_pairs={{0,64},{128,192},{256,320},{384,448},{1,65},{129,193},{257,321},{3... | collective-permute-start | bytes 1572872 | tf_op jit(solution)/shard_map/ppermute | solution.py:332
  81.7 30.7 %collective-permute-start.21 = (f32[128,512]{1,0:T(8,128)S(1)}, f32[128,512]{1,0:T(8,128)S(1)}, u32[]{:S(2)}, u32[]{:S(2)}) collective-permute-start(f32[128,512]{1,0:T(8,128)S(1)} %get-tuple-element.26.after_ref.mine_ref), channel_id=1, source_target_pairs={{0,24},{1,25},{2,26},{3,27},{4,28},{5,29},{6,30},{7,31},{8,0},{9,1... | collective-permute-start | bytes 786440 | tf_op jit(solution)/shard_map/ppermute | solution.py:329
  85.4 27.7 %collective-permute-start.20 = (f32[128,512]{1,0:T(8,128)S(1)}, f32[128,512]{1,0:T(8,128)S(1)}, u32[]{:S(2)}, u32[]{:S(2)}) collective-permute-start(f32[128,512]{1,0:T(8,128)S(1)} %get-tuple-element.26.after_ref.mine_ref), channel_id=1, source_target_pairs={{0,16},{1,17},{2,18},{3,19},{4,20},{5,21},{6,22},{7,23},{8,24},{9,... | collective-permute-start | bytes 786440 | tf_op jit(solution)/shard_map/ppermute | solution.py:329
  92.3 25.5 %collective-permute-start.19 = (f32[128,512]{1,0:T(8,128)S(1)}, f32[128,512]{1,0:T(8,128)S(1)}, u32[]{:S(2)}, u32[]{:S(2)}) collective-permute-start(f32[128,512]{1,0:T(8,128)S(1)} %get-tuple-element.26.after_ref.mine_ref), channel_id=1, source_target_pairs={{0,8},{1,9},{2,10},{3,11},{4,12},{5,13},{6,14},{7,15},{8,16},{9,17... | collective-permute-start | bytes 786440 | tf_op jit(solution)/shard_map/ppermute | solution.py:329
  117.9 6.1 %collective-permute-start.23 = (f32[512,256]{1,0:T(8,128)S(1)}, f32[512,256]{1,0:T(8,128)S(1)}, u32[]{:S(2)}, u32[]{:S(2)}) collective-permute-start(f32[512,256]{1,0:T(8,128)S(1)} %get-tuple-element.30.after_ref.top_ref), channel_id=1, source_target_pairs={{0,32},{64,96},{128,160},{192,224},{256,288},{320,352},{384,416},{... | collective-permute-start | bytes 1572872 | tf_op jit(solution)/shard_map/ppermute | solution.py:332

commit v4 on v3

v4 whole, which is shorter than its diff:
```python
import functools

import jax, jax.numpy as jnp
from jax import lax
from jax.experimental import pallas as pl
from jax.experimental.pallas import tpu as pltpu
from jax.sharding import PartitionSpec as P

HI = lax.Precision.HIGHEST
B = 128
S8 = 8

def rep(x):
    return jnp.broadcast_to(x, (S8, B))

def factor_tile(d_ref, m_ref, lt_ref):
    tiles = B // S8
    for b in range(tiles):
        rows = pl.ds(b * S8, S8)
        d = d_ref[rows, :]
        m = m_ref[rows, :]
        cols = [rep(d[:, b * S8 + k : b * S8 + k + 1]) for k in range(S8)]
        s = {}
        for i in range(S8):
            for k in range(i, S8):
                s[i, k] = rep(cols[k][i : i + 1, :])
        rd = [rep(d[j : j + 1, :]) for j in range(S8)]
        rm = [rep(m[j : j + 1, :]) for j in range(S8)]
        u, qd, qm, scale = {}, [], [], []
        for j in range(S8):
            inv = 1.0 / s[j, j]
            scale.append(lax.rsqrt(s[j, j]))
            for k in range(j + 1, S8):
                u[j, k] = s[j, k] * inv
            for i in range(j + 1, S8):
                for k in range(i, S8):
                    s[i, k] = s[i, k] - s[j, i] * u[j, k]
            qd.append(rd[j] * inv)
            qm.append(rm[j] * inv)
            for k in range(j + 1, S8):
                rd[k] = rd[k] - s[j, k] * qd[j]
                rm[k] = rm[k] - s[j, k] * qm[j]
        for t in range(b + 1, tiles):
            at = pl.ds(t * S8, S8)
            dt = d_ref[at, :]
            mt = m_ref[at, :]
            c = [rep(dt[:, b * S8 + k : b * S8 + k + 1]) for k in range(S8)]
            for j in range(S8):
                for k in range(j + 1, S8):
                    c[k] = c[k] - c[j] * u[j, k]
            for j in range(S8):
                dt = dt - c[j] * qd[j]
                mt = mt - c[j] * qm[j]
            d_ref[at, :] = dt
            m_ref[at, :] = mt
        sub = lax.broadcasted_iota(jnp.int32, (S8, B), 0)
        od, om = rd[0] * scale[0], rm[0] * scale[0]
        for j in range(1, S8):
            od = jnp.where(sub == j, rd[j] * scale[j], od)
            om = jnp.where(sub == j, rm[j] * scale[j], om)
        lt_ref[rows, :] = od
        m_ref[rows, :] = om

def dot(a, b, dims=((1,), (0,))):
    return lax.dot_general(a, b, (dims, ((), ())), precision=HI, preferred_element_type=jnp.float32)

N = 4 * B
LEFT = ((0, 0), (1, 0), (1, 1), (2, 0), (3, 0))
RIGHT = ((2, 2), (3, 2), (3, 3), (1, 2), (1, 3))


def eliminate(first, last, l_ref, inv_ref, s_ref, d_ref, m_ref, lt_ref):
    r128 = lax.broadcasted_iota(jnp.int32, (B, B), 0)
    c128 = lax.broadcasted_iota(jnp.int32, (B, B), 1)
    eye = jnp.where(r128 == c128, 1.0, 0.0).astype(jnp.float32)
    for k in range(first, last):
        lo, hi = k * B, (k + 1) * B
        d_ref[...] = s_ref[lo:hi, lo:hi]
        m_ref[...] = eye
        factor_tile(d_ref, m_ref, lt_ref)
        inv = m_ref[...]
        l_ref[lo:hi, lo:hi] = jnp.where(r128 >= c128, lt_ref[...].T, 0.0)
        inv_ref[lo:hi, lo:hi] = inv
        if k:
            inv_ref[lo:hi, :lo] = dot(inv, inv_ref[lo:hi, :lo])
        if hi < N:
            below = dot(s_ref[hi:, lo:hi], inv, ((1,), (1,)))
            l_ref[hi:, lo:hi] = below
            for i in range(k + 1, N // B):
                a, z = i * B, (i + 1) * B
                mine = below[a - hi : z - hi]
                s_ref[a:z, hi:z] -= dot(mine, below[: z - hi], ((1,), (1,)))
                inv_ref[a:z, :hi] -= dot(mine, inv_ref[lo:hi, :hi])


def first_kernel(g_ref, after_ref, s_ref, l_ref, inv_ref, d_ref, m_ref, lt_ref):
    del after_ref
    s_ref[...] = jnp.zeros((N, N), jnp.float32)
    for at, (i, j) in enumerate(LEFT + RIGHT):
        for r in range(16):
            p = (r % 2) * 8 + r // 2
            s_ref[i * B + p * 8 : i * B + p * 8 + 8, j * B : (j + 1) * B] = g_ref[r, at]
    for i, j in RIGHT[3:]:
        s_ref[j * B : (j + 1) * B, i * B : (i + 1) * B] = s_ref[i * B : (i + 1) * B, j * B : (j + 1) * B].T
    inv_ref[...] = jnp.zeros((N, N), jnp.float32)
    l_ref[...] = jnp.zeros((N, N), jnp.float32)
    eliminate(0, 2, l_ref, inv_ref, s_ref, d_ref, m_ref, lt_ref)


def second_kernel(s_in, l_in, inv_in, after_ref, s_ref, l_ref, inv_ref, d_ref, m_ref, lt_ref):
    del s_in, l_in, inv_in, after_ref
    eliminate(2, 4, l_ref, inv_ref, s_ref, d_ref, m_ref, lt_ref)


def whole():
    return pl.BlockSpec(memory_space=pltpu.VMEM)


def anywhere():
    return pl.BlockSpec(memory_space=pl.ANY)


PARAMS = pltpu.CompilerParams(vmem_limit_bytes=40 * 2**20)
SQUARE = jax.ShapeDtypeStruct((N, N), jnp.float32)


def first_half(gathered, after):
    return pl.pallas_call(
        first_kernel,
        out_shape=(SQUARE,) * 3,
        in_specs=[whole(), anywhere()],
        out_specs=(whole(),) * 3,
        scratch_shapes=[pltpu.VMEM((B, B), jnp.float32)] * 3,
        compiler_params=PARAMS,
    )(gathered, after)


def second_half(s, lower, inv, after):
    return pl.pallas_call(
        second_kernel,
        out_shape=(SQUARE,) * 3,
        in_specs=[whole()] * 3 + [anywhere()],
        out_specs=(whole(),) * 3,
        input_output_aliases={0: 0, 1: 1, 2: 2},
        scratch_shapes=[pltpu.VMEM((B, B), jnp.float32)] * 3,
        compiler_params=PARAMS,
    )(s, lower, inv, after)


def final_kernel(x_ref, q0_ref, q1_ref, q2_ref, q3_ref, top_ref, far_ref, l_ref, inv_ref, panel_ref, out_ref, u_ref, f_ref):
    row, col = lax.axis_index("row"), lax.axis_index("col")
    inv = inv_ref[...]
    half = 2 * B

    def solve_top(ref):
        u_ref[:half] = dot(inv[:half, :half], ref[:half])
        u_ref[half:] = dot(inv[half:], ref[...])

    @pl.when(lax.rem(row, 2) == 0)
    def _():
        solve_top(top_ref)

    @pl.when(lax.rem(row, 2) == 1)
    def _():
        solve_top(far_ref)

    @pl.when(row == 0)
    def _():
        f_ref[...] = l_ref[...]

    for x in range(4):

        @pl.when(jnp.logical_and(row > 0, lax.rem(col, 4) == x))
        def _(x=x):
            held = {x: q0_ref, (x + 3) % 4: q1_ref, (x + 1) % 4: q2_ref, (x + 2) % 4: q3_ref}
            for lo, left, right in ((0, held[0], held[1]), (half, held[3], held[2])):
                f_ref[lo : lo + half, :half] = dot(left[...], inv[:half, :half], ((1,), (1,)))
                f_ref[lo : lo + half, half:] = dot(left[...], inv[half:, :half], ((1,), (1,))) + dot(
                    right[...], inv[half:, half:], ((1,), (1,))
                )

    panel_ref[...] = f_ref[pl.ds(pl.multiple_of(col * 16, 16), 16), :]
    live = jnp.logical_and(row > 0, col > 1)

    @pl.when(live)
    def _():
        out_ref[...] = x_ref[...] - lax.dot_general(
            f_ref[...],
            u_ref[...],
            (((1,), (0,)), ((), ())),
            precision=lax.Precision.HIGH,
            preferred_element_type=jnp.float32,
        )

    @pl.when(jnp.logical_not(live))
    def _():
        out_ref[...] = jnp.zeros_like(out_ref)


def final(*values):
    return pl.pallas_call(
        final_kernel,
        out_shape=(
            jax.ShapeDtypeStruct((16, 512), jnp.float32),
            jax.ShapeDtypeStruct((512, 256), jnp.float32),
        ),
        in_specs=[whole()] * 9,
        out_specs=(whole(), whole()),
        scratch_shapes=[pltpu.VMEM((512, 256), jnp.float32), pltpu.VMEM((512, 512), jnp.float32)],
        compiler_params=PARAMS,
    )(*values)


def place():
    row, col = lax.axis_index("row"), lax.axis_index("col")
    return row // 2, lax.rem(row, 2), col // 4, lax.rem(col, 4)


def choose(out_ref, take, yes_ref, no_ref):
    @pl.when(take)
    def _():
        out_ref[...] = yes_ref[...]

    @pl.when(jnp.logical_not(take))
    def _():
        out_ref[...] = no_ref[...]


def f32(*shape):
    return jax.ShapeDtypeStruct(shape, jnp.float32)


def local(kernel, values, outs, aliases={}):
    return pl.pallas_call(
        kernel,
        out_shape=outs,
        in_specs=[whole()] * len(values),
        out_specs=(whole(),) * len(outs),
        input_output_aliases=aliases,
        compiler_params=PARAMS,
    )(*values)


def pack_kernel(x_ref, low_ref, high_ref):
    def put(blocks):
        for at, (i, j) in enumerate(blocks):
            j = j % 2
            for p in range(16):
                part = low_ref if p < 8 else high_ref
                part[p % 8, at] = x_ref[i * B + p * 8 : i * B + p * 8 + 8, j * B : (j + 1) * B]

    @pl.when(lax.axis_index("col") == 0)
    def _():
        put(LEFT)

    @pl.when(lax.axis_index("col") > 0)
    def _():
        put(RIGHT)


def halve(take, got_ref, have_ref, low_ref, high_ref):
    n = low_ref.shape[0]
    choose(low_ref, take, got_ref.at[:n], have_ref.at[:n])
    choose(high_ref, take, got_ref.at[n:], have_ref.at[n:])


def core_kernel(have_ref, got_ref, low_ref, high_ref):
    halve(place()[1] == 1, got_ref, have_ref, low_ref, high_ref)


def y4_kernel(have_ref, got_ref, x_ref, far_ref, low_ref, high_ref, quarter_ref):
    y, core, z, xi = place()
    halve(y >= 4, got_ref, have_ref, low_ref, high_ref)
    choose(quarter_ref, xi >= 2, far_ref, x_ref.at[: 2 * B])


def y2_kernel(have_ref, got_ref, low_ref, high_ref):
    halve(lax.rem(place()[0] // 2, 2) == 1, got_ref, have_ref, low_ref, high_ref)


def y1_kernel(have_ref, got_ref, x_ref, quarter_ref, far_ref, piece_ref, top_ref, quarter_out):
    y, core, z, xi = place()
    choose(quarter_out, z >= 4, far_ref, quarter_ref)
    top_ref[...] = x_ref[...]
    holds = jnp.logical_and(z == 0, xi < 2)

    @pl.when(holds)
    def _():
        choose(piece_ref, lax.rem(y, 2) == 1, got_ref.at[0], have_ref.at[0])

    @pl.when(jnp.logical_not(holds))
    def _():
        piece_ref[...] = jnp.zeros_like(piece_ref)


def z_kernel(quarter_in, have_ref, got_ref, top_ref, down_ref, quarter_ref, piece_ref, top_out):
    del quarter_in, quarter_ref
    y, core, z, xi = place()
    choose(piece_ref, lax.rem(z, 2) == 1, got_ref, have_ref)
    choose(top_out, y >= 4, down_ref, top_ref)


def x_kernel(own_ref, o1_ref, o2_ref, o3_ref, quarter_ref, far_ref, top_ref, down_ref, both_ref, quarter_out, top_out):
    y, core, z, xi = place()
    sides = ((own_ref, o1_ref), (o1_ref, own_ref), (o2_ref, o3_ref), (o3_ref, o2_ref))
    for x, (left, right) in enumerate(sides):

        @pl.when(xi == x)
        def _(left=left, right=right):
            both_ref[:5] = left[...]
            both_ref[5:] = right[...]

    choose(quarter_out, lax.rem(z // 2, 2) == 1, far_ref, quarter_ref)
    choose(top_out, lax.rem(y // 2, 2) == 1, down_ref, top_ref)


def gate_kernel(g_in, top_in, quarter_ref, far_ref, g_ref, top_ref, quarter_out):
    del g_in, top_in, g_ref, top_ref
    choose(quarter_out, lax.rem(place()[2], 2) == 1, far_ref, quarter_ref)


def mid_kernel(s_in, q1_in, q2_in, top_ref, down_ref, s_ref, q1_ref, q2_ref, top_out):
    del s_in, q1_in, q2_in, s_ref, q1_ref, q2_ref
    choose(top_out, lax.rem(place()[0], 2) == 1, down_ref, top_ref)


def on_device(x):
    zs, xs, ys = range(8), range(4), range(8)

    def along(v, pairs):
        return lax.ppermute(v, "col", pairs)

    def across(v, pairs):
        return lax.ppermute(v, "row", pairs)

    def by_z(v, step):
        holders = range(0, 8, 2 * step)
        return along(v, [(4 * z + i, 4 * (z + step) + i) for z in holders for i in xs])

    def by_x(v, step):
        return along(v, [(4 * z + i, 4 * z + (i + step) % 4) for z in zs for i in xs])

    far = along(x[2 * B :], [(0, 3), (1, 2)])
    low, high = local(pack_kernel, (x,), (f32(8, 5, 8, B),) * 2)
    got = across(high, [(0, 1)])
    low, high = local(core_kernel, (low, got), (f32(4, 5, 8, B),) * 2)
    got = across(high, [(0, 8), (1, 9)])
    quarter = f32(2 * B, 2 * B)
    low, high, part = local(y4_kernel, (low, got, x, far), (f32(2, 5, 8, B),) * 2 + (quarter,))
    far = by_z(part, 4)
    got = across(high, [(0, 4), (1, 5), (8, 12), (9, 13)])
    low, high = local(y2_kernel, (low, got), (f32(1, 5, 8, B),) * 2)
    got = across(high, [(4 * q + k, 4 * q + k + 2) for q in range(4) for k in (0, 1)])
    piece, top, part = local(y1_kernel, (low, got, x, part, far), (f32(5, 8, B), f32(*x.shape), quarter))

    down = across(top, [(0, 8)])
    piece += sum(along(piece, [(0, 4 * z), (1, 4 * z + 1)]) for z in (4, 2, 6))
    got = along(piece, [(4 * z + i, 4 * z + 4 + i) for z in (0, 2, 4, 6) for i in (0, 1)])
    part, piece, top = local(
        z_kernel, (part, piece, got, top, down), (quarter, f32(5, 8, B), f32(*x.shape)), {0: 0}
    )
    others = [
        along(piece, [(4 * z + i, 4 * z + j) for z in zs for i, j in pairs])
        for pairs in (((0, 1), (1, 0)), ((0, 2), (1, 3)), ((0, 3), (1, 2)))
    ]
    far = by_z(part, 2)
    down = across(top, [(0, 4), (8, 12)])
    both, part, top = local(
        x_kernel, (piece, *others, part, far, top, down), (f32(10, 8, B), quarter, f32(*x.shape))
    )
    far = by_z(part, 1)
    gathered = lax.all_gather(both, "row")
    gathered, top, part = local(
        gate_kernel, (gathered, top, part, far), (f32(16, 10, 8, B), f32(*x.shape), quarter), {0: 0, 1: 1}
    )
    down = across(top, [(4 * q, 4 * q + 2) for q in range(4)])
    near, next_ = by_x(part, 1), by_x(part, 3)
    s, lower, inv = first_half(gathered, part)
    s, near, next_, top = local(
        mid_kernel, (s, near, next_, top, down), (SQUARE, quarter, quarter, f32(*x.shape)), {0: 0, 1: 1, 2: 2}
    )
    down = across(top, [(2 * y, 2 * y + 1) for y in ys])
    opposite = by_x(near, 1)
    _, lower, inv = second_half(s, lower, inv, top)
    return final(x, part, near, next_, opposite, top, down, lower, inv)


def solution(mesh):
    return jax.shard_map(
        on_device,
        mesh=mesh,
        in_specs=(P("row", "col"),),
        out_specs=(P(("row", "col"), None), P("row", "col")),
        check_vma=False,
    )
```

time: 132 us -> 121 us (0.917)
  the two profiles are of different devices: /device:TPU:72 before, /device:TPU:1 now
where the time goes in v4:
time: 121 us; the launch traced here: 120 us
  starting transfers between devices  53.2 us (44%)
  blocking collectives  29.6 us (24%)
  Pallas kernels  25.1 us (21%)
  waiting for transfers between devices  9.92 us (8%)
    ppermute x14, starting transfers between devices, along(): return lax.ppermute(v, 'col', pairs)  42.7 us
    all_gather x1, blocking collectives, on_device(): gathered = lax.all_gather(both, 'row')  29.6 us
    pallas_call x1, Pallas kernels, first_half(): pl.pallas_call(first_kernel, out_shape=(SQUARE,) * 3, in_specs=[whole(),...  11.4 us
    ppermute x8, starting transfers between devices, across(): return lax.ppermute(v, 'row', pairs)  10.5 us
    pallas_call x1, Pallas kernels, second_half(): pl.pallas_call(second_kernel, out_shape=(SQUARE,) * 3, in_specs=[whole()]...  9.95 us
    ppermute x8, waiting for transfers between devices, across(): return lax.ppermute(v, 'row', pairs)  7.27 us
    pallas_call x1, Pallas kernels, final(): pl.pallas_call(final_kernel, out_shape=(jax.ShapeDtypeStruct((16, 512), j...  3.42 us
    ppermute x14, waiting for transfers between devices, along(): return lax.ppermute(v, 'col', pairs)  2.66 us
  transfers between devices with their start and end apart: 22, of which 7 were waited for; matrix products, arithmetic and copies ran while one was open for 0% of the time, Pallas kernels for 18%

profile of v4, /device:TPU:1, one launch (start us, length us, event | category | flops | bytes accessed | tf_op | source)
XLA Modules:
  0.0 119.8 jit_solution(6134121296552854169)
XLA Ops:
  0.6 1.0 slice.3
  1.7 5.2 %collective-permute-start.2 = (f32[256,256]{1,0:T(8,128)S(1)}, f32[256,256]{1,0:T(8,128)S(1)}, u32[]{:S(2)}, u32[]{:S(2)}) collective-permute-start(f32[256,256]{1,0:T(8,128)S(1)} %slice.3), channel_id=1, source_target_pairs={{0,3},{1,2},{32,35},{33,34},{64,67},{65,66},{96,99},{97,98},{128,1... | collective-permute-start | bytes 786440 | tf_op jit(solution)/shard_map/ppermute | solution.py:331
  7.0 1.3 %collective-permute-start = (f32[8,5,8,128]{3,2,1,0:T(8,128)S(1)}, f32[8,5,8,128]{3,2,1,0:T(8,128)S(1)}, u32[]{:S(2)}, u32[]{:S(2)}) collective-permute-start(f32[8,5,8,128]{3,2,1,0:T(8,128)S(1)} %get-tuple-element.33), channel_id=1, source_target_pairs={{0,32},{1,33},{2,34},{3,35},{4,36},{5,37},{6,38},{7,39},{8,40},{9,... | collective-permute-start | bytes 491528 | tf_op jit(solution)/shard_map/ppermute | solution.py:334
  8.3 3.8 %collective-permute-done.got_ref = f32[8,5,8,128]{3,2,1,0:T(8,128)S(1)} collective-permute-done((f32[8,5,8,128]{3,2,1,0:T(8,128)S(1)}, f32[8,5,8,128]{3,2,1,0:T(8,128)S(1)}, u32[]{:S(2)}, u32[]{:S(2)}) %collective-permute-start) | collective-permute-done | bytes 163872 | tf_op jit(solution)/shard_map/ppermute | solution.py:334
  12.1 3.0 %collective-permute-start.1 = (f32[4,5,8,128]{3,2,1,0:T(8,128)S(1)}, f32[4,5,8,128]{3,2,1,0:T(8,128)S(1)}, u32[]{:S(2)}, u32[]{:S(2)}) collective-permute-start(f32[4,5,8,128]{3,2,1,0:T(8,128)S(1)} %get-tuple-element.35), channel_id=1, source_target_pairs={{0,256},{32,288},{1,257},{33,289},{2,258},{34,290},{3,259},{35,291... | collective-permute-start | bytes 245768 | tf_op jit(solution)/shard_map/ppermute | solution.py:334
  15.2 1.5 %collective-permute-done.1.got_ref = f32[4,5,8,128]{3,2,1,0:T(8,128)S(1)} collective-permute-done((f32[4,5,8,128]{3,2,1,0:T(8,128)S(1)}, f32[4,5,8,128]{3,2,1,0:T(8,128)S(1)}, u32[]{:S(2)}, u32[]{:S(2)}) %collective-permute-start.1) | collective-permute-done | bytes 81952 | tf_op jit(solution)/shard_map/ppermute | solution.py:334
  16.7 6.9 %collective-permute-start.5 = (f32[256,256]{1,0:T(8,128)S(1)}, f32[256,256]{1,0:T(8,128)S(1)}, u32[]{:S(2)}, u32[]{:S(2)}) collective-permute-start(f32[256,256]{1,0:T(8,128)S(1)} %get-tuple-element.40.quarter_ref), channel_id=1, source_target_pairs={{0,16},{1,17},{2,18},{3,19},{32,48},{33,49},{34,50},{35,51},{64,80... | collective-permute-start | bytes 786440 | tf_op jit(solution)/shard_map/ppermute | solution.py:331
  23.6 1.3 %collective-permute-start.3 = (f32[2,5,8,128]{3,2,1,0:T(8,128)S(1)}, f32[2,5,8,128]{3,2,1,0:T(8,128)S(1)}, u32[]{:S(2)}, u32[]{:S(2)}) collective-permute-start(f32[2,5,8,128]{3,2,1,0:T(8,128)S(1)} %get-tuple-element.37), channel_id=1, source_target_pairs={{0,128},{32,160},{256,384},{288,416},{1,129},{33,161},{257,385},{2... | collective-permute-start | bytes 122888 | tf_op jit(solution)/shard_map/ppermute | solution.py:334
  24.9 1.1 collective-permute-done.3.got_ref
  26.0 1.3 %collective-permute-start.4 = (f32[1,5,8,128]{3,2,1,0:T(8,128)S(1)}, f32[1,5,8,128]{3,2,1,0:T(8,128)S(1)}, u32[]{:S(2)}, u32[]{:S(2)}) collective-permute-start(f32[1,5,8,128]{3,2,1,0:T(8,128)S(1)} %get-tuple-element.39), channel_id=1, source_target_pairs={{0,64},{32,96},{128,192},{160,224},{256,320},{288,352},{384,448},{... | collective-permute-start | bytes 61448 | tf_op jit(solution)/shard_map/ppermute | solution.py:334
  27.3 0.9 collective-permute-done.4.got_ref
  28.2 0.7 collective-permute-start.10
  28.9 7.5 %collective-permute-start.6 = (f32[5,8,128]{2,1,0:T(8,128)S(1)}, f32[5,8,128]{2,1,0:T(8,128)S(1)}, u32[]{:S(2)}, u32[]{:S(2)}) collective-permute-start(f32[5,8,128]{2,1,0:T(8,128)S(1)} %get-tuple-element.42), channel_id=1, source_target_pairs={{0,16},{1,17},{32,48},{33,49},{64,80},{65,81},{96,112},{97,113},{1... | collective-permute-start | bytes 61448 | tf_op jit(solution)/shard_map/ppermute | solution.py:331
  36.4 1.3 %collective-permute-start.7 = (f32[5,8,128]{2,1,0:T(8,128)S(1)}, f32[5,8,128]{2,1,0:T(8,128)S(1)}, u32[]{:S(2)}, u32[]{:S(2)}) collective-permute-start(f32[5,8,128]{2,1,0:T(8,128)S(1)} %get-tuple-element.42), channel_id=1, source_target_pairs={{0,8},{1,9},{32,40},{33,41},{64,72},{65,73},{96,104},{97,105},{128... | collective-permute-start | bytes 61448 | tf_op jit(solution)/shard_map/ppermute | solution.py:331
  37.7 1.3 %collective-permute-start.8 = (f32[5,8,128]{2,1,0:T(8,128)S(1)}, f32[5,8,128]{2,1,0:T(8,128)S(1)}, u32[]{:S(2)}, u32[]{:S(2)}) collective-permute-start(f32[5,8,128]{2,1,0:T(8,128)S(1)} %get-tuple-element.42), channel_id=1, source_target_pairs={{0,24},{1,25},{32,56},{33,57},{64,88},{65,89},{96,120},{97,121},{1... | collective-permute-start | bytes 61448 | tf_op jit(solution)/shard_map/ppermute | solution.py:331
  39.0 0.9 collective-permute-done.8
  39.9 1.3 %collective-permute-start.9 = (f32[5,8,128]{2,1,0:T(8,128)S(1)}, f32[5,8,128]{2,1,0:T(8,128)S(1)}, u32[]{:S(2)}, u32[]{:S(2)}) collective-permute-start(f32[5,8,128]{2,1,0:T(8,128)S(1)} %add_add_fusion.have_ref), channel_id=1, source_target_pairs={{0,4},{1,5},{8,12},{9,13},{16,20},{17,21},{24,28},{25,29},{32,36},... | collective-permute-start | bytes 61448 | tf_op jit(solution)/shard_map/ppermute | solution.py:331
  41.2 0.9 collective-permute-done.9.got_ref
  42.8 3.3 %collective-permute-start.14 = (f32[256,256]{1,0:T(8,128)S(1)}, f32[256,256]{1,0:T(8,128)S(1)}, u32[]{:S(2)}, u32[]{:S(2)}) collective-permute-start(f32[256,256]{1,0:T(8,128)S(1)} %get-tuple-element.45.quarter_ref), channel_id=1, source_target_pairs={{0,8},{1,9},{2,10},{3,11},{16,24},{17,25},{18,26},{19,27},{32,40},... | collective-permute-start | bytes 786440 | tf_op jit(solution)/shard_map/ppermute | solution.py:331
  46.1 3.1 %collective-permute-start.11 = (f32[5,8,128]{2,1,0:T(8,128)S(1)}, f32[5,8,128]{2,1,0:T(8,128)S(1)}, u32[]{:S(2)}, u32[]{:S(2)}) collective-permute-start(f32[5,8,128]{2,1,0:T(8,128)S(1)} %get-tuple-element.44.own_ref), channel_id=1, source_target_pairs={{0,1},{1,0},{4,5},{5,4},{8,9},{9,8},{12,13},{13,12},{16,17},{17,16... | collective-permute-start | bytes 61448 | tf_op jit(solution)/shard_map/ppermute | solution.py:331
  49.2 1.3 %collective-permute-start.12 = (f32[5,8,128]{2,1,0:T(8,128)S(1)}, f32[5,8,128]{2,1,0:T(8,128)S(1)}, u32[]{:S(2)}, u32[]{:S(2)}) collective-permute-start(f32[5,8,128]{2,1,0:T(8,128)S(1)} %get-tuple-element.44.own_ref), channel_id=1, source_target_pairs={{0,2},{1,3},{4,6},{5,7},{8,10},{9,11},{12,14},{13,15},{16,18},{17,... | collective-permute-start | bytes 61448 | tf_op jit(solution)/shard_map/ppermute | solution.py:331
  50.5 1.3 %collective-permute-start.13 = (f32[5,8,128]{2,1,0:T(8,128)S(1)}, f32[5,8,128]{2,1,0:T(8,128)S(1)}, u32[]{:S(2)}, u32[]{:S(2)}) collective-permute-start(f32[5,8,128]{2,1,0:T(8,128)S(1)} %get-tuple-element.44.own_ref), channel_id=1, source_target_pairs={{0,3},{1,2},{4,7},{5,6},{8,11},{9,10},{12,15},{13,14},{16,19},{17,... | collective-permute-start | bytes 61448 | tf_op jit(solution)/shard_map/ppermute | solution.py:331
  51.9 0.9 collective-permute-done.13.o3_ref
  52.8 1.3 %collective-permute-start.16 = (f32[256,256]{1,0:T(8,128)S(1)}, f32[256,256]{1,0:T(8,128)S(1)}, u32[]{:S(2)}, u32[]{:S(2)}) collective-permute-start(f32[256,256]{1,0:T(8,128)S(1)} %get-tuple-element.49.quarter_ref), channel_id=1, source_target_pairs={{0,4},{1,5},{2,6},{3,7},{8,12},{9,13},{10,14},{11,15},{16,20},{17,... | collective-permute-start | bytes 786440 | tf_op jit(solution)/shard_map/ppermute | solution.py:331
  54.1 29.6 %all-gather = f32[160,8,128]{2,1,0:T(8,128)S(1)} all-gather(f32[10,8,128]{2,1,0:T(8,128)S(1)} %get-tuple-element.47), channel_id=2, replica_groups=mesh['row'=16,'col'=32] {'row'}, dimensions={0}, use_global_device_ids=true | all-gather | bytes 696320 | tf_op jit(solution)/shard_map/all_gather | solution.py:372
  84.5 2.2 %collective-permute-start.17 = (f32[256,256]{1,0:T(8,128)S(1)}, f32[256,256]{1,0:T(8,128)S(1)}, u32[]{:S(2)}, u32[]{:S(2)}) collective-permute-start(f32[256,256]{1,0:T(8,128)S(1)} %get-tuple-element.50.after_ref.q0_ref), channel_id=1, source_target_pairs={{0,1},{1,2},{2,3},{3,0},{4,5},{5,6},{6,7},{7,4},{8,9},{9,10},{10,1... | collective-permute-start | bytes 786440 | tf_op jit(solution)/shard_map/ppermute | solution.py:331
  86.6 4.9 %collective-permute-start.18 = (f32[256,256]{1,0:T(8,128)S(1)}, f32[256,256]{1,0:T(8,128)S(1)}, u32[]{:S(2)}, u32[]{:S(2)}) collective-permute-start(f32[256,256]{1,0:T(8,128)S(1)} %get-tuple-element.50.after_ref.q0_ref), channel_id=1, source_target_pairs={{0,3},{1,0},{2,1},{3,2},{4,7},{5,4},{6,5},{7,6},{8,11},{9,8},{10,9... | collective-permute-start | bytes 786440 | tf_op jit(solution)/shard_map/ppermute | solution.py:331
  91.5 11.4 %shard_map.38 = (f32[512,512]{1,0:T(8,128)S(1)}, f32[512,512]{1,0:T(8,128)S(1)}, f32[512,512]{1,0:T(8,128)S(1)}) custom-call(f32[16,10,8,128]{3,2,1,0:T(8,128)S(1)} %get-tuple-element.51.g_ref, f32[256,256]{1,0:T(8,128)S(1)} %get-tuple-element.50.after_ref.q0_ref), custom_call_target="tpu_custom_call" | custom-call | tf_op jit(solution)/shard_map/pallas_call | solution.py:128
  103.0 1.5 %collective-permute-start.21 = (f32[512,256]{1,0:T(8,128)S(1)}, f32[512,256]{1,0:T(8,128)S(1)}, u32[]{:S(2)}, u32[]{:S(2)}) collective-permute-start(f32[512,256]{1,0:T(8,128)S(1)} %get-tuple-element.56.after_ref.top_ref), channel_id=1, source_target_pairs={{0,32},{64,96},{128,160},{192,224},{256,288},{320,352},{384,416},{... | collective-permute-start | bytes 1572872 | tf_op jit(solution)/shard_map/ppermute | solution.py:334
  104.5 1.9 %collective-permute-start.20 = (f32[256,256]{1,0:T(8,128)S(1)}, f32[256,256]{1,0:T(8,128)S(1)}, u32[]{:S(2)}, u32[]{:S(2)}) collective-permute-start(f32[256,256]{1,0:T(8,128)S(1)} %get-tuple-element.54.q1_ref), channel_id=1, source_target_pairs={{0,1},{1,2},{2,3},{3,0},{4,5},{5,6},{6,7},{7,4},{8,9},{9,10},{10,1... | collective-permute-start | bytes 786440 | tf_op jit(solution)/shard_map/ppermute | solution.py:331
  106.4 9.9 %shard_map.40 = (f32[512,512]{1,0:T(8,128)S(1)}, f32[512,512]{1,0:T(8,128)S(1)}, f32[512,512]{1,0:T(8,128)S(1)}) custom-call(f32[512,512]{1,0:T(8,128)S(1)} %get-tuple-element.57.s_in, f32[512,512]{1,0:T(8,128)S(1)} %get-tuple-element.58.l_in, f32[512,512]{1,0:T(8,128)S(1)} %get-tuple-element.59.inv_in, ...), custom_call_target="tpu_custom_call", output_to_operand_aliasing={{0}: (0, {}), {1}: (1, {}), {2}: (2, {})} | custom-call | tf_op jit(solution)/shard_map/pallas_call | solution.py:139
  116.4 3.4 %shard_map.41 = (f32[16,512]{1,0:T(8,128)}, f32[512,256]{1,0:T(8,128)}) custom-call(f32[512,256]{1,0:T(8,128)S(1)} %copy-done, f32[256,256]{1,0:T(8,128)S(1)} %get-tuple-element.50.after_ref.q0_ref, f32[256,256]{1,0:T(8,128)S(1)} %get-tuple-element.54.q1_ref, f32[256,256]{1,0:T(8,128)S(1)} %get-tuple-element.55.q2_ref, ...), custom_call_target="tpu_custom_call" | custom-call | tf_op jit(solution)/shard_map/pallas_call | solution.py:201
  (29 shorter events, 1.8 us)
Async XLA Ops:
  0.6 6.3 %copy-start = (f32[512,256]{1,0:T(8,128)S(1)}, f32[512,256]{1,0:T(8,128)}, u32[]{:S(2)}) copy-start(f32[512,256]{1,0:T(8,128)} %x_ref.7) | copy-start | bytes 1572868
  1.7 14.9 %collective-permute-start.2 = (f32[256,256]{1,0:T(8,128)S(1)}, f32[256,256]{1,0:T(8,128)S(1)}, u32[]{:S(2)}, u32[]{:S(2)}) collective-permute-start(f32[256,256]{1,0:T(8,128)S(1)} %slice.3), channel_id=1, source_target_pairs={{0,3},{1,2},{32,35},{33,34},{64,67},{65,66},{96,99},{97,98},{128,1... | collective-permute-start | bytes 786440 | tf_op jit(solution)/shard_map/ppermute | solution.py:331
  7.0 5.1 %collective-permute-start = (f32[8,5,8,128]{3,2,1,0:T(8,128)S(1)}, f32[8,5,8,128]{3,2,1,0:T(8,128)S(1)}, u32[]{:S(2)}, u32[]{:S(2)}) collective-permute-start(f32[8,5,8,128]{3,2,1,0:T(8,128)S(1)} %get-tuple-element.33), channel_id=1, source_target_pairs={{0,32},{1,33},{2,34},{3,35},{4,36},{5,37},{6,38},{7,39},{8,40},{9,... | collective-permute-start | bytes 491528 | tf_op jit(solution)/shard_map/ppermute | solution.py:334
  12.1 4.5 %collective-permute-start.1 = (f32[4,5,8,128]{3,2,1,0:T(8,128)S(1)}, f32[4,5,8,128]{3,2,1,0:T(8,128)S(1)}, u32[]{:S(2)}, u32[]{:S(2)}) collective-permute-start(f32[4,5,8,128]{3,2,1,0:T(8,128)S(1)} %get-tuple-element.35), channel_id=1, source_target_pairs={{0,256},{32,288},{1,257},{33,289},{2,258},{34,290},{3,259},{35,291... | collective-permute-start | bytes 245768 | tf_op jit(solution)/shard_map/ppermute | solution.py:334
  16.7 11.5 %collective-permute-start.5 = (f32[256,256]{1,0:T(8,128)S(1)}, f32[256,256]{1,0:T(8,128)S(1)}, u32[]{:S(2)}, u32[]{:S(2)}) collective-permute-start(f32[256,256]{1,0:T(8,128)S(1)} %get-tuple-element.40.quarter_ref), channel_id=1, source_target_pairs={{0,16},{1,17},{2,18},{3,19},{32,48},{33,49},{34,50},{35,51},{64,80... | collective-permute-start | bytes 786440 | tf_op jit(solution)/shard_map/ppermute | solution.py:331
  23.6 2.4 %collective-permute-start.3 = (f32[2,5,8,128]{3,2,1,0:T(8,128)S(1)}, f32[2,5,8,128]{3,2,1,0:T(8,128)S(1)}, u32[]{:S(2)}, u32[]{:S(2)}) collective-permute-start(f32[2,5,8,128]{3,2,1,0:T(8,128)S(1)} %get-tuple-element.37), channel_id=1, source_target_pairs={{0,128},{32,160},{256,384},{288,416},{1,129},{33,161},{257,385},{2... | collective-permute-start | bytes 122888 | tf_op jit(solution)/shard_map/ppermute | solution.py:334
  26.0 2.2 %collective-permute-start.4 = (f32[1,5,8,128]{3,2,1,0:T(8,128)S(1)}, f32[1,5,8,128]{3,2,1,0:T(8,128)S(1)}, u32[]{:S(2)}, u32[]{:S(2)}) collective-permute-start(f32[1,5,8,128]{3,2,1,0:T(8,128)S(1)} %get-tuple-element.39), channel_id=1, source_target_pairs={{0,64},{32,96},{128,192},{160,224},{256,320},{288,352},{384,448},{... | collective-permute-start | bytes 61448 | tf_op jit(solution)/shard_map/ppermute | solution.py:334
  28.2 13.9 %collective-permute-start.10 = (f32[512,256]{1,0:T(8,128)S(1)}, f32[512,256]{1,0:T(8,128)S(1)}, u32[]{:S(2)}, u32[]{:S(2)}) collective-permute-start(f32[512,256]{1,0:T(8,128)S(1)} %get-tuple-element.43.top_ref), channel_id=1, source_target_pairs={{0,256},{1,257},{2,258},{3,259},{4,260},{5,261},{6,262},{7,263},{8... | collective-permute-start | bytes 1572872 | tf_op jit(solution)/shard_map/ppermute | solution.py:334
  28.9 10.1 %collective-permute-start.6 = (f32[5,8,128]{2,1,0:T(8,128)S(1)}, f32[5,8,128]{2,1,0:T(8,128)S(1)}, u32[]{:S(2)}, u32[]{:S(2)}) collective-permute-start(f32[5,8,128]{2,1,0:T(8,128)S(1)} %get-tuple-element.42), channel_id=1, source_target_pairs={{0,16},{1,17},{32,48},{33,49},{64,80},{65,81},{96,112},{97,113},{1... | collective-permute-start | bytes 61448 | tf_op jit(solution)/shard_map/ppermute | solution.py:331
  36.4 2.6 %collective-permute-start.7 = (f32[5,8,128]{2,1,0:T(8,128)S(1)}, f32[5,8,128]{2,1,0:T(8,128)S(1)}, u32[]{:S(2)}, u32[]{:S(2)}) collective-permute-start(f32[5,8,128]{2,1,0:T(8,128)S(1)} %get-tuple-element.42), channel_id=1, source_target_pairs={{0,8},{1,9},{32,40},{33,41},{64,72},{65,73},{96,104},{97,105},{128... | collective-permute-start | bytes 61448 | tf_op jit(solution)/shard_map/ppermute | solution.py:331
  37.7 2.2 %collective-permute-start.8 = (f32[5,8,128]{2,1,0:T(8,128)S(1)}, f32[5,8,128]{2,1,0:T(8,128)S(1)}, u32[]{:S(2)}, u32[]{:S(2)}) collective-permute-start(f32[5,8,128]{2,1,0:T(8,128)S(1)} %get-tuple-element.42), channel_id=1, source_target_pairs={{0,24},{1,25},{32,56},{33,57},{64,88},{65,89},{96,120},{97,121},{1... | collective-permute-start | bytes 61448 | tf_op jit(solution)/shard_map/ppermute | solution.py:331
  39.9 2.2 %collective-permute-start.9 = (f32[5,8,128]{2,1,0:T(8,128)S(1)}, f32[5,8,128]{2,1,0:T(8,128)S(1)}, u32[]{:S(2)}, u32[]{:S(2)}) collective-permute-start(f32[5,8,128]{2,1,0:T(8,128)S(1)} %add_add_fusion.have_ref), channel_id=1, source_target_pairs={{0,4},{1,5},{8,12},{9,13},{16,20},{17,21},{24,28},{25,29},{32,36},... | collective-permute-start | bytes 61448 | tf_op jit(solution)/shard_map/ppermute | solution.py:331
  42.1 10.6 %collective-permute-start.15 = (f32[512,256]{1,0:T(8,128)S(1)}, f32[512,256]{1,0:T(8,128)S(1)}, u32[]{:S(2)}, u32[]{:S(2)}) collective-permute-start(f32[512,256]{1,0:T(8,128)S(1)} %get-tuple-element.46.top_ref), channel_id=1, source_target_pairs={{0,128},{256,384},{1,129},{257,385},{2,130},{258,386},{3,131},{259... | collective-permute-start | bytes 1572872 | tf_op jit(solution)/shard_map/ppermute | solution.py:334
  42.8 9.9 %collective-permute-start.14 = (f32[256,256]{1,0:T(8,128)S(1)}, f32[256,256]{1,0:T(8,128)S(1)}, u32[]{:S(2)}, u32[]{:S(2)}) collective-permute-start(f32[256,256]{1,0:T(8,128)S(1)} %get-tuple-element.45.quarter_ref), channel_id=1, source_target_pairs={{0,8},{1,9},{2,10},{3,11},{16,24},{17,25},{18,26},{19,27},{32,40},... | collective-permute-start | bytes 786440 | tf_op jit(solution)/shard_map/ppermute | solution.py:331
  46.1 5.7 %collective-permute-start.11 = (f32[5,8,128]{2,1,0:T(8,128)S(1)}, f32[5,8,128]{2,1,0:T(8,128)S(1)}, u32[]{:S(2)}, u32[]{:S(2)}) collective-permute-start(f32[5,8,128]{2,1,0:T(8,128)S(1)} %get-tuple-element.44.own_ref), channel_id=1, source_target_pairs={{0,1},{1,0},{4,5},{5,4},{8,9},{9,8},{12,13},{13,12},{16,17},{17,16... | collective-permute-start | bytes 61448 | tf_op jit(solution)/shard_map/ppermute | solution.py:331
  49.2 2.6 %collective-permute-start.12 = (f32[5,8,128]{2,1,0:T(8,128)S(1)}, f32[5,8,128]{2,1,0:T(8,128)S(1)}, u32[]{:S(2)}, u32[]{:S(2)}) collective-permute-start(f32[5,8,128]{2,1,0:T(8,128)S(1)} %get-tuple-element.44.own_ref), channel_id=1, source_target_pairs={{0,2},{1,3},{4,6},{5,7},{8,10},{9,11},{12,14},{13,15},{16,18},{17,... | collective-permute-start | bytes 61448 | tf_op jit(solution)/shard_map/ppermute | solution.py:331
  50.5 2.2 %collective-permute-start.13 = (f32[5,8,128]{2,1,0:T(8,128)S(1)}, f32[5,8,128]{2,1,0:T(8,128)S(1)}, u32[]{:S(2)}, u32[]{:S(2)}) collective-permute-start(f32[5,8,128]{2,1,0:T(8,128)S(1)} %get-tuple-element.44.own_ref), channel_id=1, source_target_pairs={{0,3},{1,2},{4,7},{5,6},{8,11},{9,10},{12,15},{13,14},{16,19},{17,... | collective-permute-start | bytes 61448 | tf_op jit(solution)/shard_map/ppermute | solution.py:331
  52.8 30.9 %collective-permute-start.16 = (f32[256,256]{1,0:T(8,128)S(1)}, f32[256,256]{1,0:T(8,128)S(1)}, u32[]{:S(2)}, u32[]{:S(2)}) collective-permute-start(f32[256,256]{1,0:T(8,128)S(1)} %get-tuple-element.49.quarter_ref), channel_id=1, source_target_pairs={{0,4},{1,5},{2,6},{3,7},{8,12},{9,13},{10,14},{11,15},{16,20},{17,... | collective-permute-start | bytes 786440 | tf_op jit(solution)/shard_map/ppermute | solution.py:331
  83.8 19.2 %collective-permute-start.19 = (f32[512,256]{1,0:T(8,128)S(1)}, f32[512,256]{1,0:T(8,128)S(1)}, u32[]{:S(2)}, u32[]{:S(2)}) collective-permute-start(f32[512,256]{1,0:T(8,128)S(1)} %get-tuple-element.53.top_ref), channel_id=1, source_target_pairs={{0,64},{128,192},{256,320},{384,448},{1,65},{129,193},{257,321},{3... | collective-permute-start | bytes 1572872 | tf_op jit(solution)/shard_map/ppermute | solution.py:334
  84.5 18.4 %collective-permute-start.17 = (f32[256,256]{1,0:T(8,128)S(1)}, f32[256,256]{1,0:T(8,128)S(1)}, u32[]{:S(2)}, u32[]{:S(2)}) collective-permute-start(f32[256,256]{1,0:T(8,128)S(1)} %get-tuple-element.50.after_ref.q0_ref), channel_id=1, source_target_pairs={{0,1},{1,2},{2,3},{3,0},{4,5},{5,6},{6,7},{7,4},{8,9},{9,10},{10,1... | collective-permute-start | bytes 786440 | tf_op jit(solution)/shard_map/ppermute | solution.py:331
  86.6 16.3 %collective-permute-start.18 = (f32[256,256]{1,0:T(8,128)S(1)}, f32[256,256]{1,0:T(8,128)S(1)}, u32[]{:S(2)}, u32[]{:S(2)}) collective-permute-start(f32[256,256]{1,0:T(8,128)S(1)} %get-tuple-element.50.after_ref.q0_ref), channel_id=1, source_target_pairs={{0,3},{1,0},{2,1},{3,2},{4,7},{5,4},{6,5},{7,6},{8,11},{9,8},{10,9... | collective-permute-start | bytes 786440 | tf_op jit(solution)/shard_map/ppermute | solution.py:331
  103.0 13.4 %collective-permute-start.21 = (f32[512,256]{1,0:T(8,128)S(1)}, f32[512,256]{1,0:T(8,128)S(1)}, u32[]{:S(2)}, u32[]{:S(2)}) collective-permute-start(f32[512,256]{1,0:T(8,128)S(1)} %get-tuple-element.56.after_ref.top_ref), channel_id=1, source_target_pairs={{0,32},{64,96},{128,160},{192,224},{256,288},{320,352},{384,416},{... | collective-permute-start | bytes 1572872 | tf_op jit(solution)/shard_map/ppermute | solution.py:334
  104.5 11.9 %collective-permute-start.20 = (f32[256,256]{1,0:T(8,128)S(1)}, f32[256,256]{1,0:T(8,128)S(1)}, u32[]{:S(2)}, u32[]{:S(2)}) collective-permute-start(f32[256,256]{1,0:T(8,128)S(1)} %get-tuple-element.54.q1_ref), channel_id=1, source_target_pairs={{0,1},{1,2},{2,3},{3,0},{4,5},{5,6},{6,7},{7,4},{8,9},{9,10},{10,1... | collective-permute-start | bytes 786440 | tf_op jit(solution)/shard_map/ppermute | solution.py:331

commit v5 on v4

--- a/solution.py
+++ b/solution.py
@@ -278,10 +278,10 @@
     halve(lax.rem(place()[0] // 2, 2) == 1, got_ref, have_ref, low_ref, high_ref)
 
 
-def y1_kernel(have_ref, got_ref, x_ref, quarter_ref, far_ref, piece_ref, top_ref, quarter_out):
+def y1_kernel(have_ref, got_ref, x_ref, down_ref, quarter_ref, far_ref, piece_ref, top_ref, quarter_out):
     y, core, z, xi = place()
     choose(quarter_out, z >= 4, far_ref, quarter_ref)
-    top_ref[...] = x_ref[...]
+    choose(top_ref, y >= 4, down_ref, x_ref)
     holds = jnp.logical_and(z == 0, xi < 2)
 
     @pl.when(holds)
@@ -297,7 +297,7 @@
     del quarter_in, quarter_ref
     y, core, z, xi = place()
     choose(piece_ref, lax.rem(z, 2) == 1, got_ref, have_ref)
-    choose(top_out, y >= 4, down_ref, top_ref)
+    choose(top_out, lax.rem(y // 2, 2) == 1, down_ref, top_ref)
 
 
 def x_kernel(own_ref, o1_ref, o2_ref, o3_ref, quarter_ref, far_ref, top_ref, down_ref, both_ref, quarter_out, top_out):
@@ -311,49 +311,53 @@
             both_ref[5:] = right[...]
 
     choose(quarter_out, lax.rem(z // 2, 2) == 1, far_ref, quarter_ref)
-    choose(top_out, lax.rem(y // 2, 2) == 1, down_ref, top_ref)
-
-
-def gate_kernel(g_in, top_in, quarter_ref, far_ref, g_ref, top_ref, quarter_out):
-    del g_in, top_in, g_ref, top_ref
+    choose(top_out, lax.rem(y, 2) == 1, down_ref, top_ref)
+
+
+def gate_kernel(g_in, down_in, quarter_ref, far_ref, g_ref, down_ref, quarter_out):
+    del g_in, down_in, g_ref, down_ref
     choose(quarter_out, lax.rem(place()[2], 2) == 1, far_ref, quarter_ref)
 
 
-def mid_kernel(s_in, q1_in, q2_in, top_ref, down_ref, s_ref, q1_ref, q2_ref, top_out):
-    del s_in, q1_in, q2_in, s_ref, q1_ref, q2_ref
-    choose(top_out, lax.rem(place()[0], 2) == 1, down_ref, top_ref)
+def mid_kernel(*refs):
+    del refs
 
 
 def on_device(x):
     zs, xs, ys = range(8), range(4), range(8)
-
-    def along(v, pairs):
-        return lax.ppermute(v, "col", pairs)
-
-    def across(v, pairs):
-        return lax.ppermute(v, "row", pairs)
+    below, firsts = range(1, 16), range(2)
+
+    def send(v, pairs):
+        return lax.ppermute(v, ("row", "col"), [(32 * a + b, 32 * c + d) for (a, b), (c, d) in pairs])
+
+    def along(v, pairs, rows=range(16)):
+        return send(v, [((r, a), (r, b)) for r in rows for a, b in pairs])
+
+    def across(v, pairs, cols=range(2, 32)):
+        return send(v, [((a, c), (b, c)) for c in cols for a, b in pairs])
 
     def by_z(v, step):
         holders = range(0, 8, 2 * step)
-        return along(v, [(4 * z + i, 4 * (z + step) + i) for z in holders for i in xs])
+        return along(v, [(4 * z + i, 4 * (z + step) + i) for z in holders for i in xs], below)
 
     def by_x(v, step):
-        return along(v, [(4 * z + i, 4 * z + (i + step) % 4) for z in zs for i in xs])
-
-    far = along(x[2 * B :], [(0, 3), (1, 2)])
+        return along(v, [(4 * z + i, 4 * z + (i + step) % 4) for z in zs for i in xs], below)
+
+    far = along(x[2 * B :], [(0, 3), (1, 2)], below)
+    down = across(x, [(0, 8)])
     low, high = local(pack_kernel, (x,), (f32(8, 5, 8, B),) * 2)
-    got = across(high, [(0, 1)])
+    got = across(high, [(0, 1)], firsts)
     low, high = local(core_kernel, (low, got), (f32(4, 5, 8, B),) * 2)
-    got = across(high, [(0, 8), (1, 9)])
+    got = across(high, [(0, 8), (1, 9)], firsts)
     quarter = f32(2 * B, 2 * B)
     low, high, part = local(y4_kernel, (low, got, x, far), (f32(2, 5, 8, B),) * 2 + (quarter,))
     far = by_z(part, 4)
-    got = across(high, [(0, 4), (1, 5), (8, 12), (9, 13)])
+    got = across(high, [(0, 4), (1, 5), (8, 12), (9, 13)], firsts)
     low, high = local(y2_kernel, (low, got), (f32(1, 5, 8, B),) * 2)
-    got = across(high, [(4 * q + k, 4 * q + k + 2) for q in range(4) for k in (0, 1)])
-    piece, top, part = local(y1_kernel, (low, got, x, part, far), (f32(5, 8, B), f32(*x.shape), quarter))
-
-    down = across(top, [(0, 8)])
+    got = across(high, [(4 * q + k, 4 * q + k + 2) for q in range(4) for k in (0, 1)], firsts)
+    piece, top, part = local(y1_kernel, (low, got, x, down, part, far), (f32(5, 8, B), f32(*x.shape), quarter))
+
+    down = across(top, [(0, 4), (8, 12)])
     piece += sum(along(piece, [(0, 4 * z), (1, 4 * z + 1)]) for z in (4, 2, 6))
     got = along(piece, [(4 * z + i, 4 * z + 4 + i) for z in (0, 2, 4, 6) for i in (0, 1)])
     part, piece, top = local(
@@ -364,24 +368,21 @@
         for pairs in (((0, 1), (1, 0)), ((0, 2), (1, 3)), ((0, 3), (1, 2)))
     ]
     far = by_z(part, 2)
-    down = across(top, [(0, 4), (8, 12)])
+    down = across(top, [(4 * q, 4 * q + 2) for q in range(4)])
     both, part, top = local(
         x_kernel, (piece, *others, part, far, top, down), (f32(10, 8, B), quarter, f32(*x.shape))
     )
     far = by_z(part, 1)
+    down = across(top, [(2 * y, 2 * y + 1) for y in ys])
     gathered = lax.all_gather(both, "row")
-    gathered, top, part = local(
-        gate_kernel, (gathered, top, part, far), (f32(16, 10, 8, B), f32(*x.shape), quarter), {0: 0, 1: 1}
+    gathered, down, part = local(
+        gate_kernel, (gathered, down, part, far), (f32(16, 10, 8, B), f32(*x.shape), quarter), {0: 0, 1: 1}
     )
-    down = across(top, [(4 * q, 4 * q + 2) for q in range(4)])
     near, next_ = by_x(part, 1), by_x(part, 3)
     s, lower, inv = first_half(gathered, part)
-    s, near, next_, top = local(
-        mid_kernel, (s, near, next_, top, down), (SQUARE, quarter, quarter, f32(*x.shape)), {0: 0, 1: 1, 2: 2}
-    )
-    down = across(top, [(2 * y, 2 * y + 1) for y in ys])
+    s, near, next_ = local(mid_kernel, (s, near, next_), (SQUARE, quarter, quarter), {0: 0, 1: 1, 2: 2})
     opposite = by_x(near, 1)
-    _, lower, inv = second_half(s, lower, inv, top)
+    _, lower, inv = second_half(s, lower, inv, near)
     return final(x, part, near, next_, opposite, top, down, lower, inv)
 
 

time: 121 us -> 110 us (0.909)
  starting transfers between devices: 53.2 us -> 45.4 us
  blocking collectives: 29.6 us -> 28 us
    ppermute x22, starting transfers between devices: 53.2 us -> 45.4 us  [send(): lax.ppermute(v, ('row', 'col'), [(32 * a + b, 32 * c + d) for (a, b), (c,...]
    all_gather x1, blocking collectives: 29.6 us -> 28 us  [on_device(): gathered = lax.all_gather(both, 'row')]
  transfers between devices with their start and end apart: 22 -> 22, of which waited for: 7 -> 7; matrix products, arithmetic and copies ran while one was open for 0% -> 0% of each run, Pallas kernels for 18% -> 19%
where the time goes in v5:
time: 110 us
  starting transfers between devices  45.4 us (41%)
  blocking collectives  28 us (25%)
  Pallas kernels  25.1 us (23%)
  waiting for transfers between devices  9.29 us (8%)
    ppermute x22, starting transfers between devices, send(): lax.ppermute(v, ('row', 'col'), [(32 * a + b, 32 * c + d) for (a, b), (c,...  45.4 us
    all_gather x1, blocking collectives, on_device(): gathered = lax.all_gather(both, 'row')  28 us
    pallas_call x1, Pallas kernels, first_half(): pl.pallas_call(first_kernel, out_shape=(SQUARE,) * 3, in_specs=[whole(),...  11.4 us
    pallas_call x1, Pallas kernels, second_half(): pl.pallas_call(second_kernel, out_shape=(SQUARE,) * 3, in_specs=[whole()]...  9.94 us
    ppermute x22, waiting for transfers between devices, send(): lax.ppermute(v, ('row', 'col'), [(32 * a + b, 32 * c + d) for (a, b), (c,...  9.29 us
    pallas_call x1, Pallas kernels, final(): pl.pallas_call(final_kernel, out_shape=(jax.ShapeDtypeStruct((16, 512), j...  3.46 us
  transfers between devices with their start and end apart: 22, of which 7 were waited for; matrix products, arithmetic and copies ran while one was open for 0% of the time, Pallas kernels for 19%

profile of v5, /device:TPU:1, one launch (start us, length us, event | category | flops | bytes accessed | tf_op | source)
XLA Modules:
  0.0 109.7 jit_solution(3850274071259499899)
XLA Ops:
  0.6 1.0 slice.3
  1.7 5.2 %collective-permute-start.2 = (f32[256,256]{1,0:T(8,128)S(1)}, f32[256,256]{1,0:T(8,128)S(1)}, u32[]{:S(2)}, u32[]{:S(2)}) collective-permute-start(f32[256,256]{1,0:T(8,128)S(1)} %slice.3), channel_id=1, source_target_pairs={{32,35},{33,34},{64,67},{65,66},{96,99},{97,98},{128,131},{129,130... | collective-permute-start | bytes 786440 | tf_op jit(solution)/shard_map/ppermute | solution.py:331
  6.9 0.7 collective-permute-start.5
  7.7 1.3 %collective-permute-start = (f32[8,5,8,128]{3,2,1,0:T(8,128)S(1)}, f32[8,5,8,128]{3,2,1,0:T(8,128)S(1)}, u32[]{:S(2)}, u32[]{:S(2)}) collective-permute-start(f32[8,5,8,128]{3,2,1,0:T(8,128)S(1)} %get-tuple-element.32), channel_id=1, source_target_pairs={{0,32},{1,33}} | collective-permute-start | bytes 491528 | tf_op jit(solution)/shard_map/ppermute | solution.py:331
  9.0 3.2 %collective-permute-done.got_ref = f32[8,5,8,128]{3,2,1,0:T(8,128)S(1)} collective-permute-done((f32[8,5,8,128]{3,2,1,0:T(8,128)S(1)}, f32[8,5,8,128]{3,2,1,0:T(8,128)S(1)}, u32[]{:S(2)}, u32[]{:S(2)}) %collective-permute-start) | collective-permute-done | bytes 163872 | tf_op jit(solution)/shard_map/ppermute | solution.py:331
  12.2 3.7 %collective-permute-start.1 = (f32[4,5,8,128]{3,2,1,0:T(8,128)S(1)}, f32[4,5,8,128]{3,2,1,0:T(8,128)S(1)}, u32[]{:S(2)}, u32[]{:S(2)}) collective-permute-start(f32[4,5,8,128]{3,2,1,0:T(8,128)S(1)} %get-tuple-element.34), channel_id=1, source_target_pairs={{0,256},{32,288},{1,257},{33,289}} | collective-permute-start | bytes 245768 | tf_op jit(solution)/shard_map/ppermute | solution.py:331
  15.9 1.5 %collective-permute-done.1.got_ref = f32[4,5,8,128]{3,2,1,0:T(8,128)S(1)} collective-permute-done((f32[4,5,8,128]{3,2,1,0:T(8,128)S(1)}, f32[4,5,8,128]{3,2,1,0:T(8,128)S(1)}, u32[]{:S(2)}, u32[]{:S(2)}) %collective-permute-start.1) | collective-permute-done | bytes 81952 | tf_op jit(solution)/shard_map/ppermute | solution.py:331
  17.4 1.3 %collective-permute-start.6 = (f32[256,256]{1,0:T(8,128)S(1)}, f32[256,256]{1,0:T(8,128)S(1)}, u32[]{:S(2)}, u32[]{:S(2)}) collective-permute-start(f32[256,256]{1,0:T(8,128)S(1)} %get-tuple-element.39.quarter_ref), channel_id=1, source_target_pairs={{32,48},{33,49},{34,50},{35,51},{64,80},{65,81},{66,82},{67,83},{9... | collective-permute-start | bytes 786440 | tf_op jit(solution)/shard_map/ppermute | solution.py:331
  18.7 1.6 %collective-permute-start.3 = (f32[2,5,8,128]{3,2,1,0:T(8,128)S(1)}, f32[2,5,8,128]{3,2,1,0:T(8,128)S(1)}, u32[]{:S(2)}, u32[]{:S(2)}) collective-permute-start(f32[2,5,8,128]{3,2,1,0:T(8,128)S(1)} %get-tuple-element.36), channel_id=1, source_target_pairs={{0,128},{32,160},{256,384},{288,416},{1,129},{33,161},{257,385},{2... | collective-permute-start | bytes 122888 | tf_op jit(solution)/shard_map/ppermute | solution.py:331
  20.3 1.1 collective-permute-done.3.got_ref
  21.4 1.3 %collective-permute-start.4 = (f32[1,5,8,128]{3,2,1,0:T(8,128)S(1)}, f32[1,5,8,128]{3,2,1,0:T(8,128)S(1)}, u32[]{:S(2)}, u32[]{:S(2)}) collective-permute-start(f32[1,5,8,128]{3,2,1,0:T(8,128)S(1)} %get-tuple-element.38), channel_id=1, source_target_pairs={{0,64},{32,96},{128,192},{160,224},{256,320},{288,352},{384,448},{... | collective-permute-start | bytes 61448 | tf_op jit(solution)/shard_map/ppermute | solution.py:331
  22.7 0.9 collective-permute-done.4.got_ref
  23.7 0.7 collective-permute-start.11
  24.4 6.1 %collective-permute-start.7 = (f32[5,8,128]{2,1,0:T(8,128)S(1)}, f32[5,8,128]{2,1,0:T(8,128)S(1)}, u32[]{:S(2)}, u32[]{:S(2)}) collective-permute-start(f32[5,8,128]{2,1,0:T(8,128)S(1)} %get-tuple-element.41), channel_id=1, source_target_pairs={{0,16},{1,17},{32,48},{33,49},{64,80},{65,81},{96,112},{97,113},{1... | collective-permute-start | bytes 61448 | tf_op jit(solution)/shard_map/ppermute | solution.py:331
  30.5 1.3 %collective-permute-start.8 = (f32[5,8,128]{2,1,0:T(8,128)S(1)}, f32[5,8,128]{2,1,0:T(8,128)S(1)}, u32[]{:S(2)}, u32[]{:S(2)}) collective-permute-start(f32[5,8,128]{2,1,0:T(8,128)S(1)} %get-tuple-element.41), channel_id=1, source_target_pairs={{0,8},{1,9},{32,40},{33,41},{64,72},{65,73},{96,104},{97,105},{128... | collective-permute-start | bytes 61448 | tf_op jit(solution)/shard_map/ppermute | solution.py:331
  31.8 1.3 %collective-permute-start.9 = (f32[5,8,128]{2,1,0:T(8,128)S(1)}, f32[5,8,128]{2,1,0:T(8,128)S(1)}, u32[]{:S(2)}, u32[]{:S(2)}) collective-permute-start(f32[5,8,128]{2,1,0:T(8,128)S(1)} %get-tuple-element.41), channel_id=1, source_target_pairs={{0,24},{1,25},{32,56},{33,57},{64,88},{65,89},{96,120},{97,121},{1... | collective-permute-start | bytes 61448 | tf_op jit(solution)/shard_map/ppermute | solution.py:331
  33.1 0.9 collective-permute-done.9
  34.0 1.3 %collective-permute-start.10 = (f32[5,8,128]{2,1,0:T(8,128)S(1)}, f32[5,8,128]{2,1,0:T(8,128)S(1)}, u32[]{:S(2)}, u32[]{:S(2)}) collective-permute-start(f32[5,8,128]{2,1,0:T(8,128)S(1)} %add_add_fusion.have_ref), channel_id=1, source_target_pairs={{0,4},{1,5},{8,12},{9,13},{16,20},{17,21},{24,28},{25,29},{32,36},... | collective-permute-start | bytes 61448 | tf_op jit(solution)/shard_map/ppermute | solution.py:331
  35.2 0.9 collective-permute-done.10.got_ref
  36.9 3.3 %collective-permute-start.15 = (f32[256,256]{1,0:T(8,128)S(1)}, f32[256,256]{1,0:T(8,128)S(1)}, u32[]{:S(2)}, u32[]{:S(2)}) collective-permute-start(f32[256,256]{1,0:T(8,128)S(1)} %get-tuple-element.44.quarter_ref), channel_id=1, source_target_pairs={{32,40},{33,41},{34,42},{35,43},{48,56},{49,57},{50,58},{51,59},{6... | collective-permute-start | bytes 786440 | tf_op jit(solution)/shard_map/ppermute | solution.py:331
  40.2 1.9 %collective-permute-start.12 = (f32[5,8,128]{2,1,0:T(8,128)S(1)}, f32[5,8,128]{2,1,0:T(8,128)S(1)}, u32[]{:S(2)}, u32[]{:S(2)}) collective-permute-start(f32[5,8,128]{2,1,0:T(8,128)S(1)} %get-tuple-element.43.own_ref), channel_id=1, source_target_pairs={{0,1},{1,0},{4,5},{5,4},{8,9},{9,8},{12,13},{13,12},{16,17},{17,16... | collective-permute-start | bytes 61448 | tf_op jit(solution)/shard_map/ppermute | solution.py:331
  42.1 1.3 %collective-permute-start.13 = (f32[5,8,128]{2,1,0:T(8,128)S(1)}, f32[5,8,128]{2,1,0:T(8,128)S(1)}, u32[]{:S(2)}, u32[]{:S(2)}) collective-permute-start(f32[5,8,128]{2,1,0:T(8,128)S(1)} %get-tuple-element.43.own_ref), channel_id=1, source_target_pairs={{0,2},{1,3},{4,6},{5,7},{8,10},{9,11},{12,14},{13,15},{16,18},{17,... | collective-permute-start | bytes 61448 | tf_op jit(solution)/shard_map/ppermute | solution.py:331
  43.4 1.3 %collective-permute-start.14 = (f32[5,8,128]{2,1,0:T(8,128)S(1)}, f32[5,8,128]{2,1,0:T(8,128)S(1)}, u32[]{:S(2)}, u32[]{:S(2)}) collective-permute-start(f32[5,8,128]{2,1,0:T(8,128)S(1)} %get-tuple-element.43.own_ref), channel_id=1, source_target_pairs={{0,3},{1,2},{4,7},{5,6},{8,11},{9,10},{12,15},{13,14},{16,19},{17,... | collective-permute-start | bytes 61448 | tf_op jit(solution)/shard_map/ppermute | solution.py:331
  44.7 0.9 collective-permute-done.14.o3_ref
  46.4 1.7 %collective-permute-start.18 = (f32[256,256]{1,0:T(8,128)S(1)}, f32[256,256]{1,0:T(8,128)S(1)}, u32[]{:S(2)}, u32[]{:S(2)}) collective-permute-start(f32[256,256]{1,0:T(8,128)S(1)} %get-tuple-element.48.quarter_ref), channel_id=1, source_target_pairs={{32,36},{33,37},{34,38},{35,39},{40,44},{41,45},{42,46},{43,47},{4... | collective-permute-start | bytes 786440 | tf_op jit(solution)/shard_map/ppermute | solution.py:331
  48.0 28.0 %all-gather = f32[160,8,128]{2,1,0:T(8,128)S(1)} all-gather(f32[10,8,128]{2,1,0:T(8,128)S(1)} %get-tuple-element.46), channel_id=2, replica_groups=mesh['row'=16,'col'=32] {'row'}, dimensions={0}, use_global_device_ids=true | all-gather | bytes 696320 | tf_op jit(solution)/shard_map/all_gather | solution.py:377
  76.0 1.9 %collective-permute-start.19 = (f32[256,256]{1,0:T(8,128)S(1)}, f32[256,256]{1,0:T(8,128)S(1)}, u32[]{:S(2)}, u32[]{:S(2)}) collective-permute-start(f32[256,256]{1,0:T(8,128)S(1)} %get-tuple-element.49.after_ref.q0_ref), channel_id=1, source_target_pairs={{32,33},{33,34},{34,35},{35,32},{36,37},{37,38},{38,39},{39,36},{4... | collective-permute-start | bytes 786440 | tf_op jit(solution)/shard_map/ppermute | solution.py:331
  78.0 4.8 %collective-permute-start.20 = (f32[256,256]{1,0:T(8,128)S(1)}, f32[256,256]{1,0:T(8,128)S(1)}, u32[]{:S(2)}, u32[]{:S(2)}) collective-permute-start(f32[256,256]{1,0:T(8,128)S(1)} %get-tuple-element.49.after_ref.q0_ref), channel_id=1, source_target_pairs={{32,35},{33,32},{34,33},{35,34},{36,39},{37,36},{38,37},{39,38},{4... | collective-permute-start | bytes 786440 | tf_op jit(solution)/shard_map/ppermute | solution.py:331
  82.7 11.4 %shard_map.38 = (f32[512,512]{1,0:T(8,128)S(1)}, f32[512,512]{1,0:T(8,128)S(1)}, f32[512,512]{1,0:T(8,128)S(1)}) custom-call(f32[16,10,8,128]{3,2,1,0:T(8,128)S(1)} %get-tuple-element.50.g_ref, f32[256,256]{1,0:T(8,128)S(1)} %get-tuple-element.49.after_ref.q0_ref), custom_call_target="tpu_custom_call" | custom-call | tf_op jit(solution)/shard_map/pallas_call | solution.py:128
  94.1 2.1 %collective-permute-start.21 = (f32[256,256]{1,0:T(8,128)S(1)}, f32[256,256]{1,0:T(8,128)S(1)}, u32[]{:S(2)}, u32[]{:S(2)}) collective-permute-start(f32[256,256]{1,0:T(8,128)S(1)} %get-tuple-element.52.after_ref.q1_ref), channel_id=1, source_target_pairs={{32,33},{33,34},{34,35},{35,32},{36,37},{37,38},{38,39},{39,36},{4... | collective-permute-start | bytes 786440 | tf_op jit(solution)/shard_map/ppermute | solution.py:331
  96.3 9.9 %shard_map.40 = (f32[512,512]{1,0:T(8,128)S(1)}, f32[512,512]{1,0:T(8,128)S(1)}, f32[512,512]{1,0:T(8,128)S(1)}) custom-call(f32[512,512]{1,0:T(8,128)S(1)} %get-tuple-element.55.s_in, f32[512,512]{1,0:T(8,128)S(1)} %get-tuple-element.56.l_in, f32[512,512]{1,0:T(8,128)S(1)} %get-tuple-element.57.inv_in, ...), custom_call_target="tpu_custom_call", output_to_operand_aliasing={{0}: (0, {}), {1}: (1, {}), {2}: (2, {})} | custom-call | tf_op jit(solution)/shard_map/pallas_call | solution.py:139
  106.2 3.5 %shard_map.41 = (f32[16,512]{1,0:T(8,128)}, f32[512,256]{1,0:T(8,128)}) custom-call(f32[512,256]{1,0:T(8,128)S(1)} %copy-done, f32[256,256]{1,0:T(8,128)S(1)} %get-tuple-element.49.after_ref.q0_ref, f32[256,256]{1,0:T(8,128)S(1)} %get-tuple-element.52.after_ref.q1_ref, f32[256,256]{1,0:T(8,128)S(1)} %get-tuple-element.53.q2_ref, ...), custom_call_target="tpu_custom_call" | custom-call | tf_op jit(solution)/shard_map/pallas_call | solution.py:201
  (29 shorter events, 1.7 us)
Async XLA Ops:
  0.6 6.3 %copy-start = (f32[512,256]{1,0:T(8,128)S(1)}, f32[512,256]{1,0:T(8,128)}, u32[]{:S(2)}) copy-start(f32[512,256]{1,0:T(8,128)} %x_ref.7) | copy-start | bytes 1572868
  1.7 15.7 %collective-permute-start.2 = (f32[256,256]{1,0:T(8,128)S(1)}, f32[256,256]{1,0:T(8,128)S(1)}, u32[]{:S(2)}, u32[]{:S(2)}) collective-permute-start(f32[256,256]{1,0:T(8,128)S(1)} %slice.3), channel_id=1, source_target_pairs={{32,35},{33,34},{64,67},{65,66},{96,99},{97,98},{128,131},{129,130... | collective-permute-start | bytes 786440 | tf_op jit(solution)/shard_map/ppermute | solution.py:331
  6.9 16.7 %collective-permute-start.5 = (f32[512,256]{1,0:T(8,128)S(1)}, f32[512,256]{1,0:T(8,128)S(1)}, u32[]{:S(2)}, u32[]{:S(2)}) collective-permute-start(f32[512,256]{1,0:T(8,128)S(1)} %copy-done), channel_id=1, source_target_pairs={{2,258},{3,259},{4,260},{5,261},{6,262},{7,263},{8,264},{9,265},{1... | collective-permute-start | bytes 1572872 | tf_op jit(solution)/shard_map/ppermute | solution.py:331
  7.7 4.5 %collective-permute-start = (f32[8,5,8,128]{3,2,1,0:T(8,128)S(1)}, f32[8,5,8,128]{3,2,1,0:T(8,128)S(1)}, u32[]{:S(2)}, u32[]{:S(2)}) collective-permute-start(f32[8,5,8,128]{3,2,1,0:T(8,128)S(1)} %get-tuple-element.32), channel_id=1, source_target_pairs={{0,32},{1,33}} | collective-permute-start | bytes 491528 | tf_op jit(solution)/shard_map/ppermute | solution.py:331
  12.2 5.1 %collective-permute-start.1 = (f32[4,5,8,128]{3,2,1,0:T(8,128)S(1)}, f32[4,5,8,128]{3,2,1,0:T(8,128)S(1)}, u32[]{:S(2)}, u32[]{:S(2)}) collective-permute-start(f32[4,5,8,128]{3,2,1,0:T(8,128)S(1)} %get-tuple-element.34), channel_id=1, source_target_pairs={{0,256},{32,288},{1,257},{33,289}} | collective-permute-start | bytes 245768 | tf_op jit(solution)/shard_map/ppermute | solution.py:331
  17.4 6.2 %collective-permute-start.6 = (f32[256,256]{1,0:T(8,128)S(1)}, f32[256,256]{1,0:T(8,128)S(1)}, u32[]{:S(2)}, u32[]{:S(2)}) collective-permute-start(f32[256,256]{1,0:T(8,128)S(1)} %get-tuple-element.39.quarter_ref), channel_id=1, source_target_pairs={{32,48},{33,49},{34,50},{35,51},{64,80},{65,81},{66,82},{67,83},{9... | collective-permute-start | bytes 786440 | tf_op jit(solution)/shard_map/ppermute | solution.py:331
  18.7 2.7 %collective-permute-start.3 = (f32[2,5,8,128]{3,2,1,0:T(8,128)S(1)}, f32[2,5,8,128]{3,2,1,0:T(8,128)S(1)}, u32[]{:S(2)}, u32[]{:S(2)}) collective-permute-start(f32[2,5,8,128]{3,2,1,0:T(8,128)S(1)} %get-tuple-element.36), channel_id=1, source_target_pairs={{0,128},{32,160},{256,384},{288,416},{1,129},{33,161},{257,385},{2... | collective-permute-start | bytes 122888 | tf_op jit(solution)/shard_map/ppermute | solution.py:331
  21.4 2.2 %collective-permute-start.4 = (f32[1,5,8,128]{3,2,1,0:T(8,128)S(1)}, f32[1,5,8,128]{3,2,1,0:T(8,128)S(1)}, u32[]{:S(2)}, u32[]{:S(2)}) collective-permute-start(f32[1,5,8,128]{3,2,1,0:T(8,128)S(1)} %get-tuple-element.38), channel_id=1, source_target_pairs={{0,64},{32,96},{128,192},{160,224},{256,320},{288,352},{384,448},{... | collective-permute-start | bytes 61448 | tf_op jit(solution)/shard_map/ppermute | solution.py:331
  23.7 12.5 %collective-permute-start.11 = (f32[512,256]{1,0:T(8,128)S(1)}, f32[512,256]{1,0:T(8,128)S(1)}, u32[]{:S(2)}, u32[]{:S(2)}) collective-permute-start(f32[512,256]{1,0:T(8,128)S(1)} %get-tuple-element.42.top_ref), channel_id=1, source_target_pairs={{2,130},{258,386},{3,131},{259,387},{4,132},{260,388},{5,133},{261... | collective-permute-start | bytes 1572872 | tf_op jit(solution)/shard_map/ppermute | solution.py:331
  24.4 8.7 %collective-permute-start.7 = (f32[5,8,128]{2,1,0:T(8,128)S(1)}, f32[5,8,128]{2,1,0:T(8,128)S(1)}, u32[]{:S(2)}, u32[]{:S(2)}) collective-permute-start(f32[5,8,128]{2,1,0:T(8,128)S(1)} %get-tuple-element.41), channel_id=1, source_target_pairs={{0,16},{1,17},{32,48},{33,49},{64,80},{65,81},{96,112},{97,113},{1... | collective-permute-start | bytes 61448 | tf_op jit(solution)/shard_map/ppermute | solution.py:331
  30.5 2.6 %collective-permute-start.8 = (f32[5,8,128]{2,1,0:T(8,128)S(1)}, f32[5,8,128]{2,1,0:T(8,128)S(1)}, u32[]{:S(2)}, u32[]{:S(2)}) collective-permute-start(f32[5,8,128]{2,1,0:T(8,128)S(1)} %get-tuple-element.41), channel_id=1, source_target_pairs={{0,8},{1,9},{32,40},{33,41},{64,72},{65,73},{96,104},{97,105},{128... | collective-permute-start | bytes 61448 | tf_op jit(solution)/shard_map/ppermute | solution.py:331
  31.8 2.2 %collective-permute-start.9 = (f32[5,8,128]{2,1,0:T(8,128)S(1)}, f32[5,8,128]{2,1,0:T(8,128)S(1)}, u32[]{:S(2)}, u32[]{:S(2)}) collective-permute-start(f32[5,8,128]{2,1,0:T(8,128)S(1)} %get-tuple-element.41), channel_id=1, source_target_pairs={{0,24},{1,25},{32,56},{33,57},{64,88},{65,89},{96,120},{97,121},{1... | collective-permute-start | bytes 61448 | tf_op jit(solution)/shard_map/ppermute | solution.py:331
  34.0 2.2 %collective-permute-start.10 = (f32[5,8,128]{2,1,0:T(8,128)S(1)}, f32[5,8,128]{2,1,0:T(8,128)S(1)}, u32[]{:S(2)}, u32[]{:S(2)}) collective-permute-start(f32[5,8,128]{2,1,0:T(8,128)S(1)} %add_add_fusion.have_ref), channel_id=1, source_target_pairs={{0,4},{1,5},{8,12},{9,13},{16,20},{17,21},{24,28},{25,29},{32,36},... | collective-permute-start | bytes 61448 | tf_op jit(solution)/shard_map/ppermute | solution.py:331
  36.2 9.4 %collective-permute-start.16 = (f32[512,256]{1,0:T(8,128)S(1)}, f32[512,256]{1,0:T(8,128)S(1)}, u32[]{:S(2)}, u32[]{:S(2)}) collective-permute-start(f32[512,256]{1,0:T(8,128)S(1)} %get-tuple-element.45.top_ref), channel_id=1, source_target_pairs={{2,66},{130,194},{258,322},{386,450},{3,67},{131,195},{259,323},{3... | collective-permute-start | bytes 1572872 | tf_op jit(solution)/shard_map/ppermute | solution.py:331
  36.9 8.7 %collective-permute-start.15 = (f32[256,256]{1,0:T(8,128)S(1)}, f32[256,256]{1,0:T(8,128)S(1)}, u32[]{:S(2)}, u32[]{:S(2)}) collective-permute-start(f32[256,256]{1,0:T(8,128)S(1)} %get-tuple-element.44.quarter_ref), channel_id=1, source_target_pairs={{32,40},{33,41},{34,42},{35,43},{48,56},{49,57},{50,58},{51,59},{6... | collective-permute-start | bytes 786440 | tf_op jit(solution)/shard_map/ppermute | solution.py:331
  40.2 4.5 %collective-permute-start.12 = (f32[5,8,128]{2,1,0:T(8,128)S(1)}, f32[5,8,128]{2,1,0:T(8,128)S(1)}, u32[]{:S(2)}, u32[]{:S(2)}) collective-permute-start(f32[5,8,128]{2,1,0:T(8,128)S(1)} %get-tuple-element.43.own_ref), channel_id=1, source_target_pairs={{0,1},{1,0},{4,5},{5,4},{8,9},{9,8},{12,13},{13,12},{16,17},{17,16... | collective-permute-start | bytes 61448 | tf_op jit(solution)/shard_map/ppermute | solution.py:331
  42.1 2.6 %collective-permute-start.13 = (f32[5,8,128]{2,1,0:T(8,128)S(1)}, f32[5,8,128]{2,1,0:T(8,128)S(1)}, u32[]{:S(2)}, u32[]{:S(2)}) collective-permute-start(f32[5,8,128]{2,1,0:T(8,128)S(1)} %get-tuple-element.43.own_ref), channel_id=1, source_target_pairs={{0,2},{1,3},{4,6},{5,7},{8,10},{9,11},{12,14},{13,15},{16,18},{17,... | collective-permute-start | bytes 61448 | tf_op jit(solution)/shard_map/ppermute | solution.py:331
  43.4 2.2 %collective-permute-start.14 = (f32[5,8,128]{2,1,0:T(8,128)S(1)}, f32[5,8,128]{2,1,0:T(8,128)S(1)}, u32[]{:S(2)}, u32[]{:S(2)}) collective-permute-start(f32[5,8,128]{2,1,0:T(8,128)S(1)} %get-tuple-element.43.own_ref), channel_id=1, source_target_pairs={{0,3},{1,2},{4,7},{5,6},{8,11},{9,10},{12,15},{13,14},{16,19},{17,... | collective-permute-start | bytes 61448 | tf_op jit(solution)/shard_map/ppermute | solution.py:331
  45.7 30.3 %collective-permute-start.17 = (f32[512,256]{1,0:T(8,128)S(1)}, f32[512,256]{1,0:T(8,128)S(1)}, u32[]{:S(2)}, u32[]{:S(2)}) collective-permute-start(f32[512,256]{1,0:T(8,128)S(1)} %get-tuple-element.47.top_ref), channel_id=1, source_target_pairs={{2,34},{66,98},{130,162},{194,226},{258,290},{322,354},{386,418},{... | collective-permute-start | bytes 1572872 | tf_op jit(solution)/shard_map/ppermute | solution.py:331
  46.4 29.6 %collective-permute-start.18 = (f32[256,256]{1,0:T(8,128)S(1)}, f32[256,256]{1,0:T(8,128)S(1)}, u32[]{:S(2)}, u32[]{:S(2)}) collective-permute-start(f32[256,256]{1,0:T(8,128)S(1)} %get-tuple-element.48.quarter_ref), channel_id=1, source_target_pairs={{32,36},{33,37},{34,38},{35,39},{40,44},{41,45},{42,46},{43,47},{4... | collective-permute-start | bytes 786440 | tf_op jit(solution)/shard_map/ppermute | solution.py:331
  76.0 18.1 %collective-permute-start.19 = (f32[256,256]{1,0:T(8,128)S(1)}, f32[256,256]{1,0:T(8,128)S(1)}, u32[]{:S(2)}, u32[]{:S(2)}) collective-permute-start(f32[256,256]{1,0:T(8,128)S(1)} %get-tuple-element.49.after_ref.q0_ref), channel_id=1, source_target_pairs={{32,33},{33,34},{34,35},{35,32},{36,37},{37,38},{38,39},{39,36},{4... | collective-permute-start | bytes 786440 | tf_op jit(solution)/shard_map/ppermute | solution.py:331
  78.0 16.1 %collective-permute-start.20 = (f32[256,256]{1,0:T(8,128)S(1)}, f32[256,256]{1,0:T(8,128)S(1)}, u32[]{:S(2)}, u32[]{:S(2)}) collective-permute-start(f32[256,256]{1,0:T(8,128)S(1)} %get-tuple-element.49.after_ref.q0_ref), channel_id=1, source_target_pairs={{32,35},{33,32},{34,33},{35,34},{36,39},{37,36},{38,37},{39,38},{4... | collective-permute-start | bytes 786440 | tf_op jit(solution)/shard_map/ppermute | solution.py:331
  94.1 12.1 %collective-permute-start.21 = (f32[256,256]{1,0:T(8,128)S(1)}, f32[256,256]{1,0:T(8,128)S(1)}, u32[]{:S(2)}, u32[]{:S(2)}) collective-permute-start(f32[256,256]{1,0:T(8,128)S(1)} %get-tuple-element.52.after_ref.q1_ref), channel_id=1, source_target_pairs={{32,33},{33,34},{34,35},{35,32},{36,37},{37,38},{38,39},{39,36},{4... | collective-permute-start | bytes 786440 | tf_op jit(solution)/shard_map/ppermute | solution.py:331

commit v6 on v5

--- a/solution.py
+++ b/solution.py
@@ -61,8 +61,8 @@
         lt_ref[rows, :] = od
         m_ref[rows, :] = om
 
-def dot(a, b, dims=((1,), (0,))):
-    return lax.dot_general(a, b, (dims, ((), ())), precision=HI, preferred_element_type=jnp.float32)
+def dot(a, b, dims=((1,), (0,)), precision=HI):
+    return lax.dot_general(a, b, (dims, ((), ())), precision=precision, preferred_element_type=jnp.float32)
 
 N = 4 * B
 LEFT = ((0, 0), (1, 0), (1, 1), (2, 0), (3, 0))
@@ -293,10 +293,20 @@
         piece_ref[...] = jnp.zeros_like(piece_ref)
 
 
-def z_kernel(quarter_in, have_ref, got_ref, top_ref, down_ref, quarter_ref, piece_ref, top_out):
+def z_kernel(quarter_in, have_ref, got_ref, late_ref, top_ref, down_ref, quarter_ref, piece_ref, top_out):
     del quarter_in, quarter_ref
     y, core, z, xi = place()
-    choose(piece_ref, lax.rem(z, 2) == 1, got_ref, have_ref)
+    late = jnp.logical_or(z == 4, z == 5)
+    soon = jnp.logical_and(lax.rem(z, 2) == 1, z != 5)
+
+    @pl.when(late)
+    def _():
+        piece_ref[...] = late_ref[...]
+
+    @pl.when(jnp.logical_not(late))
+    def _():
+        choose(piece_ref, soon, got_ref, have_ref)
+
     choose(top_out, lax.rem(y // 2, 2) == 1, down_ref, top_ref)
 
 
@@ -358,10 +368,13 @@
     piece, top, part = local(y1_kernel, (low, got, x, down, part, far), (f32(5, 8, B), f32(*x.shape), quarter))
 
     down = across(top, [(0, 4), (8, 12)])
-    piece += sum(along(piece, [(0, 4 * z), (1, 4 * z + 1)]) for z in (4, 2, 6))
-    got = along(piece, [(4 * z + i, 4 * z + 4 + i) for z in (0, 2, 4, 6) for i in (0, 1)])
+    piece += sum(along(piece, [(0, 4 * z), (1, 4 * z + 1)]) for z in (2, 6))
+    got = [
+        along(piece, [(4 * a + i, 4 * b + i) for a, b in pairs for i in (0, 1)])
+        for pairs in (((0, 1), (2, 3), (6, 7)), ((0, 4), (6, 5)))
+    ]
     part, piece, top = local(
-        z_kernel, (part, piece, got, top, down), (quarter, f32(5, 8, B), f32(*x.shape)), {0: 0}
+        z_kernel, (part, piece, *got, top, down), (quarter, f32(5, 8, B), f32(*x.shape)), {0: 0}
     )
     others = [
         along(piece, [(4 * z + i, 4 * z + j) for z in zs for i, j in pairs])
@@ -380,7 +393,7 @@
     )
     near, next_ = by_x(part, 1), by_x(part, 3)
     s, lower, inv = first_half(gathered, part)
-    s, near, next_ = local(mid_kernel, (s, near, next_), (SQUARE, quarter, quarter), {0: 0, 1: 1, 2: 2})
+    s, near = local(mid_kernel, (s, near), (SQUARE, quarter), {0: 0, 1: 1})
     opposite = by_x(near, 1)
     _, lower, inv = second_half(s, lower, inv, near)
     return final(x, part, near, next_, opposite, top, down, lower, inv)

time: 110 us -> 110 us (level)
  starting transfers between devices: 45.4 us -> 43.3 us
  blocking collectives: 28 us -> 30 us
    ppermute x22, starting transfers between devices: 45.4 us -> 43.3 us  [send(): lax.ppermute(v, ('row', 'col'), [(32 * a + b, 32 * c + d) for (a, b), (c,...]
    all_gather x1, blocking collectives: 28 us -> 30 us  [on_device(): gathered = lax.all_gather(both, 'row')]
where the time goes in v6:
time: 110 us
  starting transfers between devices  43.3 us (39%)
  blocking collectives  30 us (27%)
  Pallas kernels  25.1 us (23%)
  waiting for transfers between devices  9.29 us (8%)
    ppermute x22, starting transfers between devices, send(): lax.ppermute(v, ('row', 'col'), [(32 * a + b, 32 * c + d) for (a, b), (c,...  43.3 us
    all_gather x1, blocking collectives, on_device(): gathered = lax.all_gather(both, 'row')  30 us
    pallas_call x1, Pallas kernels, first_half(): pl.pallas_call(first_kernel, out_shape=(SQUARE,) * 3, in_specs=[whole(),...  11.4 us
    pallas_call x1, Pallas kernels, second_half(): pl.pallas_call(second_kernel, out_shape=(SQUARE,) * 3, in_specs=[whole()]...  9.94 us
    ppermute x22, waiting for transfers between devices, send(): lax.ppermute(v, ('row', 'col'), [(32 * a + b, 32 * c + d) for (a, b), (c,...  9.29 us
    pallas_call x1, Pallas kernels, final(): pl.pallas_call(final_kernel, out_shape=(jax.ShapeDtypeStruct((16, 512), j...  3.46 us
  transfers between devices with their start and end apart: 22, of which 7 were waited for; matrix products, arithmetic and copies ran while one was open for 0% of the time, Pallas kernels for 19%

profile of v6, /device:TPU:1, one launch (start us, length us, event | category | flops | bytes accessed | tf_op | source)
XLA Modules:
  0.0 109.7 jit_solution(6282071095079450206)
XLA Ops:
  0.6 1.0 slice.3
  1.7 5.2 %collective-permute-start.2 = (f32[256,256]{1,0:T(8,128)S(1)}, f32[256,256]{1,0:T(8,128)S(1)}, u32[]{:S(2)}, u32[]{:S(2)}) collective-permute-start(f32[256,256]{1,0:T(8,128)S(1)} %slice.3), channel_id=1, source_target_pairs={{32,35},{33,34},{64,67},{65,66},{96,99},{97,98},{128,131},{129,130... | collective-permute-start | bytes 786440 | tf_op jit(solution)/shard_map/ppermute | solution.py:341
  6.9 0.7 collective-permute-start.5
  7.7 1.3 %collective-permute-start = (f32[8,5,8,128]{3,2,1,0:T(8,128)S(1)}, f32[8,5,8,128]{3,2,1,0:T(8,128)S(1)}, u32[]{:S(2)}, u32[]{:S(2)}) collective-permute-start(f32[8,5,8,128]{3,2,1,0:T(8,128)S(1)} %get-tuple-element.31), channel_id=1, source_target_pairs={{0,32},{1,33}} | collective-permute-start | bytes 491528 | tf_op jit(solution)/shard_map/ppermute | solution.py:341
  9.0 3.2 %collective-permute-done.got_ref = f32[8,5,8,128]{3,2,1,0:T(8,128)S(1)} collective-permute-done((f32[8,5,8,128]{3,2,1,0:T(8,128)S(1)}, f32[8,5,8,128]{3,2,1,0:T(8,128)S(1)}, u32[]{:S(2)}, u32[]{:S(2)}) %collective-permute-start) | collective-permute-done | bytes 163872 | tf_op jit(solution)/shard_map/ppermute | solution.py:341
  12.2 3.7 %collective-permute-start.1 = (f32[4,5,8,128]{3,2,1,0:T(8,128)S(1)}, f32[4,5,8,128]{3,2,1,0:T(8,128)S(1)}, u32[]{:S(2)}, u32[]{:S(2)}) collective-permute-start(f32[4,5,8,128]{3,2,1,0:T(8,128)S(1)} %get-tuple-element.33), channel_id=1, source_target_pairs={{0,256},{32,288},{1,257},{33,289}} | collective-permute-start | bytes 245768 | tf_op jit(solution)/shard_map/ppermute | solution.py:341
  15.9 1.5 %collective-permute-done.1.got_ref = f32[4,5,8,128]{3,2,1,0:T(8,128)S(1)} collective-permute-done((f32[4,5,8,128]{3,2,1,0:T(8,128)S(1)}, f32[4,5,8,128]{3,2,1,0:T(8,128)S(1)}, u32[]{:S(2)}, u32[]{:S(2)}) %collective-permute-start.1) | collective-permute-done | bytes 81952 | tf_op jit(solution)/shard_map/ppermute | solution.py:341
  17.4 1.3 %collective-permute-start.6 = (f32[256,256]{1,0:T(8,128)S(1)}, f32[256,256]{1,0:T(8,128)S(1)}, u32[]{:S(2)}, u32[]{:S(2)}) collective-permute-start(f32[256,256]{1,0:T(8,128)S(1)} %get-tuple-element.38.quarter_ref), channel_id=1, source_target_pairs={{32,48},{33,49},{34,50},{35,51},{64,80},{65,81},{66,82},{67,83},{9... | collective-permute-start | bytes 786440 | tf_op jit(solution)/shard_map/ppermute | solution.py:341
  18.7 1.6 %collective-permute-start.3 = (f32[2,5,8,128]{3,2,1,0:T(8,128)S(1)}, f32[2,5,8,128]{3,2,1,0:T(8,128)S(1)}, u32[]{:S(2)}, u32[]{:S(2)}) collective-permute-start(f32[2,5,8,128]{3,2,1,0:T(8,128)S(1)} %get-tuple-element.35), channel_id=1, source_target_pairs={{0,128},{32,160},{256,384},{288,416},{1,129},{33,161},{257,385},{2... | collective-permute-start | bytes 122888 | tf_op jit(solution)/shard_map/ppermute | solution.py:341
  20.3 1.1 collective-permute-done.3.got_ref
  21.4 1.3 %collective-permute-start.4 = (f32[1,5,8,128]{3,2,1,0:T(8,128)S(1)}, f32[1,5,8,128]{3,2,1,0:T(8,128)S(1)}, u32[]{:S(2)}, u32[]{:S(2)}) collective-permute-start(f32[1,5,8,128]{3,2,1,0:T(8,128)S(1)} %get-tuple-element.37), channel_id=1, source_target_pairs={{0,64},{32,96},{128,192},{160,224},{256,320},{288,352},{384,448},{... | collective-permute-start | bytes 61448 | tf_op jit(solution)/shard_map/ppermute | solution.py:341
  22.7 0.9 collective-permute-done.4.got_ref
  24.4 1.3 %collective-permute-start.7 = (f32[5,8,128]{2,1,0:T(8,128)S(1)}, f32[5,8,128]{2,1,0:T(8,128)S(1)}, u32[]{:S(2)}, u32[]{:S(2)}) collective-permute-start(f32[5,8,128]{2,1,0:T(8,128)S(1)} %get-tuple-element.40), channel_id=1, source_target_pairs={{0,8},{1,9},{32,40},{33,41},{64,72},{65,73},{96,104},{97,105},{128... | collective-permute-start | bytes 61448 | tf_op jit(solution)/shard_map/ppermute | solution.py:341
  25.7 1.3 %collective-permute-start.8 = (f32[5,8,128]{2,1,0:T(8,128)S(1)}, f32[5,8,128]{2,1,0:T(8,128)S(1)}, u32[]{:S(2)}, u32[]{:S(2)}) collective-permute-start(f32[5,8,128]{2,1,0:T(8,128)S(1)} %get-tuple-element.40), channel_id=1, source_target_pairs={{0,24},{1,25},{32,56},{33,57},{64,88},{65,89},{96,120},{97,121},{1... | collective-permute-start | bytes 61448 | tf_op jit(solution)/shard_map/ppermute | solution.py:341
  27.0 0.9 collective-permute-done.8
  27.9 4.0 %collective-permute-start.10 = (f32[5,8,128]{2,1,0:T(8,128)S(1)}, f32[5,8,128]{2,1,0:T(8,128)S(1)}, u32[]{:S(2)}, u32[]{:S(2)}) collective-permute-start(f32[5,8,128]{2,1,0:T(8,128)S(1)} %add_add_fusion.have_ref), channel_id=1, source_target_pairs={{0,16},{1,17},{24,20},{25,21},{32,48},{33,49},{56,52},{57,53},{64,... | collective-permute-start | bytes 61448 | tf_op jit(solution)/shard_map/ppermute | solution.py:341
  31.8 1.3 %collective-permute-start.9 = (f32[5,8,128]{2,1,0:T(8,128)S(1)}, f32[5,8,128]{2,1,0:T(8,128)S(1)}, u32[]{:S(2)}, u32[]{:S(2)}) collective-permute-start(f32[5,8,128]{2,1,0:T(8,128)S(1)} %add_add_fusion.have_ref), channel_id=1, source_target_pairs={{0,4},{1,5},{8,12},{9,13},{24,28},{25,29},{32,36},{33,37},{40,44},... | collective-permute-start | bytes 61448 | tf_op jit(solution)/shard_map/ppermute | solution.py:341
  33.2 0.9 collective-permute-done.9.got_ref
  34.8 1.3 %collective-permute-start.15 = (f32[256,256]{1,0:T(8,128)S(1)}, f32[256,256]{1,0:T(8,128)S(1)}, u32[]{:S(2)}, u32[]{:S(2)}) collective-permute-start(f32[256,256]{1,0:T(8,128)S(1)} %get-tuple-element.43.quarter_ref), channel_id=1, source_target_pairs={{32,40},{33,41},{34,42},{35,43},{48,56},{49,57},{50,58},{51,59},{6... | collective-permute-start | bytes 786440 | tf_op jit(solution)/shard_map/ppermute | solution.py:341
  36.1 1.9 %collective-permute-start.12 = (f32[5,8,128]{2,1,0:T(8,128)S(1)}, f32[5,8,128]{2,1,0:T(8,128)S(1)}, u32[]{:S(2)}, u32[]{:S(2)}) collective-permute-start(f32[5,8,128]{2,1,0:T(8,128)S(1)} %get-tuple-element.42.own_ref), channel_id=1, source_target_pairs={{0,1},{1,0},{4,5},{5,4},{8,9},{9,8},{12,13},{13,12},{16,17},{17,16... | collective-permute-start | bytes 61448 | tf_op jit(solution)/shard_map/ppermute | solution.py:341
  38.0 1.3 %collective-permute-start.13 = (f32[5,8,128]{2,1,0:T(8,128)S(1)}, f32[5,8,128]{2,1,0:T(8,128)S(1)}, u32[]{:S(2)}, u32[]{:S(2)}) collective-permute-start(f32[5,8,128]{2,1,0:T(8,128)S(1)} %get-tuple-element.42.own_ref), channel_id=1, source_target_pairs={{0,2},{1,3},{4,6},{5,7},{8,10},{9,11},{12,14},{13,15},{16,18},{17,... | collective-permute-start | bytes 61448 | tf_op jit(solution)/shard_map/ppermute | solution.py:341
  39.3 1.3 %collective-permute-start.14 = (f32[5,8,128]{2,1,0:T(8,128)S(1)}, f32[5,8,128]{2,1,0:T(8,128)S(1)}, u32[]{:S(2)}, u32[]{:S(2)}) collective-permute-start(f32[5,8,128]{2,1,0:T(8,128)S(1)} %get-tuple-element.42.own_ref), channel_id=1, source_target_pairs={{0,3},{1,2},{4,7},{5,6},{8,11},{9,10},{12,15},{13,14},{16,19},{17,... | collective-permute-start | bytes 61448 | tf_op jit(solution)/shard_map/ppermute | solution.py:341
  40.6 0.9 collective-permute-done.14.o3_ref
  41.6 0.7 collective-permute-start.17
  42.3 3.6 %collective-permute-start.18 = (f32[256,256]{1,0:T(8,128)S(1)}, f32[256,256]{1,0:T(8,128)S(1)}, u32[]{:S(2)}, u32[]{:S(2)}) collective-permute-start(f32[256,256]{1,0:T(8,128)S(1)} %get-tuple-element.47.quarter_ref), channel_id=1, source_target_pairs={{32,36},{33,37},{34,38},{35,39},{40,44},{41,45},{42,46},{43,47},{4... | collective-permute-start | bytes 786440 | tf_op jit(solution)/shard_map/ppermute | solution.py:341
  45.9 30.0 %all-gather = f32[160,8,128]{2,1,0:T(8,128)S(1)} all-gather(f32[10,8,128]{2,1,0:T(8,128)S(1)} %get-tuple-element.45), channel_id=2, replica_groups=mesh['row'=16,'col'=32] {'row'}, dimensions={0}, use_global_device_ids=true | all-gather | bytes 696320 | tf_op jit(solution)/shard_map/all_gather | solution.py:390
  76.0 1.9 %collective-permute-start.19 = (f32[256,256]{1,0:T(8,128)S(1)}, f32[256,256]{1,0:T(8,128)S(1)}, u32[]{:S(2)}, u32[]{:S(2)}) collective-permute-start(f32[256,256]{1,0:T(8,128)S(1)} %get-tuple-element.48.after_ref.q0_ref), channel_id=1, source_target_pairs={{32,33},{33,34},{34,35},{35,32},{36,37},{37,38},{38,39},{39,36},{4... | collective-permute-start | bytes 786440 | tf_op jit(solution)/shard_map/ppermute | solution.py:341
  77.9 4.8 %collective-permute-start.20 = (f32[256,256]{1,0:T(8,128)S(1)}, f32[256,256]{1,0:T(8,128)S(1)}, u32[]{:S(2)}, u32[]{:S(2)}) collective-permute-start(f32[256,256]{1,0:T(8,128)S(1)} %get-tuple-element.48.after_ref.q0_ref), channel_id=1, source_target_pairs={{32,35},{33,32},{34,33},{35,34},{36,39},{37,36},{38,37},{39,38},{4... | collective-permute-start | bytes 786440 | tf_op jit(solution)/shard_map/ppermute | solution.py:341
  82.7 11.4 %shard_map.38 = (f32[512,512]{1,0:T(8,128)S(1)}, f32[512,512]{1,0:T(8,128)S(1)}, f32[512,512]{1,0:T(8,128)S(1)}) custom-call(f32[16,10,8,128]{3,2,1,0:T(8,128)S(1)} %get-tuple-element.49.g_ref, f32[256,256]{1,0:T(8,128)S(1)} %get-tuple-element.48.after_ref.q0_ref), custom_call_target="tpu_custom_call" | custom-call | tf_op jit(solution)/shard_map/pallas_call | solution.py:128
  94.1 2.1 %collective-permute-start.21 = (f32[256,256]{1,0:T(8,128)S(1)}, f32[256,256]{1,0:T(8,128)S(1)}, u32[]{:S(2)}, u32[]{:S(2)}) collective-permute-start(f32[256,256]{1,0:T(8,128)S(1)} %get-tuple-element.51.after_ref.q1_ref), channel_id=1, source_target_pairs={{32,33},{33,34},{34,35},{35,32},{36,37},{37,38},{38,39},{39,36},{4... | collective-permute-start | bytes 786440 | tf_op jit(solution)/shard_map/ppermute | solution.py:341
  96.2 9.9 %shard_map.40 = (f32[512,512]{1,0:T(8,128)S(1)}, f32[512,512]{1,0:T(8,128)S(1)}, f32[512,512]{1,0:T(8,128)S(1)}) custom-call(f32[512,512]{1,0:T(8,128)S(1)} %get-tuple-element.53.s_in, f32[512,512]{1,0:T(8,128)S(1)} %get-tuple-element.54.l_in, f32[512,512]{1,0:T(8,128)S(1)} %get-tuple-element.55.inv_in, ...), custom_call_target="tpu_custom_call", output_to_operand_aliasing={{0}: (0, {}), {1}: (1, {}), {2}: (2, {})} | custom-call | tf_op jit(solution)/shard_map/pallas_call | solution.py:139
  106.2 3.5 %shard_map.41 = (f32[16,512]{1,0:T(8,128)}, f32[512,256]{1,0:T(8,128)}) custom-call(f32[512,256]{1,0:T(8,128)S(1)} %copy-done, f32[256,256]{1,0:T(8,128)S(1)} %get-tuple-element.48.after_ref.q0_ref, f32[256,256]{1,0:T(8,128)S(1)} %get-tuple-element.51.after_ref.q1_ref, f32[256,256]{1,0:T(8,128)S(1)} %collective-permute-done.20.q2_ref, ...), custom_call_target="tpu_custom_call" | custom-call | tf_op jit(solution)/shard_map/pallas_call | solution.py:201
  (29 shorter events, 1.7 us)
Async XLA Ops:
  0.6 6.3 %copy-start = (f32[512,256]{1,0:T(8,128)S(1)}, f32[512,256]{1,0:T(8,128)}, u32[]{:S(2)}) copy-start(f32[512,256]{1,0:T(8,128)} %x_ref.7) | copy-start | bytes 1572868
  1.7 15.7 %collective-permute-start.2 = (f32[256,256]{1,0:T(8,128)S(1)}, f32[256,256]{1,0:T(8,128)S(1)}, u32[]{:S(2)}, u32[]{:S(2)}) collective-permute-start(f32[256,256]{1,0:T(8,128)S(1)} %slice.3), channel_id=1, source_target_pairs={{32,35},{33,34},{64,67},{65,66},{96,99},{97,98},{128,131},{129,130... | collective-permute-start | bytes 786440 | tf_op jit(solution)/shard_map/ppermute | solution.py:341
  6.9 16.7 %collective-permute-start.5 = (f32[512,256]{1,0:T(8,128)S(1)}, f32[512,256]{1,0:T(8,128)S(1)}, u32[]{:S(2)}, u32[]{:S(2)}) collective-permute-start(f32[512,256]{1,0:T(8,128)S(1)} %copy-done), channel_id=1, source_target_pairs={{2,258},{3,259},{4,260},{5,261},{6,262},{7,263},{8,264},{9,265},{1... | collective-permute-start | bytes 1572872 | tf_op jit(solution)/shard_map/ppermute | solution.py:341
  7.7 4.5 %collective-permute-start = (f32[8,5,8,128]{3,2,1,0:T(8,128)S(1)}, f32[8,5,8,128]{3,2,1,0:T(8,128)S(1)}, u32[]{:S(2)}, u32[]{:S(2)}) collective-permute-start(f32[8,5,8,128]{3,2,1,0:T(8,128)S(1)} %get-tuple-element.31), channel_id=1, source_target_pairs={{0,32},{1,33}} | collective-permute-start | bytes 491528 | tf_op jit(solution)/shard_map/ppermute | solution.py:341
  12.2 5.1 %collective-permute-start.1 = (f32[4,5,8,128]{3,2,1,0:T(8,128)S(1)}, f32[4,5,8,128]{3,2,1,0:T(8,128)S(1)}, u32[]{:S(2)}, u32[]{:S(2)}) collective-permute-start(f32[4,5,8,128]{3,2,1,0:T(8,128)S(1)} %get-tuple-element.33), channel_id=1, source_target_pairs={{0,256},{32,288},{1,257},{33,289}} | collective-permute-start | bytes 245768 | tf_op jit(solution)/shard_map/ppermute | solution.py:341
  17.4 6.2 %collective-permute-start.6 = (f32[256,256]{1,0:T(8,128)S(1)}, f32[256,256]{1,0:T(8,128)S(1)}, u32[]{:S(2)}, u32[]{:S(2)}) collective-permute-start(f32[256,256]{1,0:T(8,128)S(1)} %get-tuple-element.38.quarter_ref), channel_id=1, source_target_pairs={{32,48},{33,49},{34,50},{35,51},{64,80},{65,81},{66,82},{67,83},{9... | collective-permute-start | bytes 786440 | tf_op jit(solution)/shard_map/ppermute | solution.py:341
  18.7 2.7 %collective-permute-start.3 = (f32[2,5,8,128]{3,2,1,0:T(8,128)S(1)}, f32[2,5,8,128]{3,2,1,0:T(8,128)S(1)}, u32[]{:S(2)}, u32[]{:S(2)}) collective-permute-start(f32[2,5,8,128]{3,2,1,0:T(8,128)S(1)} %get-tuple-element.35), channel_id=1, source_target_pairs={{0,128},{32,160},{256,384},{288,416},{1,129},{33,161},{257,385},{2... | collective-permute-start | bytes 122888 | tf_op jit(solution)/shard_map/ppermute | solution.py:341
  21.4 2.2 %collective-permute-start.4 = (f32[1,5,8,128]{3,2,1,0:T(8,128)S(1)}, f32[1,5,8,128]{3,2,1,0:T(8,128)S(1)}, u32[]{:S(2)}, u32[]{:S(2)}) collective-permute-start(f32[1,5,8,128]{3,2,1,0:T(8,128)S(1)} %get-tuple-element.37), channel_id=1, source_target_pairs={{0,64},{32,96},{128,192},{160,224},{256,320},{288,352},{384,448},{... | collective-permute-start | bytes 61448 | tf_op jit(solution)/shard_map/ppermute | solution.py:341
  23.7 10.4 %collective-permute-start.11 = (f32[512,256]{1,0:T(8,128)S(1)}, f32[512,256]{1,0:T(8,128)S(1)}, u32[]{:S(2)}, u32[]{:S(2)}) collective-permute-start(f32[512,256]{1,0:T(8,128)S(1)} %get-tuple-element.41.top_ref), channel_id=1, source_target_pairs={{2,130},{258,386},{3,131},{259,387},{4,132},{260,388},{5,133},{261... | collective-permute-start | bytes 1572872 | tf_op jit(solution)/shard_map/ppermute | solution.py:341
  24.4 2.6 %collective-permute-start.7 = (f32[5,8,128]{2,1,0:T(8,128)S(1)}, f32[5,8,128]{2,1,0:T(8,128)S(1)}, u32[]{:S(2)}, u32[]{:S(2)}) collective-permute-start(f32[5,8,128]{2,1,0:T(8,128)S(1)} %get-tuple-element.40), channel_id=1, source_target_pairs={{0,8},{1,9},{32,40},{33,41},{64,72},{65,73},{96,104},{97,105},{128... | collective-permute-start | bytes 61448 | tf_op jit(solution)/shard_map/ppermute | solution.py:341
  25.7 2.2 %collective-permute-start.8 = (f32[5,8,128]{2,1,0:T(8,128)S(1)}, f32[5,8,128]{2,1,0:T(8,128)S(1)}, u32[]{:S(2)}, u32[]{:S(2)}) collective-permute-start(f32[5,8,128]{2,1,0:T(8,128)S(1)} %get-tuple-element.40), channel_id=1, source_target_pairs={{0,24},{1,25},{32,56},{33,57},{64,88},{65,89},{96,120},{97,121},{1... | collective-permute-start | bytes 61448 | tf_op jit(solution)/shard_map/ppermute | solution.py:341
  27.9 5.3 %collective-permute-start.10 = (f32[5,8,128]{2,1,0:T(8,128)S(1)}, f32[5,8,128]{2,1,0:T(8,128)S(1)}, u32[]{:S(2)}, u32[]{:S(2)}) collective-permute-start(f32[5,8,128]{2,1,0:T(8,128)S(1)} %add_add_fusion.have_ref), channel_id=1, source_target_pairs={{0,16},{1,17},{24,20},{25,21},{32,48},{33,49},{56,52},{57,53},{64,... | collective-permute-start | bytes 61448 | tf_op jit(solution)/shard_map/ppermute | solution.py:341
  31.8 2.2 %collective-permute-start.9 = (f32[5,8,128]{2,1,0:T(8,128)S(1)}, f32[5,8,128]{2,1,0:T(8,128)S(1)}, u32[]{:S(2)}, u32[]{:S(2)}) collective-permute-start(f32[5,8,128]{2,1,0:T(8,128)S(1)} %add_add_fusion.have_ref), channel_id=1, source_target_pairs={{0,4},{1,5},{8,12},{9,13},{24,28},{25,29},{32,36},{33,37},{40,44},... | collective-permute-start | bytes 61448 | tf_op jit(solution)/shard_map/ppermute | solution.py:341
  34.1 7.4 %collective-permute-start.16 = (f32[512,256]{1,0:T(8,128)S(1)}, f32[512,256]{1,0:T(8,128)S(1)}, u32[]{:S(2)}, u32[]{:S(2)}) collective-permute-start(f32[512,256]{1,0:T(8,128)S(1)} %get-tuple-element.44.top_ref), channel_id=1, source_target_pairs={{2,66},{130,194},{258,322},{386,450},{3,67},{131,195},{259,323},{3... | collective-permute-start | bytes 1572872 | tf_op jit(solution)/shard_map/ppermute | solution.py:341
  34.8 6.7 %collective-permute-start.15 = (f32[256,256]{1,0:T(8,128)S(1)}, f32[256,256]{1,0:T(8,128)S(1)}, u32[]{:S(2)}, u32[]{:S(2)}) collective-permute-start(f32[256,256]{1,0:T(8,128)S(1)} %get-tuple-element.43.quarter_ref), channel_id=1, source_target_pairs={{32,40},{33,41},{34,42},{35,43},{48,56},{49,57},{50,58},{51,59},{6... | collective-permute-start | bytes 786440 | tf_op jit(solution)/shard_map/ppermute | solution.py:341
  36.1 4.5 %collective-permute-start.12 = (f32[5,8,128]{2,1,0:T(8,128)S(1)}, f32[5,8,128]{2,1,0:T(8,128)S(1)}, u32[]{:S(2)}, u32[]{:S(2)}) collective-permute-start(f32[5,8,128]{2,1,0:T(8,128)S(1)} %get-tuple-element.42.own_ref), channel_id=1, source_target_pairs={{0,1},{1,0},{4,5},{5,4},{8,9},{9,8},{12,13},{13,12},{16,17},{17,16... | collective-permute-start | bytes 61448 | tf_op jit(solution)/shard_map/ppermute | solution.py:341
  38.0 2.6 %collective-permute-start.13 = (f32[5,8,128]{2,1,0:T(8,128)S(1)}, f32[5,8,128]{2,1,0:T(8,128)S(1)}, u32[]{:S(2)}, u32[]{:S(2)}) collective-permute-start(f32[5,8,128]{2,1,0:T(8,128)S(1)} %get-tuple-element.42.own_ref), channel_id=1, source_target_pairs={{0,2},{1,3},{4,6},{5,7},{8,10},{9,11},{12,14},{13,15},{16,18},{17,... | collective-permute-start | bytes 61448 | tf_op jit(solution)/shard_map/ppermute | solution.py:341
  39.3 2.2 %collective-permute-start.14 = (f32[5,8,128]{2,1,0:T(8,128)S(1)}, f32[5,8,128]{2,1,0:T(8,128)S(1)}, u32[]{:S(2)}, u32[]{:S(2)}) collective-permute-start(f32[5,8,128]{2,1,0:T(8,128)S(1)} %get-tuple-element.42.own_ref), channel_id=1, source_target_pairs={{0,3},{1,2},{4,7},{5,6},{8,11},{9,10},{12,15},{13,14},{16,19},{17,... | collective-permute-start | bytes 61448 | tf_op jit(solution)/shard_map/ppermute | solution.py:341
  41.6 34.4 %collective-permute-start.17 = (f32[512,256]{1,0:T(8,128)S(1)}, f32[512,256]{1,0:T(8,128)S(1)}, u32[]{:S(2)}, u32[]{:S(2)}) collective-permute-start(f32[512,256]{1,0:T(8,128)S(1)} %get-tuple-element.46.top_ref), channel_id=1, source_target_pairs={{2,34},{66,98},{130,162},{194,226},{258,290},{322,354},{386,418},{... | collective-permute-start | bytes 1572872 | tf_op jit(solution)/shard_map/ppermute | solution.py:341
  42.3 33.7 %collective-permute-start.18 = (f32[256,256]{1,0:T(8,128)S(1)}, f32[256,256]{1,0:T(8,128)S(1)}, u32[]{:S(2)}, u32[]{:S(2)}) collective-permute-start(f32[256,256]{1,0:T(8,128)S(1)} %get-tuple-element.47.quarter_ref), channel_id=1, source_target_pairs={{32,36},{33,37},{34,38},{35,39},{40,44},{41,45},{42,46},{43,47},{4... | collective-permute-start | bytes 786440 | tf_op jit(solution)/shard_map/ppermute | solution.py:341
  76.0 18.1 %collective-permute-start.19 = (f32[256,256]{1,0:T(8,128)S(1)}, f32[256,256]{1,0:T(8,128)S(1)}, u32[]{:S(2)}, u32[]{:S(2)}) collective-permute-start(f32[256,256]{1,0:T(8,128)S(1)} %get-tuple-element.48.after_ref.q0_ref), channel_id=1, source_target_pairs={{32,33},{33,34},{34,35},{35,32},{36,37},{37,38},{38,39},{39,36},{4... | collective-permute-start | bytes 786440 | tf_op jit(solution)/shard_map/ppermute | solution.py:341
  77.9 28.2 %collective-permute-start.20 = (f32[256,256]{1,0:T(8,128)S(1)}, f32[256,256]{1,0:T(8,128)S(1)}, u32[]{:S(2)}, u32[]{:S(2)}) collective-permute-start(f32[256,256]{1,0:T(8,128)S(1)} %get-tuple-element.48.after_ref.q0_ref), channel_id=1, source_target_pairs={{32,35},{33,32},{34,33},{35,34},{36,39},{37,36},{38,37},{39,38},{4... | collective-permute-start | bytes 786440 | tf_op jit(solution)/shard_map/ppermute | solution.py:341
  94.1 12.1 %collective-permute-start.21 = (f32[256,256]{1,0:T(8,128)S(1)}, f32[256,256]{1,0:T(8,128)S(1)}, u32[]{:S(2)}, u32[]{:S(2)}) collective-permute-start(f32[256,256]{1,0:T(8,128)S(1)} %get-tuple-element.51.after_ref.q1_ref), channel_id=1, source_target_pairs={{32,33},{33,34},{34,35},{35,32},{36,37},{37,38},{38,39},{39,36},{4... | collective-permute-start | bytes 786440 | tf_op jit(solution)/shard_map/ppermute | solution.py:341

commit v7 on v6

--- a/solution.py
+++ b/solution.py
@@ -391,9 +391,10 @@
     gathered, down, part = local(
         gate_kernel, (gathered, down, part, far), (f32(16, 10, 8, B), f32(*x.shape), quarter), {0: 0, 1: 1}
     )
-    near, next_ = by_x(part, 1), by_x(part, 3)
+    near = by_x(part, 1)
     s, lower, inv = first_half(gathered, part)
-    s, near = local(mid_kernel, (s, near), (SQUARE, quarter), {0: 0, 1: 1})
+    s, near, part = local(mid_kernel, (s, near, part), (SQUARE, quarter, quarter), {0: 0, 1: 1, 2: 2})
+    next_ = by_x(part, 3)
     opposite = by_x(near, 1)
     _, lower, inv = second_half(s, lower, inv, near)
     return final(x, part, near, next_, opposite, top, down, lower, inv)

time: 110 us -> 110 us (level)
  blocking collectives: 30 us -> 28.2 us
    all_gather x1, blocking collectives: 30 us -> 28.2 us  [on_device(): gathered = lax.all_gather(both, 'row')]
  transfers between devices with their start and end apart: 22 -> 22, of which waited for: 7 -> 7; matrix products, arithmetic and copies ran while one was open for 0% -> 0% of each run, Pallas kernels for 19% -> 20%
where the time goes in v7:
time: 110 us; the launch traced here: 109 us
  starting transfers between devices  44.2 us (40%)
  blocking collectives  28.2 us (26%)
  Pallas kernels  25 us (23%)
  waiting for transfers between devices  9.89 us (9%)
    ppermute x22, starting transfers between devices, send(): lax.ppermute(v, ('row', 'col'), [(32 * a + b, 32 * c + d) for (a, b), (c,...  44.2 us
    all_gather x1, blocking collectives, on_device(): gathered = lax.all_gather(both, 'row')  28.2 us
    pallas_call x1, Pallas kernels, first_half(): pl.pallas_call(first_kernel, out_shape=(SQUARE,) * 3, in_specs=[whole(),...  11.4 us
    pallas_call x1, Pallas kernels, second_half(): pl.pallas_call(second_kernel, out_shape=(SQUARE,) * 3, in_specs=[whole()]...  9.95 us
    ppermute x22, waiting for transfers between devices, send(): lax.ppermute(v, ('row', 'col'), [(32 * a + b, 32 * c + d) for (a, b), (c,...  9.89 us
    pallas_call x1, Pallas kernels, final(): pl.pallas_call(final_kernel, out_shape=(jax.ShapeDtypeStruct((16, 512), j...  3.42 us
  transfers between devices with their start and end apart: 22, of which 7 were waited for; matrix products, arithmetic and copies ran while one was open for 0% of the time, Pallas kernels for 20%

profile of v7, /device:TPU:1, one launch (start us, length us, event | category | flops | bytes accessed | tf_op | source)
XLA Modules:
  0.0 109.3 jit_solution(14764166407495209193)
XLA Ops:
  0.6 1.0 slice.3
  1.7 5.2 %collective-permute-start.2 = (f32[256,256]{1,0:T(8,128)S(1)}, f32[256,256]{1,0:T(8,128)S(1)}, u32[]{:S(2)}, u32[]{:S(2)}) collective-permute-start(f32[256,256]{1,0:T(8,128)S(1)} %slice.3), channel_id=1, source_target_pairs={{32,35},{33,34},{64,67},{65,66},{96,99},{97,98},{128,131},{129,130... | collective-permute-start | bytes 786440 | tf_op jit(solution)/shard_map/ppermute | solution.py:341
  6.9 0.7 collective-permute-start.5
  7.7 1.3 %collective-permute-start = (f32[8,5,8,128]{3,2,1,0:T(8,128)S(1)}, f32[8,5,8,128]{3,2,1,0:T(8,128)S(1)}, u32[]{:S(2)}, u32[]{:S(2)}) collective-permute-start(f32[8,5,8,128]{3,2,1,0:T(8,128)S(1)} %get-tuple-element.32), channel_id=1, source_target_pairs={{0,32},{1,33}} | collective-permute-start | bytes 491528 | tf_op jit(solution)/shard_map/ppermute | solution.py:341
  9.0 3.2 %collective-permute-done.got_ref = f32[8,5,8,128]{3,2,1,0:T(8,128)S(1)} collective-permute-done((f32[8,5,8,128]{3,2,1,0:T(8,128)S(1)}, f32[8,5,8,128]{3,2,1,0:T(8,128)S(1)}, u32[]{:S(2)}, u32[]{:S(2)}) %collective-permute-start) | collective-permute-done | bytes 163872 | tf_op jit(solution)/shard_map/ppermute | solution.py:341
  12.2 3.7 %collective-permute-start.1 = (f32[4,5,8,128]{3,2,1,0:T(8,128)S(1)}, f32[4,5,8,128]{3,2,1,0:T(8,128)S(1)}, u32[]{:S(2)}, u32[]{:S(2)}) collective-permute-start(f32[4,5,8,128]{3,2,1,0:T(8,128)S(1)} %get-tuple-element.34), channel_id=1, source_target_pairs={{0,256},{32,288},{1,257},{33,289}} | collective-permute-start | bytes 245768 | tf_op jit(solution)/shard_map/ppermute | solution.py:341
  15.9 1.5 %collective-permute-done.1.got_ref = f32[4,5,8,128]{3,2,1,0:T(8,128)S(1)} collective-permute-done((f32[4,5,8,128]{3,2,1,0:T(8,128)S(1)}, f32[4,5,8,128]{3,2,1,0:T(8,128)S(1)}, u32[]{:S(2)}, u32[]{:S(2)}) %collective-permute-start.1) | collective-permute-done | bytes 81952 | tf_op jit(solution)/shard_map/ppermute | solution.py:341
  17.4 1.3 %collective-permute-start.6 = (f32[256,256]{1,0:T(8,128)S(1)}, f32[256,256]{1,0:T(8,128)S(1)}, u32[]{:S(2)}, u32[]{:S(2)}) collective-permute-start(f32[256,256]{1,0:T(8,128)S(1)} %get-tuple-element.39.quarter_ref), channel_id=1, source_target_pairs={{32,48},{33,49},{34,50},{35,51},{64,80},{65,81},{66,82},{67,83},{9... | collective-permute-start | bytes 786440 | tf_op jit(solution)/shard_map/ppermute | solution.py:341
  18.7 1.6 %collective-permute-start.3 = (f32[2,5,8,128]{3,2,1,0:T(8,128)S(1)}, f32[2,5,8,128]{3,2,1,0:T(8,128)S(1)}, u32[]{:S(2)}, u32[]{:S(2)}) collective-permute-start(f32[2,5,8,128]{3,2,1,0:T(8,128)S(1)} %get-tuple-element.36), channel_id=1, source_target_pairs={{0,128},{32,160},{256,384},{288,416},{1,129},{33,161},{257,385},{2... | collective-permute-start | bytes 122888 | tf_op jit(solution)/shard_map/ppermute | solution.py:341
  20.3 1.1 collective-permute-done.3.got_ref
  21.4 1.3 %collective-permute-start.4 = (f32[1,5,8,128]{3,2,1,0:T(8,128)S(1)}, f32[1,5,8,128]{3,2,1,0:T(8,128)S(1)}, u32[]{:S(2)}, u32[]{:S(2)}) collective-permute-start(f32[1,5,8,128]{3,2,1,0:T(8,128)S(1)} %get-tuple-element.38), channel_id=1, source_target_pairs={{0,64},{32,96},{128,192},{160,224},{256,320},{288,352},{384,448},{... | collective-permute-start | bytes 61448 | tf_op jit(solution)/shard_map/ppermute | solution.py:341
  22.7 0.9 collective-permute-done.4.got_ref
  23.7 0.7 collective-permute-start.11
  24.4 1.3 %collective-permute-start.8 = (f32[5,8,128]{2,1,0:T(8,128)S(1)}, f32[5,8,128]{2,1,0:T(8,128)S(1)}, u32[]{:S(2)}, u32[]{:S(2)}) collective-permute-start(f32[5,8,128]{2,1,0:T(8,128)S(1)} %get-tuple-element.41), channel_id=1, source_target_pairs={{0,24},{1,25},{32,56},{33,57},{64,88},{65,89},{96,120},{97,121},{1... | collective-permute-start | bytes 61448 | tf_op jit(solution)/shard_map/ppermute | solution.py:341
  25.7 1.3 %collective-permute-start.7 = (f32[5,8,128]{2,1,0:T(8,128)S(1)}, f32[5,8,128]{2,1,0:T(8,128)S(1)}, u32[]{:S(2)}, u32[]{:S(2)}) collective-permute-start(f32[5,8,128]{2,1,0:T(8,128)S(1)} %get-tuple-element.41), channel_id=1, source_target_pairs={{0,8},{1,9},{32,40},{33,41},{64,72},{65,73},{96,104},{97,105},{128... | collective-permute-start | bytes 61448 | tf_op jit(solution)/shard_map/ppermute | solution.py:341
  27.0 0.9 collective-permute-done.7
  27.9 4.0 %collective-permute-start.10 = (f32[5,8,128]{2,1,0:T(8,128)S(1)}, f32[5,8,128]{2,1,0:T(8,128)S(1)}, u32[]{:S(2)}, u32[]{:S(2)}) collective-permute-start(f32[5,8,128]{2,1,0:T(8,128)S(1)} %add_add_fusion.have_ref), channel_id=1, source_target_pairs={{0,16},{1,17},{24,20},{25,21},{32,48},{33,49},{56,52},{57,53},{64,... | collective-permute-start | bytes 61448 | tf_op jit(solution)/shard_map/ppermute | solution.py:341
  31.8 1.3 %collective-permute-start.9 = (f32[5,8,128]{2,1,0:T(8,128)S(1)}, f32[5,8,128]{2,1,0:T(8,128)S(1)}, u32[]{:S(2)}, u32[]{:S(2)}) collective-permute-start(f32[5,8,128]{2,1,0:T(8,128)S(1)} %add_add_fusion.have_ref), channel_id=1, source_target_pairs={{0,4},{1,5},{8,12},{9,13},{24,28},{25,29},{32,36},{33,37},{40,44},... | collective-permute-start | bytes 61448 | tf_op jit(solution)/shard_map/ppermute | solution.py:341
  33.2 0.9 collective-permute-done.9.got_ref
  34.8 1.3 %collective-permute-start.15 = (f32[256,256]{1,0:T(8,128)S(1)}, f32[256,256]{1,0:T(8,128)S(1)}, u32[]{:S(2)}, u32[]{:S(2)}) collective-permute-start(f32[256,256]{1,0:T(8,128)S(1)} %get-tuple-element.44.quarter_ref), channel_id=1, source_target_pairs={{32,40},{33,41},{34,42},{35,43},{48,56},{49,57},{50,58},{51,59},{6... | collective-permute-start | bytes 786440 | tf_op jit(solution)/shard_map/ppermute | solution.py:341
  36.1 1.3 %collective-permute-start.14 = (f32[5,8,128]{2,1,0:T(8,128)S(1)}, f32[5,8,128]{2,1,0:T(8,128)S(1)}, u32[]{:S(2)}, u32[]{:S(2)}) collective-permute-start(f32[5,8,128]{2,1,0:T(8,128)S(1)} %get-tuple-element.43.own_ref), channel_id=1, source_target_pairs={{0,3},{1,2},{4,7},{5,6},{8,11},{9,10},{12,15},{13,14},{16,19},{17,... | collective-permute-start | bytes 61448 | tf_op jit(solution)/shard_map/ppermute | solution.py:341
  37.4 1.3 %collective-permute-start.13 = (f32[5,8,128]{2,1,0:T(8,128)S(1)}, f32[5,8,128]{2,1,0:T(8,128)S(1)}, u32[]{:S(2)}, u32[]{:S(2)}) collective-permute-start(f32[5,8,128]{2,1,0:T(8,128)S(1)} %get-tuple-element.43.own_ref), channel_id=1, source_target_pairs={{0,2},{1,3},{4,6},{5,7},{8,10},{9,11},{12,14},{13,15},{16,18},{17,... | collective-permute-start | bytes 61448 | tf_op jit(solution)/shard_map/ppermute | solution.py:341
  38.7 3.0 %collective-permute-start.12 = (f32[5,8,128]{2,1,0:T(8,128)S(1)}, f32[5,8,128]{2,1,0:T(8,128)S(1)}, u32[]{:S(2)}, u32[]{:S(2)}) collective-permute-start(f32[5,8,128]{2,1,0:T(8,128)S(1)} %get-tuple-element.43.own_ref), channel_id=1, source_target_pairs={{0,1},{1,0},{4,5},{5,4},{8,9},{9,8},{12,13},{13,12},{16,17},{17,16... | collective-permute-start | bytes 61448 | tf_op jit(solution)/shard_map/ppermute | solution.py:341
  41.8 1.5 %collective-permute-done.12.o1_ref = f32[5,8,128]{2,1,0:T(8,128)S(1)} collective-permute-done((f32[5,8,128]{2,1,0:T(8,128)S(1)}, f32[5,8,128]{2,1,0:T(8,128)S(1)}, u32[]{:S(2)}, u32[]{:S(2)}) %collective-permute-start.12) | collective-permute-done | bytes 20512 | tf_op jit(solution)/shard_map/ppermute | solution.py:341
  44.0 3.6 %collective-permute-start.18 = (f32[256,256]{1,0:T(8,128)S(1)}, f32[256,256]{1,0:T(8,128)S(1)}, u32[]{:S(2)}, u32[]{:S(2)}) collective-permute-start(f32[256,256]{1,0:T(8,128)S(1)} %get-tuple-element.48.quarter_ref), channel_id=1, source_target_pairs={{32,36},{33,37},{34,38},{35,39},{40,44},{41,45},{42,46},{43,47},{4... | collective-permute-start | bytes 786440 | tf_op jit(solution)/shard_map/ppermute | solution.py:341
  47.6 28.2 %all-gather = f32[160,8,128]{2,1,0:T(8,128)S(1)} all-gather(f32[10,8,128]{2,1,0:T(8,128)S(1)} %get-tuple-element.46), channel_id=2, replica_groups=mesh['row'=16,'col'=32] {'row'}, dimensions={0}, use_global_device_ids=true | all-gather | bytes 696320 | tf_op jit(solution)/shard_map/all_gather | solution.py:390
  75.8 1.9 %collective-permute-start.19 = (f32[256,256]{1,0:T(8,128)S(1)}, f32[256,256]{1,0:T(8,128)S(1)}, u32[]{:S(2)}, u32[]{:S(2)}) collective-permute-start(f32[256,256]{1,0:T(8,128)S(1)} %get-tuple-element.50.after_ref.refs_2_), channel_id=1, source_target_pairs={{32,33},{33,34},{34,35},{35,32},{36,37},{37,38},{38,39},{39,36},{4... | collective-permute-start | bytes 786440 | tf_op jit(solution)/shard_map/ppermute | solution.py:341
  77.8 11.4 %shard_map.38 = (f32[512,512]{1,0:T(8,128)S(1)}, f32[512,512]{1,0:T(8,128)S(1)}, f32[512,512]{1,0:T(8,128)S(1)}) custom-call(f32[16,10,8,128]{3,2,1,0:T(8,128)S(1)} %get-tuple-element.49.g_ref, f32[256,256]{1,0:T(8,128)S(1)} %get-tuple-element.50.after_ref.refs_2_), custom_call_target="tpu_custom_call" | custom-call | tf_op jit(solution)/shard_map/pallas_call | solution.py:128
  89.2 4.8 %collective-permute-start.20 = (f32[256,256]{1,0:T(8,128)S(1)}, f32[256,256]{1,0:T(8,128)S(1)}, u32[]{:S(2)}, u32[]{:S(2)}) collective-permute-start(f32[256,256]{1,0:T(8,128)S(1)} %get-tuple-element.52.q0_ref), channel_id=1, source_target_pairs={{32,35},{33,32},{34,33},{35,34},{36,39},{37,36},{38,37},{39,38},{4... | collective-permute-start | bytes 786440 | tf_op jit(solution)/shard_map/ppermute | solution.py:341
  93.9 1.9 %collective-permute-start.21 = (f32[256,256]{1,0:T(8,128)S(1)}, f32[256,256]{1,0:T(8,128)S(1)}, u32[]{:S(2)}, u32[]{:S(2)}) collective-permute-start(f32[256,256]{1,0:T(8,128)S(1)} %get-tuple-element.53.after_ref.q1_ref), channel_id=1, source_target_pairs={{32,33},{33,34},{34,35},{35,32},{36,37},{37,38},{38,39},{39,36},{4... | collective-permute-start | bytes 786440 | tf_op jit(solution)/shard_map/ppermute | solution.py:341
  95.9 9.9 %shard_map.40 = (f32[512,512]{1,0:T(8,128)S(1)}, f32[512,512]{1,0:T(8,128)S(1)}, f32[512,512]{1,0:T(8,128)S(1)}) custom-call(f32[512,512]{1,0:T(8,128)S(1)} %get-tuple-element.55.s_in, f32[512,512]{1,0:T(8,128)S(1)} %get-tuple-element.56.l_in, f32[512,512]{1,0:T(8,128)S(1)} %get-tuple-element.57.inv_in, ...), custom_call_target="tpu_custom_call", output_to_operand_aliasing={{0}: (0, {}), {1}: (1, {}), {2}: (2, {})} | custom-call | tf_op jit(solution)/shard_map/pallas_call | solution.py:139
  105.8 3.4 %shard_map.41 = (f32[16,512]{1,0:T(8,128)}, f32[512,256]{1,0:T(8,128)}) custom-call(f32[512,256]{1,0:T(8,128)S(1)} %copy-done, f32[256,256]{1,0:T(8,128)S(1)} %get-tuple-element.52.q0_ref, f32[256,256]{1,0:T(8,128)S(1)} %get-tuple-element.53.after_ref.q1_ref, f32[256,256]{1,0:T(8,128)S(1)} %collective-permute-done.20.q2_ref, ...), custom_call_target="tpu_custom_call" | custom-call | tf_op jit(solution)/shard_map/pallas_call | solution.py:201
  (29 shorter events, 1.7 us)
Async XLA Ops:
  0.6 6.3 %copy-start = (f32[512,256]{1,0:T(8,128)S(1)}, f32[512,256]{1,0:T(8,128)}, u32[]{:S(2)}) copy-start(f32[512,256]{1,0:T(8,128)} %x_ref.7) | copy-start | bytes 1572868
  1.7 15.7 %collective-permute-start.2 = (f32[256,256]{1,0:T(8,128)S(1)}, f32[256,256]{1,0:T(8,128)S(1)}, u32[]{:S(2)}, u32[]{:S(2)}) collective-permute-start(f32[256,256]{1,0:T(8,128)S(1)} %slice.3), channel_id=1, source_target_pairs={{32,35},{33,34},{64,67},{65,66},{96,99},{97,98},{128,131},{129,130... | collective-permute-start | bytes 786440 | tf_op jit(solution)/shard_map/ppermute | solution.py:341
  6.9 16.7 %collective-permute-start.5 = (f32[512,256]{1,0:T(8,128)S(1)}, f32[512,256]{1,0:T(8,128)S(1)}, u32[]{:S(2)}, u32[]{:S(2)}) collective-permute-start(f32[512,256]{1,0:T(8,128)S(1)} %copy-done), channel_id=1, source_target_pairs={{2,258},{3,259},{4,260},{5,261},{6,262},{7,263},{8,264},{9,265},{1... | collective-permute-start | bytes 1572872 | tf_op jit(solution)/shard_map/ppermute | solution.py:341
  7.7 4.5 %collective-permute-start = (f32[8,5,8,128]{3,2,1,0:T(8,128)S(1)}, f32[8,5,8,128]{3,2,1,0:T(8,128)S(1)}, u32[]{:S(2)}, u32[]{:S(2)}) collective-permute-start(f32[8,5,8,128]{3,2,1,0:T(8,128)S(1)} %get-tuple-element.32), channel_id=1, source_target_pairs={{0,32},{1,33}} | collective-permute-start | bytes 491528 | tf_op jit(solution)/shard_map/ppermute | solution.py:341
  12.2 5.1 %collective-permute-start.1 = (f32[4,5,8,128]{3,2,1,0:T(8,128)S(1)}, f32[4,5,8,128]{3,2,1,0:T(8,128)S(1)}, u32[]{:S(2)}, u32[]{:S(2)}) collective-permute-start(f32[4,5,8,128]{3,2,1,0:T(8,128)S(1)} %get-tuple-element.34), channel_id=1, source_target_pairs={{0,256},{32,288},{1,257},{33,289}} | collective-permute-start | bytes 245768 | tf_op jit(solution)/shard_map/ppermute | solution.py:341
  17.4 6.2 %collective-permute-start.6 = (f32[256,256]{1,0:T(8,128)S(1)}, f32[256,256]{1,0:T(8,128)S(1)}, u32[]{:S(2)}, u32[]{:S(2)}) collective-permute-start(f32[256,256]{1,0:T(8,128)S(1)} %get-tuple-element.39.quarter_ref), channel_id=1, source_target_pairs={{32,48},{33,49},{34,50},{35,51},{64,80},{65,81},{66,82},{67,83},{9... | collective-permute-start | bytes 786440 | tf_op jit(solution)/shard_map/ppermute | solution.py:341
  18.7 2.7 %collective-permute-start.3 = (f32[2,5,8,128]{3,2,1,0:T(8,128)S(1)}, f32[2,5,8,128]{3,2,1,0:T(8,128)S(1)}, u32[]{:S(2)}, u32[]{:S(2)}) collective-permute-start(f32[2,5,8,128]{3,2,1,0:T(8,128)S(1)} %get-tuple-element.36), channel_id=1, source_target_pairs={{0,128},{32,160},{256,384},{288,416},{1,129},{33,161},{257,385},{2... | collective-permute-start | bytes 122888 | tf_op jit(solution)/shard_map/ppermute | solution.py:341
  21.4 2.2 %collective-permute-start.4 = (f32[1,5,8,128]{3,2,1,0:T(8,128)S(1)}, f32[1,5,8,128]{3,2,1,0:T(8,128)S(1)}, u32[]{:S(2)}, u32[]{:S(2)}) collective-permute-start(f32[1,5,8,128]{3,2,1,0:T(8,128)S(1)} %get-tuple-element.38), channel_id=1, source_target_pairs={{0,64},{32,96},{128,192},{160,224},{256,320},{288,352},{384,448},{... | collective-permute-start | bytes 61448 | tf_op jit(solution)/shard_map/ppermute | solution.py:341
  23.7 10.4 %collective-permute-start.11 = (f32[512,256]{1,0:T(8,128)S(1)}, f32[512,256]{1,0:T(8,128)S(1)}, u32[]{:S(2)}, u32[]{:S(2)}) collective-permute-start(f32[512,256]{1,0:T(8,128)S(1)} %get-tuple-element.42.top_ref), channel_id=1, source_target_pairs={{2,130},{258,386},{3,131},{259,387},{4,132},{260,388},{5,133},{261... | collective-permute-start | bytes 1572872 | tf_op jit(solution)/shard_map/ppermute | solution.py:341
  24.4 2.6 %collective-permute-start.8 = (f32[5,8,128]{2,1,0:T(8,128)S(1)}, f32[5,8,128]{2,1,0:T(8,128)S(1)}, u32[]{:S(2)}, u32[]{:S(2)}) collective-permute-start(f32[5,8,128]{2,1,0:T(8,128)S(1)} %get-tuple-element.41), channel_id=1, source_target_pairs={{0,24},{1,25},{32,56},{33,57},{64,88},{65,89},{96,120},{97,121},{1... | collective-permute-start | bytes 61448 | tf_op jit(solution)/shard_map/ppermute | solution.py:341
  25.7 2.2 %collective-permute-start.7 = (f32[5,8,128]{2,1,0:T(8,128)S(1)}, f32[5,8,128]{2,1,0:T(8,128)S(1)}, u32[]{:S(2)}, u32[]{:S(2)}) collective-permute-start(f32[5,8,128]{2,1,0:T(8,128)S(1)} %get-tuple-element.41), channel_id=1, source_target_pairs={{0,8},{1,9},{32,40},{33,41},{64,72},{65,73},{96,104},{97,105},{128... | collective-permute-start | bytes 61448 | tf_op jit(solution)/shard_map/ppermute | solution.py:341
  27.9 5.3 %collective-permute-start.10 = (f32[5,8,128]{2,1,0:T(8,128)S(1)}, f32[5,8,128]{2,1,0:T(8,128)S(1)}, u32[]{:S(2)}, u32[]{:S(2)}) collective-permute-start(f32[5,8,128]{2,1,0:T(8,128)S(1)} %add_add_fusion.have_ref), channel_id=1, source_target_pairs={{0,16},{1,17},{24,20},{25,21},{32,48},{33,49},{56,52},{57,53},{64,... | collective-permute-start | bytes 61448 | tf_op jit(solution)/shard_map/ppermute | solution.py:341
  31.8 2.2 %collective-permute-start.9 = (f32[5,8,128]{2,1,0:T(8,128)S(1)}, f32[5,8,128]{2,1,0:T(8,128)S(1)}, u32[]{:S(2)}, u32[]{:S(2)}) collective-permute-start(f32[5,8,128]{2,1,0:T(8,128)S(1)} %add_add_fusion.have_ref), channel_id=1, source_target_pairs={{0,4},{1,5},{8,12},{9,13},{24,28},{25,29},{32,36},{33,37},{40,44},... | collective-permute-start | bytes 61448 | tf_op jit(solution)/shard_map/ppermute | solution.py:341
  34.1 9.1 %collective-permute-start.16 = (f32[512,256]{1,0:T(8,128)S(1)}, f32[512,256]{1,0:T(8,128)S(1)}, u32[]{:S(2)}, u32[]{:S(2)}) collective-permute-start(f32[512,256]{1,0:T(8,128)S(1)} %get-tuple-element.45.top_ref), channel_id=1, source_target_pairs={{2,66},{130,194},{258,322},{386,450},{3,67},{131,195},{259,323},{3... | collective-permute-start | bytes 1572872 | tf_op jit(solution)/shard_map/ppermute | solution.py:341
  34.8 8.4 %collective-permute-start.15 = (f32[256,256]{1,0:T(8,128)S(1)}, f32[256,256]{1,0:T(8,128)S(1)}, u32[]{:S(2)}, u32[]{:S(2)}) collective-permute-start(f32[256,256]{1,0:T(8,128)S(1)} %get-tuple-element.44.quarter_ref), channel_id=1, source_target_pairs={{32,40},{33,41},{34,42},{35,43},{48,56},{49,57},{50,58},{51,59},{6... | collective-permute-start | bytes 786440 | tf_op jit(solution)/shard_map/ppermute | solution.py:341
  36.1 5.6 %collective-permute-start.14 = (f32[5,8,128]{2,1,0:T(8,128)S(1)}, f32[5,8,128]{2,1,0:T(8,128)S(1)}, u32[]{:S(2)}, u32[]{:S(2)}) collective-permute-start(f32[5,8,128]{2,1,0:T(8,128)S(1)} %get-tuple-element.43.own_ref), channel_id=1, source_target_pairs={{0,3},{1,2},{4,7},{5,6},{8,11},{9,10},{12,15},{13,14},{16,19},{17,... | collective-permute-start | bytes 61448 | tf_op jit(solution)/shard_map/ppermute | solution.py:341
  37.4 4.4 %collective-permute-start.13 = (f32[5,8,128]{2,1,0:T(8,128)S(1)}, f32[5,8,128]{2,1,0:T(8,128)S(1)}, u32[]{:S(2)}, u32[]{:S(2)}) collective-permute-start(f32[5,8,128]{2,1,0:T(8,128)S(1)} %get-tuple-element.43.own_ref), channel_id=1, source_target_pairs={{0,2},{1,3},{4,6},{5,7},{8,10},{9,11},{12,14},{13,15},{16,18},{17,... | collective-permute-start | bytes 61448 | tf_op jit(solution)/shard_map/ppermute | solution.py:341
  38.7 4.5 %collective-permute-start.12 = (f32[5,8,128]{2,1,0:T(8,128)S(1)}, f32[5,8,128]{2,1,0:T(8,128)S(1)}, u32[]{:S(2)}, u32[]{:S(2)}) collective-permute-start(f32[5,8,128]{2,1,0:T(8,128)S(1)} %get-tuple-element.43.own_ref), channel_id=1, source_target_pairs={{0,1},{1,0},{4,5},{5,4},{8,9},{9,8},{12,13},{13,12},{16,17},{17,16... | collective-permute-start | bytes 61448 | tf_op jit(solution)/shard_map/ppermute | solution.py:341
  43.3 32.5 %collective-permute-start.17 = (f32[512,256]{1,0:T(8,128)S(1)}, f32[512,256]{1,0:T(8,128)S(1)}, u32[]{:S(2)}, u32[]{:S(2)}) collective-permute-start(f32[512,256]{1,0:T(8,128)S(1)} %get-tuple-element.47.top_ref), channel_id=1, source_target_pairs={{2,34},{66,98},{130,162},{194,226},{258,290},{322,354},{386,418},{... | collective-permute-start | bytes 1572872 | tf_op jit(solution)/shard_map/ppermute | solution.py:341
  44.0 31.8 %collective-permute-start.18 = (f32[256,256]{1,0:T(8,128)S(1)}, f32[256,256]{1,0:T(8,128)S(1)}, u32[]{:S(2)}, u32[]{:S(2)}) collective-permute-start(f32[256,256]{1,0:T(8,128)S(1)} %get-tuple-element.48.quarter_ref), channel_id=1, source_target_pairs={{32,36},{33,37},{34,38},{35,39},{40,44},{41,45},{42,46},{43,47},{4... | collective-permute-start | bytes 786440 | tf_op jit(solution)/shard_map/ppermute | solution.py:341
  75.8 13.3 %collective-permute-start.19 = (f32[256,256]{1,0:T(8,128)S(1)}, f32[256,256]{1,0:T(8,128)S(1)}, u32[]{:S(2)}, u32[]{:S(2)}) collective-permute-start(f32[256,256]{1,0:T(8,128)S(1)} %get-tuple-element.50.after_ref.refs_2_), channel_id=1, source_target_pairs={{32,33},{33,34},{34,35},{35,32},{36,37},{37,38},{38,39},{39,36},{4... | collective-permute-start | bytes 786440 | tf_op jit(solution)/shard_map/ppermute | solution.py:341
  89.2 16.6 %collective-permute-start.20 = (f32[256,256]{1,0:T(8,128)S(1)}, f32[256,256]{1,0:T(8,128)S(1)}, u32[]{:S(2)}, u32[]{:S(2)}) collective-permute-start(f32[256,256]{1,0:T(8,128)S(1)} %get-tuple-element.52.q0_ref), channel_id=1, source_target_pairs={{32,35},{33,32},{34,33},{35,34},{36,39},{37,36},{38,37},{39,38},{4... | collective-permute-start | bytes 786440 | tf_op jit(solution)/shard_map/ppermute | solution.py:341
  93.9 11.9 %collective-permute-start.21 = (f32[256,256]{1,0:T(8,128)S(1)}, f32[256,256]{1,0:T(8,128)S(1)}, u32[]{:S(2)}, u32[]{:S(2)}) collective-permute-start(f32[256,256]{1,0:T(8,128)S(1)} %get-tuple-element.53.after_ref.q1_ref), channel_id=1, source_target_pairs={{32,33},{33,34},{34,35},{35,32},{36,37},{37,38},{38,39},{39,36},{4... | collective-permute-start | bytes 786440 | tf_op jit(solution)/shard_map/ppermute | solution.py:341
